TPU v7x, 512 devices: a whole 4x8x8 slice. The times are simulated.
512 devices in a mesh: qb: 16 (over y_lo, z), kb: 16 (over y_hi, x), pair: 2 (over core).
Axes of the slice: x: 4, y: 8 (y_hi: 4, y_lo: 2; y = y_hi * 2 + y_lo), z: 8, core: 2. Of those that a mesh axis runs over, the one named last changes fastest.
Arguments:
- queries: bfloat16 [2, 32768, 256], P('pair', ('qb', 'kb')), may hold values from -24 to 24
- keys: bfloat16 [2, 32768, 256], P('pair', ('kb', 'qb')), may hold values from -24 to 24
- values: bfloat16 [2, 32768, 256], P('pair', ('kb', 'qb')), may hold values from -6 to 6
- out_grad: bfloat16 [2, 32768, 256], P('pair', ('qb', 'kb')), may hold values from -0.796875 to 0.796875
- token_error: float32 [2, 32768], P('pair', ('qb', 'kb')), may hold values from 0.25 to 16
- block_mask: int32 [2, 256, 256], P(None, 'qb', 'kb'), may hold values from 0 to 1, as said below
Outputs:
- query_grad: bfloat16 [2, 32768, 256], P('pair', ('qb', 'kb'))
- key_grad: bfloat16 [2, 32768, 256], P('pair', ('kb', 'qb'))
- value_grad: bfloat16 [2, 32768, 256], P('pair', ('kb', 'qb'))
Inputs may be any that keep to these rules, and one draw needn't show every extreme that they name: `block_mask`: entries are 0 or 1. With blocks in groups of 16 consecutive blocks, for every head the tile of query group a and key group b holds exactly 32 >> bitlen(|a - b|) ones, where bitlen(0) = 0, bitlen(1) = 1, bitlen(2) = bitlen(3) = 2, bitlen(4) to bitlen(7) = 3 and so on; every diagonal block (i, i) is one.
All inputs are finite; a program needn't handle non-finite values.
Results may differ from a plain program's by a relative error of at most 0.015.
Values may be sent and summed in bfloat16 or wider, within the bound.
No kernel may reach another device: no remote copies, remote signals or barrier semaphores. Data moves between devices by JAX's collectives and lax.ppermute only.
A program may use at most 64 MiB of HBM per device.

v0:
```python
import jax
import jax.numpy as jnp
from jax import lax
from jax.sharding import PartitionSpec as P

DH = 128
HEADS = 2
BLK = 128


beta_pref = 20.0
neg_big = -1e30


def swapped(value, axis, bit):
    mask = 2**bit
    pairs = [(source, source ^ mask) for source in range(lax.axis_size(axis))]
    return lax.ppermute(value, axis, pairs)


def joined(x, axis, combine):
    everything = jax.tree.map(lambda part: lax.all_gather(part, axis), x)
    first = jax.tree.map(lambda part: part[0], everything)

    def turn(k, so_far):
        return combine(so_far, jax.tree.map(lambda part: part[k], everything))

    return lax.fori_loop(1, lax.axis_size(axis), turn, first)


def pair_lists(tile_mask, capacity):
    rows_at, cols_at = jnp.nonzero(tile_mask, size=capacity, fill_value=0)
    rows_at = rows_at.astype(jnp.int32)
    cols_at = cols_at.astype(jnp.int32)
    live_pair = jnp.arange(capacity) < jnp.sum(tile_mask)
    return (rows_at, cols_at, live_pair)


def segment_rows(rows_at, per_pair, block_count):
    return jnp.zeros((block_count,) + per_pair.shape[1:], jnp.float32).at[rows_at].add(per_pair)


def head_scores(query_pairs, key_pairs, live_pair):
    scores = jnp.einsum(
        "pid,pjd->pij", query_pairs, key_pairs, preferred_element_type=jnp.float32
    ) * DH ** (-0.5)
    return jnp.where(live_pair[:, None, None], scores, neg_big)


def probabilities(scores, rows_at, live_pair, row_top, row_total):
    shifted = jnp.exp(scores - row_top[rows_at][:, :, None]) / row_total[rows_at][:, :, None]
    return jnp.where(live_pair[:, None, None], shifted, 0.0)


def combine_two(former, latter):
    row_top = jnp.maximum(former[0], latter[0])
    former_weight = jnp.exp(former[0] - row_top)
    latter_weight = jnp.exp(latter[0] - row_top)
    return (row_top, former[1] * former_weight + latter[1] * latter_weight)


def body(queries, keys, values, out_grad, token_error, block_mask):
    block_count = block_mask.shape[1]
    capacity = max(block_count * block_count // 8, block_count)
    pair_side = lax.axis_index("pair")
    own_total = jnp.sum(token_error)
    token_count = token_error.shape[1] * lax.axis_size("qb") * lax.axis_size("kb")
    own_latent = lax.psum(own_total, ("qb", "kb"))
    partner_sum = swapped(own_latent, "pair", 0)
    winner_mean = jnp.where(pair_side == 0, own_latent, partner_sum) / token_count
    loser_mean = jnp.where(pair_side == 0, partner_sum, own_latent) / token_count
    keep_share = jax.nn.sigmoid(-beta_pref * (loser_mean - winner_mean))
    factor = jnp.where(pair_side == 0, 1.0 + beta_pref * keep_share, -beta_pref * keep_share)
    query_heads = []
    grad_heads = []
    key_heads = []
    value_heads = []
    row_part, grad_part = (
        lax.all_gather(queries, "kb", axis=1, tiled=True),
        lax.all_gather(out_grad, "kb", axis=1, tiled=True),
    )
    key_part, value_part = (
        lax.all_gather(keys, "qb", axis=1, tiled=True),
        lax.all_gather(values, "qb", axis=1, tiled=True),
    )
    for head_at in range(HEADS):
        column_start = head_at * DH
        query_heads.append(
            row_part[0, :, column_start : column_start + DH].reshape(block_count, BLK, DH)
        )
        grad_heads.append(
            grad_part[0, :, column_start : column_start + DH].reshape(block_count, BLK, DH)
        )
        key_heads.append(
            key_part[0, :, column_start : column_start + DH].reshape(block_count, BLK, DH)
        )
        value_heads.append(
            value_part[0, :, column_start : column_start + DH].reshape(block_count, BLK, DH)
        )
    pair_data = []
    top_list = []
    total_list = []
    for head_at in range(HEADS):
        rows_at, cols_at, live_pair = pair_lists(block_mask[head_at], capacity)
        query_pairs = query_heads[head_at][rows_at]
        grad_pairs = grad_heads[head_at][rows_at]
        key_pairs = key_heads[head_at][cols_at]
        value_pairs = value_heads[head_at][cols_at]
        scores = head_scores(query_pairs, key_pairs, live_pair)
        grad_scores = jnp.einsum(
            "pid,pjd->pij", grad_pairs, value_pairs, preferred_element_type=jnp.float32
        )
        row_top = (
            jnp.full((block_count, BLK), neg_big, jnp.float32)
            .at[rows_at]
            .max(jnp.max(scores, axis=2))
        )
        local_exp = jnp.where(
            live_pair[:, None, None], jnp.exp(scores - row_top[rows_at][:, :, None]), 0.0
        )
        top_list.append(row_top)
        total_list.append(segment_rows(rows_at, jnp.sum(local_exp, axis=2), block_count))
        pair_data.append(
            (rows_at, cols_at, query_pairs, key_pairs, grad_pairs, scores, grad_scores, live_pair)
        )
    row_tops, row_totals = joined((jnp.stack(top_list), jnp.stack(total_list)), "kb", combine_two)
    local_deltas = jnp.stack(
        [
            segment_rows(
                record[0],
                jnp.sum(
                    probabilities(
                        record[5], record[0], record[7], row_tops[head_at], row_totals[head_at]
                    )
                    * record[6],
                    axis=2,
                ),
                block_count,
            )
            for head_at, record in enumerate(pair_data)
        ]
    )
    deltas = lax.psum(local_deltas, "kb")
    score_scale = DH ** (-0.5)
    query_terms = []
    key_terms = []
    value_terms = []
    for head_at in range(HEADS):
        rows_at, cols_at, query_pairs, key_pairs, grad_pairs, scores, grad_scores, live_pair = (
            pair_data[head_at]
        )
        weights = probabilities(scores, rows_at, live_pair, row_tops[head_at], row_totals[head_at])
        dscore = (weights * (grad_scores - deltas[head_at][rows_at][:, :, None])).astype(
            jnp.bfloat16
        )
        weights_low = weights.astype(jnp.bfloat16)
        query_pair_grads = (
            jnp.einsum("pij,pjd->pid", dscore, key_pairs, preferred_element_type=jnp.float32)
            * score_scale
        )
        key_pair_grads = (
            jnp.einsum("pij,pid->pjd", dscore, query_pairs, preferred_element_type=jnp.float32)
            * score_scale
        )
        value_pair_grads = jnp.einsum(
            "pij,pid->pjd", weights_low, grad_pairs, preferred_element_type=jnp.float32
        )
        query_terms.append(segment_rows(rows_at, query_pair_grads, block_count) * factor)
        key_terms.append(segment_rows(cols_at, key_pair_grads, block_count) * factor)
        value_terms.append(segment_rows(cols_at, value_pair_grads, block_count) * factor)
    query_whole = jnp.stack(query_terms, axis=2).reshape(1, block_count * BLK, HEADS * DH)
    key_whole = jnp.stack(key_terms, axis=2).reshape(1, block_count * BLK, HEADS * DH)
    value_whole = jnp.stack(value_terms, axis=2).reshape(1, block_count * BLK, HEADS * DH)
    query_grad = lax.psum_scatter(
        query_whole.astype(jnp.bfloat16), "kb", scatter_dimension=1, tiled=True
    )
    key_grad, value_grad = (
        lax.psum_scatter(
            key_whole.astype(jnp.bfloat16), "qb", scatter_dimension=1, tiled=True
        ).astype(jnp.float32),
        lax.psum_scatter(
            value_whole.astype(jnp.bfloat16), "qb", scatter_dimension=1, tiled=True
        ).astype(jnp.float32),
    )
    return (query_grad, key_grad.astype(jnp.bfloat16), value_grad.astype(jnp.bfloat16))


def solution(mesh):
    return jax.shard_map(
        body,
        mesh=mesh,
        in_specs=(
            P("pair", ("qb", "kb"), None),
            P("pair", ("kb", "qb"), None),
            P("pair", ("kb", "qb"), None),
            P("pair", ("qb", "kb"), None),
            P("pair", ("qb", "kb")),
            P(None, "qb", "kb"),
        ),
        out_specs=(
            P("pair", ("qb", "kb"), None),
            P("pair", ("kb", "qb"), None),
            P("pair", ("kb", "qb"), None),
        ),
        check_vma=False,
    )
```

profile of v0, /device:TPU:6, one launch (start us, length us, event | category | flops | bytes accessed | tf_op | source)
XLA Modules:
  0.0 1265.2 jit_solution(18273497892351449103)
XLA Ops:
  10.7 687.5 %psum.15 = f32[]{:T(128)} all-reduce(f32[]{:T(128)} %reduce_sum.89), channel_id=1, replica_groups=mesh['qb'=16,'kb'=16,'pair'=2] {'qb','kb'}, use_global_device_ids=true, to_apply=%region_29.30 | all-reduce | flops 1 | bytes 8 | tf_op jit(solution)/shard_map/psum | solution.py:68
  703.0 2.3 scatter_custom_fusion
  706.2 2.3 scatter_custom_fusion.2
  716.1 2.4 fusion.46
  725.3 2.5 fusion.48
  733.1 45.6 %all-gather.1 = f32[32,16,128]{2,1,0:T(8,128)S(1)} all-gather(f32[2,16,128]{2,1,0:T(8,128)S(1)} %pad_maximum_fusion.4), channel_id=3, replica_groups=mesh['qb'=16,'kb'=16,'pair'=2] {'kb'}, dimensions={0}, use_global_device_ids=true | all-gather | bytes 278528 | tf_op jit(solution)/shard_map/all_gather | solution.py:22
  778.7 39.6 %all-gather = f32[32,16,128]{2,1,0:T(8,128)S(1)} all-gather(f32[2,16,128]{2,1,0:T(8,128)S(1)} %pad_maximum_fusion.3), channel_id=2, replica_groups=mesh['qb'=16,'kb'=16,'pair'=2] {'kb'}, dimensions={0}, use_global_device_ids=true | all-gather | bytes 278528 | tf_op jit(solution)/shard_map/all_gather | solution.py:22
  826.0 3.6 fusion.4
  829.7 4.7 scatter_fusion.4
  834.4 3.0 fusion.2
  838.5 7.2 scatter_fusion.5
  848.3 3.2 reshape.710
  851.4 2.7 copy.95
  854.3 34.9 %all-gather.13.cloned.1.call-done = bf16[1,2048,256]{2,1,0:T(8,128)(2,1)} async-done(((bf16[1,128,256]{2,1,0:T(8,128)(2,1)}), bf16[1,2048,256]{2,1,0:T(8,128)(2,1)}) %all-gather.13.cloned.1.call-update) | async-done | bytes 1048592 | tf_op jit(solution)/shard_map/all_gather | solution.py:84
  892.1 4.4 multiply_reduce_fusion.1
  898.3 3.7 multiply_reduce_fusion
  903.5 70.9 %psum.14 = f32[2,16,128]{2,1,0:T(8,128)S(1)} all-reduce(f32[2,16,128]{2,1,0:T(8,128)S(1)} %pad_maximum_fusion.5), channel_id=1, replica_groups=mesh['qb'=16,'kb'=16,'pair'=2] {'kb'}, use_global_device_ids=true, to_apply=%region_26.27 | all-reduce | flops 4096 | bytes 32768 | tf_op jit(solution)/shard_map/psum | solution.py:143
  975.0 3.1 multiply_convert_fusion.1
  978.1 2.2 convolution_multiply_fusion.1
  980.4 3.0 copy.60
  983.9 2.5 multiply_convert_fusion
  990.2 4.7 scatter_fusion.2
  995.0 4.7 scatter_fusion.3
  1001.1 3.2 reshape.709
  1004.2 2.9 copy.96
  1009.3 3.1 copy.54
  1014.3 3.0 copy.57
  1017.4 2.7 scatter_fusion
  1020.2 4.7 scatter_fusion.1
  1028.0 13.8 %reduce-scatter.14.cloned.1.call-done = bf16[128,256]{1,0:T(8,128)(2,1)} async-done(((bf16[2048,256]{1,0:T(8,128)(2,1)}), bf16[128,256]{1,0:T(8,128)(2,1)}) %reduce-scatter.14.cloned.1.call-update) | async-done | bytes 65552
  1043.4 122.6 %reduce-scatter.12.cloned.1.call-done = bf16[128,256]{1,0:T(8,128)(2,1)} async-done(((bf16[2048,256]{1,0:T(8,128)(2,1)}), bf16[128,256]{1,0:T(8,128)(2,1)}) %reduce-scatter.12.cloned.1.call-update) | async-done | bytes 65552
  1167.6 89.2 %reduce-scatter.10.cloned.1.call-done = bf16[128,256]{1,0:T(8,128)(2,1)} async-done(((bf16[2048,256]{1,0:T(8,128)(2,1)}), bf16[128,256]{1,0:T(8,128)(2,1)}) %reduce-scatter.10.cloned.1.call-update) | async-done | bytes 65552
  (153 shorter events, 62.5 us)
Async XLA Ops:
  7.2 706.8 %all-gather.7.cloned.1.call-start = ((), (), s32[]{:S(2)}) async-start(), calls=%async_computation.3 | async-start | bytes 1114112 | tf_op jit(solution)/shard_map/all_gather | solution.py:79
  7.9 708.2 %all-gather.9.cloned.1.call-start = ((), (), s32[]{:S(2)}) async-start(), calls=%async_computation.4 | async-start | bytes 1114112 | tf_op jit(solution)/shard_map/all_gather | solution.py:83
  8.6 811.5 %all-gather.11.cloned.1.call-start = ((), (), s32[]{:S(2)}) async-start(), calls=%async_computation.5 | async-start | bytes 1114112 | tf_op jit(solution)/shard_map/all_gather | solution.py:80
  9.4 879.8 %all-gather.13.cloned.1.call-start = ((), (), s32[]{:S(2)}) async-start(), calls=%async_computation.6 | async-start | bytes 1114112 | tf_op jit(solution)/shard_map/all_gather | solution.py:84
  698.1 13.4 %collective-permute-start = (f32[]{:T(128)}, f32[]{:T(128)}, u32[]{:S(2)}, u32[]{:S(2)}) collective-permute-start(f32[]{:T(128)} %psum.15), channel_id=1, source_target_pairs={{0,1},{1,0},{2,3},{3,2},{4,5},{5,4},{6,7},{7,6},{8,9},{9,8},{10,11... | collective-permute-start | bytes 20 | tf_op jit(solution)/shard_map/ppermute | solution.py:18
  700.1 341.8 %reduce-scatter.14.cloned.1.call-start = ((), (), s32[]{:S(2)}) async-start(), calls=%async_computation.9 | async-start | bytes 1114112
  716.0 3.2 copy-start.5
  719.3 2.2 copy-start.1
  721.5 3.1 copy-start.11
  725.3 2.5 copy-start.3
  845.7 1.2 copy-start
  854.2 311.8 %reduce-scatter.12.cloned.1.call-start = ((), (), s32[]{:S(2)}) async-start(), calls=%async_computation.8 | async-start | bytes 1114112
  975.0 3.1 copy-start.6
  983.9 3.5 copy-start.7
  986.4 1.0 copy-start.8
  1004.2 3.3 copy-start.2
  1007.2 249.6 %reduce-scatter.10.cloned.1.call-start = ((), (), s32[]{:S(2)}) async-start(), calls=%async_computation.7 | async-start | bytes 1114112
  1009.3 3.1 copy-start.4
  1009.3 3.1 copy-start.9
  1014.3 3.1 copy-start.10
Sparse Core Ops, SparseCore 0:
  11.0 61.3 all-gather.6
  74.4 71.9 all-gather.8
  149.4 53.9 all-gather.10
  700.2 188.9 all-gather.12
  891.9 149.9 reduce-scatter.13
  1044.7 121.2 reduce-scatter.11
  1170.1 86.6 reduce-scatter.9
where the time goes:
time: 1270 us
  blocking collectives  844 us (66%)
  waiting for transfers between devices  263 us (21%)
  local copies, waits for them, and re-layouts  58.5 us (5%)
  other arithmetic  54.3 us (4%)
  matrix products  26.2 us (2%)
  between operations  17.1 us (1%)
    psum x1, blocking collectives, body(): own_latent = lax.psum(own_total, ('qb', 'kb'))  687 us
    unnamed x10, waiting for transfers between devices  228 us
    all_gather x2, blocking collectives, joined(): everything = jax.tree.map(lambda part: lax.all_gather(part, axis), x)  85.2 us
    psum x1, blocking collectives, body(): deltas = lax.psum(local_deltas, 'kb')  70.9 us
    all_gather x1, waiting for transfers between devices, body(): lax.all_gather(values, 'qb', axis=1, tiled=True)  34.9 us
    scatter-add x10, other arithmetic, segment_rows(): jnp.zeros((block_count,) + per_pair.shape[1:], jnp.float32).at[rows_at]  31.5 us
  transfers between devices with their start and end apart: 8, of which 4 were waited for; matrix products, arithmetic and copies ran while one was open for 11% of the time, Pallas kernels for 0%

commit v1 on v0

v1 whole, which is shorter than its diff:
```python
import functools

import jax
import jax.numpy as jnp
from jax import lax
from jax.experimental import pallas as pl
from jax.experimental.pallas import tpu as pltpu
from jax.sharding import PartitionSpec as P

DH = 128
HEADS = 2
BLK = 128
GB = 16
WIDE = HEADS * DH
ROWS = BLK + 8
SLOTS = HEADS * GB
STAT = 3 * SLOTS + 8
LIST = 40

beta_pref = 20.0
neg_big = -1e30
score_scale = DH ** (-0.5)
log2_scale = score_scale * 1.4426950408889634

Y_GROUPS = [[x + 4 * y for y in range(4)] for x in range(4)]
X_GROUPS = [[x + 4 * y for x in range(4)] for y in range(4)]
Z_GROUPS = [[z + 8 * y for z in range(8)] for y in range(2)]
Y_PAIRS = [(s, s ^ 8) for s in range(16)]

VMEM = pl.BlockSpec(memory_space=pltpu.VMEM)
SMEM = pl.BlockSpec(memory_space=pltpu.SMEM)
ANY = pl.BlockSpec(memory_space=pl.ANY)
PARAMS = pltpu.CompilerParams(vmem_limit_bytes=40 * 1024 * 1024)


def dot(a, b, dims):
    return lax.dot_general(a, b, (dims, ((), ())), preferred_element_type=jnp.float32)


def pack_kernel(queries, keys, values, out_grad, token_error, qg_ref, kv_ref):
    qg_ref[:, :WIDE] = queries[0]
    qg_ref[:, WIDE:] = out_grad[0]
    total = jnp.sum(token_error[...], axis=1, keepdims=True)
    high = total.astype(jnp.bfloat16).astype(jnp.float32)
    rest = total - high
    middle = rest.astype(jnp.bfloat16).astype(jnp.float32)
    low = rest - middle
    row = lax.broadcasted_iota(jnp.int32, (8, 2 * WIDE), 0)
    sums = jnp.where(row == 0, high, jnp.where(row == 1, middle, jnp.where(row == 2, low, 0.0)))
    sums = jnp.concatenate([sums, jnp.zeros_like(sums)], axis=0).astype(jnp.bfloat16)[:8]
    for slot in range(8):
        kv_ref[slot, :BLK, :WIDE] = keys[0]
        kv_ref[slot, :BLK, WIDE:] = values[0]
        kv_ref[slot, BLK:, :] = sums


def list_kernel(mask, side, lists):
    for head in range(HEADS):

        def step(at, count):
            row = at // GB
            col = at % GB
            lists[2 * head, count] = (row % 4) * 4 + row // 4
            lists[2 * head + 1, count] = col ^ (side[0] * 8)
            return jnp.minimum(count + mask[head, row, col], LIST - 1)

        count = lax.fori_loop(0, GB * GB, step, 0, unroll=4)
        lists[2 * HEADS, head] = count


def load_keys(near, far, kv, sems):
    one = pltpu.make_async_copy(near, kv.at[pl.ds(0, 8)], sems.at[0])
    two = pltpu.make_async_copy(far, kv.at[pl.ds(8, 8)], sems.at[1])
    one.start()
    two.start()
    one.wait()
    two.wait()


def pair_of(lists, head, at, qg, kv):
    row, col = lists[2 * head, at], lists[2 * head + 1, at]
    first, second = head * DH, WIDE + head * DH
    query, grad = qg[row, :, first : first + DH], qg[row, :, second : second + DH]
    key, value = kv[col, :BLK, first : first + DH], kv[col, :BLK, second : second + DH]
    scores = dot(key, query, ((1,), (1,))) * log2_scale
    grad_scores = dot(value, grad, ((1,), (1,)))
    return row, col, query, grad, key, scores, grad_scores


def stat_kernel(lists, qg, near, far, stat, kv, top, total, delta, sems):
    load_keys(near, far, kv, sems)
    top[...] = jnp.full_like(top, neg_big)
    total[...] = jnp.zeros_like(total)
    delta[...] = jnp.zeros_like(delta)

    def step(p, carry):
        found = []
        for head in range(HEADS):
            for u in range(2):
                row, _, _, _, _, scores, grad_scores = pair_of(lists, head, 2 * p + u, qg, kv)
                own_top = jnp.max(scores, axis=0, keepdims=True)
                shifted = jnp.exp2(scores - own_top)
                own_total = jnp.sum(shifted, axis=0, keepdims=True)
                own_delta = jnp.sum(shifted * grad_scores, axis=0, keepdims=True)
                found.append((head * GB + row, own_top, own_total, own_delta))
        for at, own_top, own_total, own_delta in found:
            old_top = top[at]
            new_top = jnp.maximum(old_top, own_top)
            old_weight = jnp.exp2(old_top - new_top)
            own_weight = jnp.exp2(own_top - new_top)
            top[at] = new_top
            total[at] = total[at] * old_weight + own_total * own_weight
            delta[at] = delta[at] * old_weight + own_delta * own_weight
        return carry

    lax.fori_loop(0, lists[2 * HEADS, 0] // 2, step, 0)
    for at in range(SLOTS):
        stat[at : at + 1, :] = top[at]
        stat[SLOTS + at : SLOTS + at + 1, :] = total[at]
        stat[2 * SLOTS + at : 2 * SLOTS + at + 1, :] = delta[at]
    sums = kv[0, BLK:, :DH].astype(jnp.float32)
    for slot in range(1, GB):
        sums = sums + kv[slot, BLK:, :DH].astype(jnp.float32)
    sums = jnp.sum(sums, axis=0, keepdims=True)
    stat[3 * SLOTS :, :] = jnp.broadcast_to(sums, (8, DH))


def grad_kernel(lists, qg, near, far, stats, qout, kvnear, kvfar, latent, kv, shift, delta, qacc, kacc, vacc, sems):
    load_keys(near, far, kv, sems)
    tops = stats[0, :SLOTS]
    for part in range(1, GB):
        tops = jnp.maximum(tops, stats[part, :SLOTS])
    totals = jnp.zeros_like(tops)
    deltas = jnp.zeros_like(tops)
    sums = jnp.zeros((8, DH), jnp.float32)
    for part in range(GB):
        weight = jnp.exp2(stats[part, :SLOTS] - tops)
        totals = totals + stats[part, SLOTS : 2 * SLOTS] * weight
        deltas = deltas + stats[part, 2 * SLOTS : 3 * SLOTS] * weight
        sums = sums + stats[part, 3 * SLOTS :]
    latent[...] = sums
    tops = tops + jnp.log2(totals)
    deltas = deltas / totals
    for at in range(SLOTS):
        shift[at] = tops[at : at + 1]
        delta[at] = deltas[at : at + 1]
    qacc[...] = jnp.zeros_like(qacc)
    kacc[...] = jnp.zeros_like(kacc)
    vacc[...] = jnp.zeros_like(vacc)

    def step(p, carry):
        found = []
        for head in range(HEADS):
            for u in range(2):
                row, col, query, grad, key, scores, grad_scores = pair_of(lists, head, 2 * p + u, qg, kv)
                rat, cat = head * GB + row, head * GB + col
                weights = jnp.exp2(scores - shift[rat])
                dscore = (weights * (grad_scores - delta[rat])).astype(jnp.bfloat16)
                weights_low = weights.astype(jnp.bfloat16)
                found.append(
                    (
                        rat,
                        cat,
                        dot(dscore, key, ((0,), (0,))),
                        dot(dscore, query, ((1,), (0,))),
                        dot(weights_low, grad, ((1,), (0,))),
                    )
                )
        for rat, cat, qterm, kterm, vterm in found:
            qacc[rat] += qterm
            kacc[cat] += kterm
            vacc[cat] += vterm
        return carry

    lax.fori_loop(0, lists[2 * HEADS, 0] // 2, step, 0)
    for slot in range(GB):
        for head in range(HEADS):
            at, lanes = head * GB + slot, slice(head * DH, head * DH + DH)
            more = slice(WIDE + head * DH, WIDE + head * DH + DH)
            kvout = kvnear if slot < 8 else kvfar
            qout[slot, :, lanes] = qacc[at].astype(jnp.bfloat16)
            kvout[slot % 8, :, lanes] = kacc[at].astype(jnp.bfloat16)
            kvout[slot % 8, :, more] = vacc[at].astype(jnp.bfloat16)


def shape(*dims, dtype=jnp.bfloat16):
    return jax.ShapeDtypeStruct(dims, dtype)


def body(queries, keys, values, out_grad, token_error, block_mask):
    pair_side = lax.axis_index("pair")
    token_count = token_error.shape[1] * lax.axis_size("qb") * lax.axis_size("kb")
    qg, kv = pl.pallas_call(
        pack_kernel,
        out_shape=(shape(BLK, 2 * WIDE), shape(8, ROWS, 2 * WIDE)),
        in_specs=[VMEM] * 5,
        out_specs=(VMEM, VMEM),
        name="pack",
    )(queries, keys, values, out_grad, token_error)
    side = (lax.axis_index("qb") // 8).astype(jnp.int32).reshape(1)
    lists = pl.pallas_call(
        list_kernel,
        out_shape=shape(2 * HEADS + 1, LIST, dtype=jnp.int32),
        in_specs=[SMEM, SMEM],
        out_specs=SMEM,
        name="pair_lists",
    )(block_mask, side)
    near = lax.all_to_all(kv, "qb", 0, 0, axis_index_groups=Z_GROUPS)
    qg = lax.all_gather(qg, "kb", axis_index_groups=Y_GROUPS)
    far = lax.ppermute(near, "qb", Y_PAIRS)
    qg = lax.all_to_all(
        jnp.broadcast_to(qg[None], (4, 4, BLK, 2 * WIDE)), "kb", 0, 0, axis_index_groups=X_GROUPS
    ).reshape(GB, BLK, 2 * WIDE)

    row_scratch = pltpu.VMEM((SLOTS, 1, DH), jnp.float32)
    block_scratch = pltpu.VMEM((SLOTS, BLK, DH), jnp.float32)
    kv_scratch = pltpu.VMEM((GB, ROWS, 2 * WIDE), jnp.bfloat16)
    copies = pltpu.SemaphoreType.DMA((2,))
    stat = pl.pallas_call(
        stat_kernel,
        out_shape=shape(STAT, DH, dtype=jnp.float32),
        in_specs=[SMEM, VMEM, ANY, ANY],
        out_specs=VMEM,
        scratch_shapes=[kv_scratch, row_scratch, row_scratch, row_scratch, copies],
        compiler_params=PARAMS,
        name="row_stats",
    )(lists, qg, near, far)
    stats = lax.all_to_all(jnp.broadcast_to(stat[None], (GB, STAT, DH)), "kb", 0, 0)
    qpart, kvnear, kvfar, latent = pl.pallas_call(
        grad_kernel,
        out_shape=(
            shape(GB, BLK, WIDE),
            shape(8, BLK, 2 * WIDE),
            shape(8, BLK, 2 * WIDE),
            shape(8, DH, dtype=jnp.float32),
        ),
        in_specs=[SMEM, VMEM, ANY, ANY, VMEM],
        out_specs=(VMEM,) * 4,
        scratch_shapes=[kv_scratch, row_scratch, row_scratch, block_scratch, block_scratch, block_scratch, copies],
        compiler_params=PARAMS,
        name="grads",
    )(lists, qg, near, far, stats)

    own_latent = latent[0, 0]
    partner = lax.ppermute(latent, "pair", [(0, 1), (1, 0)])[0, 0]
    winner_mean = jnp.where(pair_side == 0, own_latent, partner) / token_count
    loser_mean = jnp.where(pair_side == 0, partner, own_latent) / token_count
    keep_share = jax.nn.sigmoid(-beta_pref * (loser_mean - winner_mean))
    factor = jnp.where(pair_side == 0, 1.0 + beta_pref * keep_share, -beta_pref * keep_share)

    kvmore = lax.ppermute(kvfar, "qb", Y_PAIRS)
    qpart = lax.all_to_all(qpart.reshape(4, 4, BLK, WIDE), "kb", 0, 0, axis_index_groups=X_GROUPS)
    qpart = jnp.sum(qpart.astype(jnp.float32), axis=0).astype(jnp.bfloat16)
    kvpart = (kvnear.astype(jnp.float32) + kvmore.astype(jnp.float32)).astype(jnp.bfloat16)
    kvpart = lax.all_to_all(kvpart, "qb", 0, 0, axis_index_groups=Z_GROUPS)
    qpart = lax.all_to_all(qpart, "kb", 0, 0, axis_index_groups=Y_GROUPS)
    kvsum = jnp.sum(kvpart.astype(jnp.float32), axis=0, keepdims=True) * factor
    qsum = jnp.sum(qpart.astype(jnp.float32), axis=0, keepdims=True)
    query_grad = (qsum * (factor * score_scale)).astype(jnp.bfloat16)
    key_grad = (kvsum[..., :WIDE] * score_scale).astype(jnp.bfloat16)
    value_grad = kvsum[..., WIDE:].astype(jnp.bfloat16)
    return (query_grad, key_grad, value_grad)


def solution(mesh):
    return jax.shard_map(
        body,
        mesh=mesh,
        in_specs=(
            P("pair", ("qb", "kb"), None),
            P("pair", ("kb", "qb"), None),
            P("pair", ("kb", "qb"), None),
            P("pair", ("qb", "kb"), None),
            P("pair", ("qb", "kb")),
            P(None, "qb", "kb"),
        ),
        out_specs=(
            P("pair", ("qb", "kb"), None),
            P("pair", ("kb", "qb"), None),
            P("pair", ("kb", "qb"), None),
        ),
        check_vma=False,
    )
```

time: 1270 us -> 202 us (0.16)
  blocking collectives: 844 us -> 72.7 us
  waiting for transfers between devices: 263 us -> 52.4 us
  local copies, waits for them, and re-layouts: 58.5 us -> 4.99 us
  other arithmetic: 54.3 us -> 3.67 us
  starting transfers between devices: 2.45 us -> 39.2 us
  matrix products: 26.2 us -> 0 us
  Pallas kernels: 0 us -> 23.9 us
  between operations: 17.1 us -> 3.44 us
    psum x2 -> x0, blocking collectives: 758 us -> none  [the longest x1 687 us: body(): own_latent = lax.psum(own_total, ('qb', 'kb'))]
    unnamed x10 -> x0, waiting for transfers between devices: 228 us -> none
    all_gather x2 -> x1, blocking collectives: 85.2 us -> 19.6 us  [body(): qg = lax.all_gather(qg, 'kb', axis_index_groups=Y_GROUPS)]
    all_to_all x0 -> x2, blocking collectives: none -> 53.1 us  [the longest x1 29.2 us: body(): lax.all_to_all(jnp.broadcast_to(stat[None], (GB, STAT, DH)), 'kb', 0, 0)]
    all_to_all x0 -> x4, waiting for transfers between devices: none -> 48.3 us  [the longest x1 19.1 us: body(): kvpart = lax.all_to_all(kvpart, 'qb', 0, 0, axis_index_groups=Z_GROUPS)]
    scatter-add x12 -> x0, other arithmetic: 36.2 us -> none  [the longest x10 31.5 us: segment_rows(): jnp.zeros((block_count,) + per_pair.shape[1:], jnp.float32).at[rows_at]]
    all_gather x4 -> x0, waiting for transfers between devices: 35 us -> none  [the longest x1 34.9 us: body(): lax.all_gather(values, 'qb', axis=1, tiled=True)]
    all_to_all x0 -> x4, starting transfers between devices: none -> 30.8 us  [the longest x1 12 us: body(): qpart = lax.all_to_all(qpart, 'kb', 0, 0, axis_index_groups=Y_GROUPS)]
  transfers between devices with their start and end apart: 8 -> 7, of which waited for: 4 -> 6; matrix products, arithmetic and copies ran while one was open for 11% -> 2% of each run, Pallas kernels for 0% -> 5%
where the time goes in v1:
time: 202 us; the launch traced here: 200 us
  blocking collectives  72.7 us (36%)
  waiting for transfers between devices  52.4 us (26%)
  starting transfers between devices  39.2 us (19%)
  Pallas kernels  23.9 us (12%)
  local copies, waits for them, and re-layouts  4.99 us (2%)
  other arithmetic  3.67 us (2%)
  between operations  3.44 us (2%)
    all_to_all x1, blocking collectives, body(): lax.all_to_all(jnp.broadcast_to(stat[None], (GB, STAT, DH)), 'kb', 0, 0)  29.2 us
    all_to_all x1, blocking collectives, body(): lax.all_to_all(qpart.reshape(4, 4, BLK, WIDE), 'kb', 0, 0, axis_index_gro...  24 us
    all_gather x1, blocking collectives, body(): qg = lax.all_gather(qg, 'kb', axis_index_groups=Y_GROUPS)  19.6 us
    all_to_all x1, waiting for transfers between devices, body(): kvpart = lax.all_to_all(kvpart, 'qb', 0, 0, axis_index_groups=Z_GROUPS)  19.1 us
    all_to_all x1, starting transfers between devices, body(): qpart = lax.all_to_all(qpart, 'kb', 0, 0, axis_index_groups=Y_GROUPS)  12 us
    all_to_all x1, waiting for transfers between devices, body(): near = lax.all_to_all(kv, 'qb', 0, 0, axis_index_groups=Z_GROUPS)  10.6 us
    all_to_all x1, waiting for transfers between devices, body(): lax.all_to_all(jnp.broadcast_to(qg[None], (4, 4, BLK, 2 * WIDE)), 'kb', 0...  10.6 us
    all_to_all x1, starting transfers between devices, body(): near = lax.all_to_all(kv, 'qb', 0, 0, axis_index_groups=Z_GROUPS)  10.4 us
  transfers between devices with their start and end apart: 7, of which 6 were waited for; matrix products, arithmetic and copies ran while one was open for 2% of the time, Pallas kernels for 5%

profile of v1, /device:TPU:6, one launch (start us, length us, event | category | flops | bytes accessed | tf_op | source)
XLA Modules:
  0.0 200.4 jit_solution(8400970553107997192)
XLA Ops:
  0.6 2.0 %pack.1 = (bf16[128,512]{1,0:T(8,128)(2,1)}, bf16[8,136,512]{2,1,0:T(8,128)(2,1)}) custom-call(bf16[1,128,256]{2,1,0:T(8,128)(2,1)} %queries.1, bf16[1,128,256]{2,1,0:T(8,128)(2,1)} %keys.1, bf16[1,128,256]{2,1,0:T(8,128)(2,1)} %values.1, bf16[1,128,256]{2,1,0:T(8,128)(2,1)} %out_grad.1, f32[1,128]{1,0:T(1,128)} %token_error.1), custom_call_target="tpu_custom_call" | custom-call | tf_op jit(solution)/shard_map/pack/pallas_call | solution.py:193
  2.7 10.4 %all-to-all-start.1 = ((bf16[8,136,512]{2,1,0:T(8,128)(2,1)}), bf16[8,136,512]{2,1,0:T(8,128)(2,1)S(1)}, u32[]{:S(2)}, u32[]{:S(2)}) async-start(bf16[8,136,512]{2,1,0:T(8,128)(2,1)} %get-tuple-element.10), calls=%async_computation.1 | async-start | bytes 2228224 | tf_op jit(solution)/shard_map/all_to_all | solution.py:208
  13.1 19.6 %all-gather = bf16[512,512]{1,0:T(8,128)(2,1)S(1)} all-gather(bf16[128,512]{1,0:T(8,128)(2,1)S(1)} %copy-done.3), channel_id=2, replica_groups={{0,8,16,24},{2,10,18,26},{4,12,20,28},{6,14,22,30},{1,9,17,25},{3,11,19..., dimensions={0}, use_global_device_ids=true | all-gather | bytes 655360 | tf_op jit(solution)/shard_map/all_gather | solution.py:209
  32.7 10.6 %all-to-all-done.1.near = bf16[8,136,512]{2,1,0:T(8,128)(2,1)S(1)} async-done(((bf16[8,136,512]{2,1,0:T(8,128)(2,1)}), bf16[8,136,512]{2,1,0:T(8,128)(2,1)S(1)}, u32[]{:S(2)}, u32[]{:S(2)}) %all-to-all-start.1) | async-done | bytes 1114144 | tf_op jit(solution)/shard_map/all_to_all | solution.py:208
  43.3 1.6 broadcast_in_dim.4
  44.8 4.8 %all-to-all-start = ((bf16[4,4,128,512]{3,2,1,0:T(8,128)(2,1)}), bf16[4,4,128,512]{3,2,1,0:T(8,128)(2,1)S(1)}, u32[]{:S(2)}, u32[]{:S(2)}) async-start(bf16[4,4,128,512]{3,2,1,0:T(8,128)(2,1)} %broadcast_in_dim.4), calls=%async_computation | async-start | bytes 4194304 | tf_op jit(solution)/shard_map/all_to_all | solution.py:211
  49.6 3.5 %collective-permute-start = (bf16[8,136,512]{2,1,0:T(8,128)(2,1)S(1)}, bf16[8,136,512]{2,1,0:T(8,128)(2,1)}, u32[]{:S(2)}, u32[]{:S(2)}) collective-permute-start(bf16[8,136,512]{2,1,0:T(8,128)(2,1)S(1)} %all-to-all-done.1.near), channel_id=1, source_target_pairs={{0,256},{32,288},{64,320},{96,352},{128,384},{160,416},{192,448},{... | collective-permute-start | bytes 3342344 | tf_op jit(solution)/shard_map/ppermute | solution.py:210
  53.1 10.3 %pair_lists.1.lists = s32[5,40]{1,0:T(8,128)} custom-call(s32[2,16,16]{2,1,0:T(8,128)} %mask.1, s32[1]{0:T(128)} %bitcast.side), custom_call_target="tpu_custom_call" | custom-call | tf_op jit(solution)/shard_map/pair_lists/pallas_call | solution.py:201
  63.5 10.6 %all-to-all-done = bf16[4,4,128,512]{3,2,1,0:T(8,128)(2,1)S(1)} async-done(((bf16[4,4,128,512]{3,2,1,0:T(8,128)(2,1)}), bf16[4,4,128,512]{3,2,1,0:T(8,128)(2,1)S(1)}, u32[]{:S(2)}, u32[]{:S(2)}) %all-to-all-start) | async-done | bytes 2097184 | tf_op jit(solution)/shard_map/all_to_all | solution.py:211
  74.1 3.5 %collective-permute-done.far = bf16[8,136,512]{2,1,0:T(8,128)(2,1)} collective-permute-done((bf16[8,136,512]{2,1,0:T(8,128)(2,1)S(1)}, bf16[8,136,512]{2,1,0:T(8,128)(2,1)}, u32[]{:S(2)}, u32[]{:S(2)}) %collective-permute-start) | collective-permute-done | bytes 1114144 | tf_op jit(solution)/shard_map/ppermute | solution.py:210
  77.5 0.7 copy-done.2
  78.2 3.5 %row_stats.1 = f32[104,128]{1,0:T(8,128)S(1)} custom-call(s32[5,40]{1,0:T(8,128)S(1)} %copy-done.2, bf16[16,128,512]{2,1,0:T(8,128)(2,1)S(1)} %bitcast.10, bf16[8,136,512]{2,1,0:T(8,128)(2,1)S(1)} %all-to-all-done.1.near, bf16[8,136,512]{2,1,0:T(8,128)(2,1)} %collective-permute-done.far), custom_call_target="tpu_custom_call" | custom-call | tf_op jit(solution)/shard_map/row_stats/pallas_call | solution.py:219
  81.7 0.1 broadcast_in_dim.5
  81.8 29.2 %all_to_all.30.stats = f32[16,104,128]{2,1,0:T(8,128)S(1)} all-to-all(f32[16,104,128]{2,1,0:T(8,128)S(1)} %broadcast_in_dim.5), channel_id=1, replica_groups=mesh['qb'=16,'kb'=16,'pair'=2] {'kb'}, dimensions={0} | all-to-all | bytes 1703936 | tf_op jit(solution)/shard_map/all_to_all | solution.py:228
  110.9 8.0 %grads.1 = (bf16[16,128,256]{2,1,0:T(8,128)(2,1)S(1)}, bf16[8,128,512]{2,1,0:T(8,128)(2,1)S(1)}, bf16[8,128,512]{2,1,0:T(8,128)(2,1)}, f32[8,128]{1,0:T(8,128)S(1)}) custom-call(s32[5,40]{1,0:T(8,128)S(1)} %copy-done.2, bf16[16,128,512]{2,1,0:T(8,128)(2,1)S(1)} %bitcast.11, bf16[8,136,512]{2,1,0:T(8,128)(2,1)S(1)} %all-to-all-done.1.near, ...), custom_call_target="tpu_custom_call" | custom-call | tf_op jit(solution)/shard_map/grads/pallas_call | solution.py:229
  119.0 1.0 copy-done
  120.0 3.1 %collective-permute-start.2 = (bf16[8,128,512]{2,1,0:T(8,128)(2,1)}, bf16[8,128,512]{2,1,0:T(8,128)(2,1)S(1)}, u32[]{:S(2)}, u32[]{:S(2)}) collective-permute-start(bf16[8,128,512]{2,1,0:T(8,128)(2,1)} %get-tuple-element.14), channel_id=1, source_target_pairs={{0,256},{32,288},{64,320},{96,352},{128,384},{160,416},{192,448},{... | collective-permute-start | bytes 3145736 | tf_op jit(solution)/shard_map/ppermute | solution.py:251
  123.1 24.0 %all_to_all.31 = bf16[4,4,128,256]{3,2,1,0:T(8,128)(2,1)S(1)} all-to-all(bf16[4,4,128,256]{3,2,1,0:T(8,128)(2,1)S(1)} %bitcast.12), channel_id=1, replica_groups={{0,2,4,6},{8,10,12,14},{16,18,20,22},{24,26,28,30},{1,3,5,7},{9,11,13,1..., dimensions={0} | all-to-all | bytes 2097152 | tf_op jit(solution)/shard_map/all_to_all | solution.py:252
  147.0 0.9 reduce_sum.30
  147.9 12.0 %all-to-all-start.4 = ((bf16[4,128,256]{2,1,0:T(8,128)(2,1)}), bf16[4,128,256]{2,1,0:T(8,128)(2,1)S(1)}, u32[]{:S(2)}, u32[]{:S(2)}) async-start(bf16[4,128,256]{2,1,0:T(8,128)(2,1)} %reduce_sum.30), calls=%async_computation.4 | async-start | bytes 524288 | tf_op jit(solution)/shard_map/all_to_all | solution.py:256
  160.0 1.3 add_convert_fusion
  161.3 8.1 %all-to-all-done.4 = bf16[4,128,256]{2,1,0:T(8,128)(2,1)S(1)} async-done(((bf16[4,128,256]{2,1,0:T(8,128)(2,1)}), bf16[4,128,256]{2,1,0:T(8,128)(2,1)S(1)}, u32[]{:S(2)}, u32[]{:S(2)}) %all-to-all-start.4) | async-done | bytes 262176 | tf_op jit(solution)/shard_map/all_to_all | solution.py:256
  169.3 3.6 %all-to-all-start.5 = ((bf16[8,128,512]{2,1,0:T(8,128)(2,1)}), bf16[8,128,512]{2,1,0:T(8,128)(2,1)S(1)}, u32[]{:S(2)}, u32[]{:S(2)}) async-start(bf16[8,128,512]{2,1,0:T(8,128)(2,1)} %add_convert_fusion), calls=%async_computation.5 | async-start | bytes 2097152 | tf_op jit(solution)/shard_map/all_to_all | solution.py:255
  172.9 1.9 collective-permute-start.1
  174.8 0.5 slice.14
  175.3 0.6 collective-permute-done.1
  175.9 0.5 slice.13
  179.2 0.6 fusion.1
  179.8 19.1 %all-to-all-done.5 = bf16[8,128,512]{2,1,0:T(8,128)(2,1)S(1)} async-done(((bf16[8,128,512]{2,1,0:T(8,128)(2,1)}), bf16[8,128,512]{2,1,0:T(8,128)(2,1)S(1)}, u32[]{:S(2)}, u32[]{:S(2)}) %all-to-all-start.5) | async-done | bytes 1048608 | tf_op jit(solution)/shard_map/all_to_all | solution.py:255
  198.9 0.1 convert_reduce_fusion
  199.1 0.6 slice.23
  199.7 0.6 fusion
  (9 shorter events, 0.1 us)
Async XLA Ops:
  2.7 10.5 %copy-start.3 = (bf16[128,512]{1,0:T(8,128)(2,1)S(1)}, bf16[128,512]{1,0:T(8,128)(2,1)}, u32[]{:S(2)}) copy-start(bf16[128,512]{1,0:T(8,128)(2,1)} %get-tuple-element.9) | copy-start | bytes 393220
  2.7 40.6 %all-to-all-start.1 = ((bf16[8,136,512]{2,1,0:T(8,128)(2,1)}), bf16[8,136,512]{2,1,0:T(8,128)(2,1)S(1)}, u32[]{:S(2)}, u32[]{:S(2)}) async-start(bf16[8,136,512]{2,1,0:T(8,128)(2,1)} %get-tuple-element.10), calls=%async_computation.1 | async-start | bytes 2228224 | tf_op jit(solution)/shard_map/all_to_all | solution.py:208
  44.8 29.2 %all-to-all-start = ((bf16[4,4,128,512]{3,2,1,0:T(8,128)(2,1)}), bf16[4,4,128,512]{3,2,1,0:T(8,128)(2,1)S(1)}, u32[]{:S(2)}, u32[]{:S(2)}) async-start(bf16[4,4,128,512]{3,2,1,0:T(8,128)(2,1)} %broadcast_in_dim.4), calls=%async_computation | async-start | bytes 4194304 | tf_op jit(solution)/shard_map/all_to_all | solution.py:211
  49.6 27.9 %collective-permute-start = (bf16[8,136,512]{2,1,0:T(8,128)(2,1)S(1)}, bf16[8,136,512]{2,1,0:T(8,128)(2,1)}, u32[]{:S(2)}, u32[]{:S(2)}) collective-permute-start(bf16[8,136,512]{2,1,0:T(8,128)(2,1)S(1)} %all-to-all-done.1.near), channel_id=1, source_target_pairs={{0,256},{32,288},{64,320},{96,352},{128,384},{160,416},{192,448},{... | collective-permute-start | bytes 3342344 | tf_op jit(solution)/shard_map/ppermute | solution.py:210
  77.5 0.7 copy-start.2
  119.0 1.0 copy-start
  120.0 40.0 %copy-start.1 = (bf16[8,128,512]{2,1,0:T(8,128)(2,1)S(1)}, bf16[8,128,512]{2,1,0:T(8,128)(2,1)}, u32[]{:S(2)}) copy-start(bf16[8,128,512]{2,1,0:T(8,128)(2,1)} %copy-done) | copy-start | bytes 3145732
  120.0 40.0 %collective-permute-start.2 = (bf16[8,128,512]{2,1,0:T(8,128)(2,1)}, bf16[8,128,512]{2,1,0:T(8,128)(2,1)S(1)}, u32[]{:S(2)}, u32[]{:S(2)}) collective-permute-start(bf16[8,128,512]{2,1,0:T(8,128)(2,1)} %get-tuple-element.14), channel_id=1, source_target_pairs={{0,256},{32,288},{64,320},{96,352},{128,384},{160,416},{192,448},{... | collective-permute-start | bytes 3145736 | tf_op jit(solution)/shard_map/ppermute | solution.py:251
  147.9 21.4 %all-to-all-start.4 = ((bf16[4,128,256]{2,1,0:T(8,128)(2,1)}), bf16[4,128,256]{2,1,0:T(8,128)(2,1)S(1)}, u32[]{:S(2)}, u32[]{:S(2)}) async-start(bf16[4,128,256]{2,1,0:T(8,128)(2,1)} %reduce_sum.30), calls=%async_computation.4 | async-start | bytes 524288 | tf_op jit(solution)/shard_map/all_to_all | solution.py:256
  169.3 29.6 %all-to-all-start.5 = ((bf16[8,128,512]{2,1,0:T(8,128)(2,1)}), bf16[8,128,512]{2,1,0:T(8,128)(2,1)S(1)}, u32[]{:S(2)}, u32[]{:S(2)}) async-start(bf16[8,128,512]{2,1,0:T(8,128)(2,1)} %add_convert_fusion), calls=%async_computation.5 | async-start | bytes 2097152 | tf_op jit(solution)/shard_map/all_to_all | solution.py:255
  172.9 3.1 %collective-permute-start.1 = (f32[8,128]{1,0:T(8,128)S(1)}, f32[8,128]{1,0:T(8,128)S(1)}, u32[]{:S(2)}, u32[]{:S(2)}) collective-permute-start(f32[8,128]{1,0:T(8,128)S(1)} %get-tuple-element.12), channel_id=1, source_target_pairs={{0,1},{1,0},{2,3},{3,2},{4,5},{5,4},{6,7},{7,6},{8,9},{9,8},{10,11... | collective-permute-start | bytes 12296 | tf_op jit(solution)/shard_map/ppermute | solution.py:245

commit v2 on v1

v2 whole, which is shorter than its diff:
```python
import jax
import jax.numpy as jnp
from jax import lax
from jax.experimental import pallas as pl
from jax.experimental.pallas import tpu as pltpu
from jax.sharding import PartitionSpec as P

DH = 128
HEADS = 2
BLK = 128
GB = 16
WIDE = HEADS * DH
ROWS = BLK + 16
SLOTS = HEADS * GB
STAT = 3 * SLOTS + 8
LIST = 40

beta_pref = 20.0
neg_big = -1e30
score_scale = DH ** (-0.5)
log2_scale = score_scale * 1.4426950408889634

Y_GROUPS = [[x + 4 * y for y in range(4)] for x in range(4)]
X_GROUPS = [[x + 4 * y for x in range(4)] for y in range(4)]
Z_GROUPS = [[z + 8 * y for z in range(8)] for y in range(2)]
Y_PAIRS = [(s, s ^ 8) for s in range(16)]

VMEM = pl.BlockSpec(memory_space=pltpu.VMEM)
SMEM = pl.BlockSpec(memory_space=pltpu.SMEM)
PARAMS = pltpu.CompilerParams(vmem_limit_bytes=40 * 1024 * 1024)


def dot(a, b, dims):
    return lax.dot_general(a, b, (dims, ((), ())), preferred_element_type=jnp.float32)


def pack_kernel(queries, keys, values, out_grad, token_error, qg_ref, kv_ref):
    qg_ref[:, :WIDE] = queries[0]
    qg_ref[:, WIDE:] = out_grad[0]
    total = jnp.sum(token_error[...], axis=1, keepdims=True)
    high = total.astype(jnp.bfloat16).astype(jnp.float32)
    rest = total - high
    middle = rest.astype(jnp.bfloat16).astype(jnp.float32)
    low = rest - middle
    row = lax.broadcasted_iota(jnp.int32, (16, 2 * WIDE), 0)
    sums = jnp.where(row == 0, high, jnp.where(row == 1, middle, jnp.where(row == 2, low, 0.0)))
    kv_ref[:BLK, :WIDE] = keys[0]
    kv_ref[:BLK, WIDE:] = values[0]
    kv_ref[BLK:, :] = sums.astype(jnp.bfloat16)


def list_kernel(mask, side, lists):
    flip = side[0]
    for head in range(HEADS):

        def step(row, count):
            first = ((row & 3) * 4 + (row >> 2)) * GB
            for col in range(GB):
                lists[head, count] = first + (2 * (col % 8) + ((col // 8) ^ flip))
                count = jnp.minimum(count + mask[head, row, col], LIST - 1)
            return count

        lists[HEADS, head] = lax.fori_loop(0, GB, step, 0)


def pair_of(lists, head, at, qg, kv):
    both = lists[head, at]
    row, col = both >> 4, both & 15
    first, second = head * DH, WIDE + head * DH
    query, grad = qg[row, :, first : first + DH], qg[row, :, second : second + DH]
    key, value = kv[col, :BLK, first : first + DH], kv[col, :BLK, second : second + DH]
    scores = dot(key, query, ((1,), (1,))) * log2_scale
    grad_scores = dot(value, grad, ((1,), (1,)))
    return row, col, query, grad, scores, grad_scores


def stat_kernel(lists, qg, kv, stats, top, total, delta):
    top[...] = jnp.full_like(top, neg_big)
    total[...] = jnp.zeros_like(total)
    delta[...] = jnp.zeros_like(delta)

    def step(p, carry):
        found = []
        for head in range(HEADS):
            for u in range(2):
                row, _, _, _, scores, grad_scores = pair_of(lists, head, 2 * p + u, qg, kv)
                own_top = jnp.max(scores, axis=0, keepdims=True)
                shifted = jnp.exp2(scores - own_top)
                own_total = jnp.sum(shifted, axis=0, keepdims=True)
                own_delta = jnp.sum(shifted * grad_scores, axis=0, keepdims=True)
                found.append((head * GB + row, own_top, own_total, own_delta))
        for at, own_top, own_total, own_delta in found:
            old_top = top[at]
            new_top = jnp.maximum(old_top, own_top)
            old_weight = jnp.exp2(old_top - new_top)
            own_weight = jnp.exp2(own_top - new_top)
            top[at] = new_top
            total[at] = total[at] * old_weight + own_total * own_weight
            delta[at] = delta[at] * old_weight + own_delta * own_weight
        return carry

    lax.fori_loop(0, lists[HEADS, 0] // 2, step, 0)
    for at in range(SLOTS):
        stats[0, at : at + 1, :] = top[at]
        stats[0, SLOTS + at : SLOTS + at + 1, :] = total[at]
        stats[0, 2 * SLOTS + at : 2 * SLOTS + at + 1, :] = delta[at]
    sums = kv[0, BLK:, :DH].astype(jnp.float32)
    for slot in range(1, GB):
        sums = sums + kv[slot, BLK:, :DH].astype(jnp.float32)
    sums = jnp.sum(sums, axis=0, keepdims=True)
    stats[0, 3 * SLOTS :, :] = jnp.broadcast_to(sums, (8, DH))
    own = stats[0]
    for part in range(1, GB):
        stats[part] = own


def key_kernel(lists, qg, kv, stats, kvout, dscores, latent, shift, delta, kacc, vacc):
    tops = stats[0, :SLOTS]
    for part in range(1, GB):
        tops = jnp.maximum(tops, stats[part, :SLOTS])
    totals = jnp.zeros_like(tops)
    deltas = jnp.zeros_like(tops)
    sums = jnp.zeros((8, DH), jnp.float32)
    for part in range(GB):
        weight = jnp.exp2(stats[part, :SLOTS] - tops)
        totals = totals + stats[part, SLOTS : 2 * SLOTS] * weight
        deltas = deltas + stats[part, 2 * SLOTS : 3 * SLOTS] * weight
        sums = sums + stats[part, 3 * SLOTS :]
    latent[...] = sums
    tops = tops + jnp.log2(totals)
    deltas = deltas / totals
    for at in range(SLOTS):
        shift[at] = tops[at : at + 1]
        delta[at] = deltas[at : at + 1]
    kacc[...] = jnp.zeros_like(kacc)
    vacc[...] = jnp.zeros_like(vacc)

    def step(p, carry):
        found = []
        for head in range(HEADS):
            for u in range(2):
                row, col, query, grad, scores, grad_scores = pair_of(lists, head, 2 * p + u, qg, kv)
                rat, cat = head * GB + row, head * GB + col
                weights = jnp.exp2(scores - shift[rat])
                dscore = (weights * (grad_scores - delta[rat])).astype(jnp.bfloat16)
                weights_low = weights.astype(jnp.bfloat16)
                dscores[head, 2 * p + u] = dscore
                found.append((cat, dot(dscore, query, ((1,), (0,))), dot(weights_low, grad, ((1,), (0,)))))
        for cat, kterm, vterm in found:
            kacc[cat] += kterm
            vacc[cat] += vterm
        return carry

    lax.fori_loop(0, lists[HEADS, 0] // 2, step, 0)
    for slot in range(GB):
        for head in range(HEADS):
            first, second = head * DH, WIDE + head * DH
            kvout[slot, :, first : first + DH] = kacc[head * GB + slot].astype(jnp.bfloat16)
            kvout[slot, :, second : second + DH] = vacc[head * GB + slot].astype(jnp.bfloat16)


def query_kernel(lists, kv, dscores, qout, qacc):
    qacc[...] = jnp.zeros_like(qacc)

    def step(p, carry):
        found = []
        for head in range(HEADS):
            for u in range(2):
                both = lists[head, 2 * p + u]
                key = kv[both & 15, :BLK, head * DH : head * DH + DH]
                found.append((head * GB + (both >> 4), dot(dscores[head, 2 * p + u], key, ((0,), (0,)))))
        for rat, qterm in found:
            qacc[rat] += qterm
        return carry

    lax.fori_loop(0, lists[HEADS, 0] // 2, step, 0)
    for slot in range(GB):
        for head in range(HEADS):
            qout[slot, :, head * DH : head * DH + DH] = qacc[head * GB + slot].astype(jnp.bfloat16)


def shape(*dims, dtype=jnp.bfloat16):
    return jax.ShapeDtypeStruct(dims, dtype)


def body(queries, keys, values, out_grad, token_error, block_mask):
    pair_side = lax.axis_index("pair")
    token_count = token_error.shape[1] * lax.axis_size("qb") * lax.axis_size("kb")
    qg, kv = pl.pallas_call(
        pack_kernel,
        out_shape=(shape(BLK, 2 * WIDE), shape(ROWS, 2 * WIDE)),
        in_specs=[VMEM] * 5,
        out_specs=(VMEM, VMEM),
        name="pack",
    )(queries, keys, values, out_grad, token_error)
    side = (lax.axis_index("qb") // 8).astype(jnp.int32).reshape(1)
    lists = pl.pallas_call(
        list_kernel,
        out_shape=shape(HEADS + 1, LIST, dtype=jnp.int32),
        in_specs=[SMEM, SMEM],
        out_specs=SMEM,
        name="pair_lists",
    )(block_mask, side)
    far = lax.ppermute(kv, "qb", Y_PAIRS)
    kv = lax.all_gather(jnp.stack([kv, far]), "qb", axis_index_groups=Z_GROUPS).reshape(GB, ROWS, 2 * WIDE)
    qg = lax.all_gather(qg, "kb", axis_index_groups=Y_GROUPS)
    qg = lax.all_to_all(
        jnp.broadcast_to(qg[None], (4, 4, BLK, 2 * WIDE)), "kb", 0, 0, axis_index_groups=X_GROUPS
    ).reshape(GB, BLK, 2 * WIDE)

    row_scratch = pltpu.VMEM((SLOTS, 1, DH), jnp.float32)
    block_scratch = pltpu.VMEM((SLOTS, BLK, DH), jnp.float32)
    stats = pl.pallas_call(
        stat_kernel,
        out_shape=shape(GB, STAT, DH, dtype=jnp.float32),
        in_specs=[SMEM, VMEM, VMEM],
        out_specs=VMEM,
        scratch_shapes=[row_scratch, row_scratch, row_scratch],
        compiler_params=PARAMS,
        name="row_stats",
    )(lists, qg, kv)
    stats = lax.all_to_all(stats, "kb", 0, 0)
    kvpart, dscores, latent = pl.pallas_call(
        key_kernel,
        out_shape=(
            shape(GB, BLK, 2 * WIDE),
            shape(HEADS, 2 * GB, BLK, BLK),
            shape(8, DH, dtype=jnp.float32),
        ),
        in_specs=[SMEM, VMEM, VMEM, VMEM],
        out_specs=(VMEM,) * 3,
        scratch_shapes=[row_scratch, row_scratch, block_scratch, block_scratch],
        compiler_params=PARAMS,
        name="key_value_grads",
    )(lists, qg, kv, stats)
    kvpart = lax.psum_scatter(
        kvpart.reshape(8, 2 * BLK, 2 * WIDE), "qb", scatter_dimension=0, axis_index_groups=Z_GROUPS
    )
    qpart = pl.pallas_call(
        query_kernel,
        out_shape=shape(GB, BLK, WIDE),
        in_specs=[SMEM, VMEM, VMEM],
        out_specs=VMEM,
        scratch_shapes=[block_scratch],
        compiler_params=PARAMS,
        name="query_grads",
    )(lists, kv, dscores)

    own_latent = latent[0, 0]
    partner = lax.ppermute(latent, "pair", [(0, 1), (1, 0)])[0, 0]
    winner_mean = jnp.where(pair_side == 0, own_latent, partner) / token_count
    loser_mean = jnp.where(pair_side == 0, partner, own_latent) / token_count
    keep_share = jax.nn.sigmoid(-beta_pref * (loser_mean - winner_mean))
    factor = jnp.where(pair_side == 0, 1.0 + beta_pref * keep_share, -beta_pref * keep_share)

    qpart = lax.all_to_all(qpart.reshape(4, 4, BLK, WIDE), "kb", 0, 0, axis_index_groups=X_GROUPS)
    qpart = jnp.sum(qpart.astype(jnp.float32), axis=0).astype(jnp.bfloat16)
    qpart = lax.all_to_all(qpart, "kb", 0, 0, axis_index_groups=Y_GROUPS)
    qsum = jnp.sum(qpart.astype(jnp.float32), axis=0, keepdims=True)
    query_grad = (qsum * (factor * score_scale)).astype(jnp.bfloat16)

    far = lax.ppermute(kvpart[BLK:], "qb", Y_PAIRS)
    kvsum = (kvpart[:BLK].astype(jnp.float32) + far.astype(jnp.float32))[None] * factor
    key_grad = (kvsum[..., :WIDE] * score_scale).astype(jnp.bfloat16)
    value_grad = kvsum[..., WIDE:].astype(jnp.bfloat16)
    return (query_grad, key_grad, value_grad)


def solution(mesh):
    return jax.shard_map(
        body,
        mesh=mesh,
        in_specs=(
            P("pair", ("qb", "kb"), None),
            P("pair", ("kb", "qb"), None),
            P("pair", ("kb", "qb"), None),
            P("pair", ("qb", "kb"), None),
            P("pair", ("qb", "kb")),
            P(None, "qb", "kb"),
        ),
        out_specs=(
            P("pair", ("qb", "kb"), None),
            P("pair", ("kb", "qb"), None),
            P("pair", ("kb", "qb"), None),
        ),
        check_vma=False,
    )
```

time: 202 us -> 181 us (0.90)
  starting transfers between devices: 39.2 us -> 16.8 us
  between operations: 3.44 us -> 16.8 us
  Pallas kernels: 23.9 us -> 13.2 us
  local copies, waits for them, and re-layouts: 4.99 us -> 12.3 us
  waiting for transfers between devices: 52.4 us -> 45.7 us
  blocking collectives: 72.7 us -> 70.3 us
    all_to_all x2 -> x0, waiting for transfers between devices: 29.7 us -> none  [the longest x1 19.1 us: body(): kvpart = lax.all_to_all(kvpart, 'qb', 0, 0, axis_index_groups=Z_GROUPS)]
    reduce_scatter x0 -> x1, waiting for transfers between devices: none -> 14.3 us  [body(): lax.psum_scatter(kvpart.reshape(8, 2 * BLK, 2 * WIDE), 'qb', scatter_dime...]
    all_to_all x2 -> x0, starting transfers between devices: 14 us -> none  [the longest x1 10.4 us: body(): near = lax.all_to_all(kv, 'qb', 0, 0, axis_index_groups=Z_GROUPS)]
    pallas_call x4 -> x5, Pallas kernels: 23.9 us -> 13.2 us  [the longest x1 4.52 us: body(): pl.pallas_call(key_kernel, out_shape=(shape(GB, BLK, 2 * WIDE), shape(HEA...]
    all_to_all x1, starting transfers between devices: 12 us -> 3.41 us  [body(): qpart = lax.all_to_all(qpart, 'kb', 0, 0, axis_index_groups=Y_GROUPS)]
    all_to_all x1, waiting for transfers between devices: 10.6 us -> 17.2 us  [body(): lax.all_to_all(jnp.broadcast_to(qg[None], (4, 4, BLK, 2 * WIDE)), 'kb', 0...]
    unnamed x8 -> x18, local copies, waits for them, and re-layouts: 1.71 us -> 8.21 us
    all_to_all x1, waiting for transfers between devices: 8.06 us -> 2.8 us  [body(): qpart = lax.all_to_all(qpart, 'kb', 0, 0, axis_index_groups=Y_GROUPS)]
  transfers between devices with their start and end apart: 7 -> 7, of which waited for: 6 -> 7; matrix products, arithmetic and copies ran while one was open for 2% -> 2% of each run, Pallas kernels for 5% -> 3%
where the time goes in v2:
time: 181 us; the launch traced here: 180 us
  blocking collectives  70.3 us (39%)
  waiting for transfers between devices  45.7 us (25%)
  starting transfers between devices  16.8 us (9%)
  between operations  16.8 us (9%)
  Pallas kernels  13.2 us (7%)
  local copies, waits for them, and re-layouts  12.3 us (7%)
  other arithmetic  4.82 us (3%)
    all_to_all x1, blocking collectives, body(): stats = lax.all_to_all(stats, 'kb', 0, 0)  26.9 us
    all_to_all x1, blocking collectives, body(): lax.all_to_all(qpart.reshape(4, 4, BLK, WIDE), 'kb', 0, 0, axis_index_gro...  23.9 us
    all_gather x1, blocking collectives, body(): qg = lax.all_gather(qg, 'kb', axis_index_groups=Y_GROUPS)  19.5 us
    all_to_all x1, waiting for transfers between devices, body(): lax.all_to_all(jnp.broadcast_to(qg[None], (4, 4, BLK, 2 * WIDE)), 'kb', 0...  17.2 us
    reduce_scatter x1, waiting for transfers between devices, body(): lax.psum_scatter(kvpart.reshape(8, 2 * BLK, 2 * WIDE), 'qb', scatter_dime...  14.3 us
    unnamed x18, local copies, waits for them, and re-layouts  8.21 us
    all_to_all x1, starting transfers between devices, body(): lax.all_to_all(jnp.broadcast_to(qg[None], (4, 4, BLK, 2 * WIDE)), 'kb', 0...  4.77 us
    pallas_call x1, Pallas kernels, body(): pl.pallas_call(key_kernel, out_shape=(shape(GB, BLK, 2 * WIDE), shape(HEA...  4.52 us
  transfers between devices with their start and end apart: 7, of which 7 were waited for; matrix products, arithmetic and copies ran while one was open for 2% of the time, Pallas kernels for 3%

profile of v2, /device:TPU:6, one launch (start us, length us, event | category | flops | bytes accessed | tf_op | source)
XLA Modules:
  0.0 180.0 jit_solution(17923855427667699658)
XLA Ops:
  7.2 1.7 pack.1
  8.9 3.5 %collective-permute-start = (bf16[144,512]{1,0:T(8,128)(2,1)}, bf16[144,512]{1,0:T(8,128)(2,1)S(1)}, u32[]{:S(2)}, u32[]{:S(2)}) collective-permute-start(bf16[144,512]{1,0:T(8,128)(2,1)} %get-tuple-element.8), channel_id=1, source_target_pairs={{0,256},{32,288},{64,320},{96,352},{128,384},{160,416},{192,448},{... | collective-permute-start | bytes 442376 | tf_op jit(solution)/shard_map/ppermute | solution.py:204
  12.4 4.2 %collective-permute-done = bf16[144,512]{1,0:T(8,128)(2,1)S(1)} collective-permute-done((bf16[144,512]{1,0:T(8,128)(2,1)}, bf16[144,512]{1,0:T(8,128)(2,1)S(1)}, u32[]{:S(2)}, u32[]{:S(2)}) %collective-permute-start) | collective-permute-done | bytes 147488 | tf_op jit(solution)/shard_map/ppermute | solution.py:204
  16.6 1.6 pad_maximum_fusion
  18.2 19.5 %all-gather.1 = bf16[512,512]{1,0:T(8,128)(2,1)S(1)} all-gather(bf16[128,512]{1,0:T(8,128)(2,1)} %get-tuple-element.9), channel_id=3, replica_groups={{0,8,16,24},{2,10,18,26},{4,12,20,28},{6,14,22,30},{1,9,17,25},{3,11,19..., dimensions={0}, use_global_device_ids=true | all-gather | bytes 655360 | tf_op jit(solution)/shard_map/all_gather | solution.py:206
  37.8 1.5 broadcast_in_dim.2
  39.3 4.8 %all-to-all-start = ((bf16[4,4,128,512]{3,2,1,0:T(8,128)(2,1)}), bf16[4,4,128,512]{3,2,1,0:T(8,128)(2,1)S(1)}, u32[]{:S(2)}, u32[]{:S(2)}) async-start(bf16[4,4,128,512]{3,2,1,0:T(8,128)(2,1)} %broadcast_in_dim.2), calls=%async_computation | async-start | bytes 4194304 | tf_op jit(solution)/shard_map/all_to_all | solution.py:207
  44.1 3.2 %pair_lists.1.lists = s32[3,40]{1,0:T(4,128)} custom-call(s32[2,16,16]{2,1,0:T(8,128)} %mask.1, s32[1]{0:T(128)} %bitcast.side), custom_call_target="tpu_custom_call" | custom-call | tf_op jit(solution)/shard_map/pair_lists/pallas_call | solution.py:197
  47.3 17.2 %all-to-all-done = bf16[4,4,128,512]{3,2,1,0:T(8,128)(2,1)S(1)} async-done(((bf16[4,4,128,512]{3,2,1,0:T(8,128)(2,1)}), bf16[4,4,128,512]{3,2,1,0:T(8,128)(2,1)S(1)}, u32[]{:S(2)}, u32[]{:S(2)}) %all-to-all-start) | async-done | bytes 2097184 | tf_op jit(solution)/shard_map/all_to_all | solution.py:207
  64.5 3.6 %all-gather.4.cloned.1.call-done.kv = bf16[16,144,512]{2,1,0:T(8,128)(2,1)} async-done(((bf16[2,144,512]{2,1,0:T(8,128)(2,1)}), bf16[16,144,512]{2,1,0:T(8,128)(2,1)}) %all-gather.4.cloned.1.call-update) | async-done | bytes 2359312 | tf_op jit(solution)/shard_map/all_gather | solution.py:205
  68.1 1.7 copy-done
  69.8 0.7 copy-done.7
  70.5 2.1 %row_stats.1 = f32[16,104,128]{2,1,0:T(8,128)S(1)} custom-call(s32[3,40]{1,0:T(4,128)S(1)} %copy-done.7, bf16[16,128,512]{2,1,0:T(8,128)(2,1)S(1)} %bitcast.20, bf16[16,144,512]{2,1,0:T(8,128)(2,1)S(1)} %copy-done), custom_call_target="tpu_custom_call" | custom-call | tf_op jit(solution)/shard_map/row_stats/pallas_call | solution.py:213
  72.5 26.9 %all_to_all.20.stats = f32[16,104,128]{2,1,0:T(8,128)S(1)} all-to-all(f32[16,104,128]{2,1,0:T(8,128)S(1)} %row_stats.1), channel_id=1, replica_groups=mesh['qb'=16,'kb'=16,'pair'=2] {'kb'}, dimensions={0} | all-to-all | bytes 1703936 | tf_op jit(solution)/shard_map/all_to_all | solution.py:222
  99.4 1.6 copy-done.3
  101.0 4.5 %key_value_grads.1 = (bf16[16,128,512]{2,1,0:T(8,128)(2,1)S(1)}, bf16[2,32,128,128]{3,2,1,0:T(8,128)(2,1)S(1)}, f32[8,128]{1,0:T(8,128)S(1)}) custom-call(s32[3,40]{1,0:T(4,128)S(1)} %copy-done.8, bf16[16,128,512]{2,1,0:T(8,128)(2,1)S(1)} %bitcast.21, bf16[16,144,512]{2,1,0:T(8,128)(2,1)S(1)} %copy-done, f32[16,104,128]{2,1,0:T(8,128)S(1)} %all_to_all.20.stats), custom_call_target="tpu_custom_call" | custom-call | tf_op jit(solution)/shard_map/key_value_grads/pallas_call | solution.py:223
  105.6 1.4 copy-done.4
  106.9 1.3 copy-done.6
  108.3 1.6 copy-done.5
  109.9 1.7 query_grads.1
  111.6 23.9 %all_to_all.21 = bf16[4,4,128,256]{3,2,1,0:T(8,128)(2,1)S(1)} all-to-all(bf16[4,4,128,256]{3,2,1,0:T(8,128)(2,1)S(1)} %bitcast.22), channel_id=1, replica_groups={{0,2,4,6},{8,10,12,14},{16,18,20,22},{24,26,28,30},{1,3,5,7},{9,11,13,1..., dimensions={0} | all-to-all | bytes 2097152 | tf_op jit(solution)/shard_map/all_to_all | solution.py:256
  135.5 0.9 reduce_sum.21
  136.4 3.4 %all-to-all-start.3 = ((bf16[4,128,256]{2,1,0:T(8,128)(2,1)}), bf16[4,128,256]{2,1,0:T(8,128)(2,1)S(1)}, u32[]{:S(2)}, u32[]{:S(2)}) async-start(bf16[4,128,256]{2,1,0:T(8,128)(2,1)} %reduce_sum.21), calls=%async_computation.3 | async-start | bytes 524288 | tf_op jit(solution)/shard_map/all_to_all | solution.py:258
  139.8 1.9 %collective-permute-start.1 = (f32[8,128]{1,0:T(8,128)S(1)}, f32[8,128]{1,0:T(8,128)S(1)}, u32[]{:S(2)}, u32[]{:S(2)}) collective-permute-start(f32[8,128]{1,0:T(8,128)S(1)} %get-tuple-element.11), channel_id=1, source_target_pairs={{0,1},{1,0},{2,3},{3,2},{4,5},{5,4},{6,7},{7,6},{8,9},{9,8},{10,11... | collective-permute-start | bytes 12296 | tf_op jit(solution)/shard_map/ppermute | solution.py:250
  146.1 2.8 %all-to-all-done.3 = bf16[4,128,256]{2,1,0:T(8,128)(2,1)S(1)} async-done(((bf16[4,128,256]{2,1,0:T(8,128)(2,1)}), bf16[4,128,256]{2,1,0:T(8,128)(2,1)S(1)}, u32[]{:S(2)}, u32[]{:S(2)}) %all-to-all-start.3) | async-done | bytes 262176 | tf_op jit(solution)/shard_map/all_to_all | solution.py:258
  148.9 14.3 %reduce-scatter.2.cloned.1.call-done = bf16[1,256,512]{2,1,0:T(8,128)(2,1)} async-done(((bf16[8,256,512]{2,1,0:T(8,128)(2,1)}), bf16[1,256,512]{2,1,0:T(8,128)(2,1)}) %reduce-scatter.2.cloned.1.call-update) | async-done | bytes 262160 | tf_op jit(solution)/shard_map/reduce_scatter | solution.py:236
  163.2 0.9 slice_bitcast_fusion
  164.1 3.2 %collective-permute-start.2 = (bf16[128,512]{1,0:T(8,128)(2,1)S(1)}, bf16[128,512]{1,0:T(8,128)(2,1)S(1)}, u32[]{:S(2)}, u32[]{:S(2)}) collective-permute-start(bf16[128,512]{1,0:T(8,128)(2,1)S(1)} %slice_bitcast_fusion), channel_id=1, source_target_pairs={{0,256},{32,288},{64,320},{96,352},{128,384},{160,416},{192,448},{... | collective-permute-start | bytes 393224 | tf_op jit(solution)/shard_map/ppermute | solution.py:262
  167.3 0.6 fusion.3
  167.9 3.0 %collective-permute-done.2 = bf16[128,512]{1,0:T(8,128)(2,1)S(1)} collective-permute-done((bf16[128,512]{1,0:T(8,128)(2,1)S(1)}, bf16[128,512]{1,0:T(8,128)(2,1)S(1)}, u32[]{:S(2)}, u32[]{:S(2)}) %collective-permute-start.2) | collective-permute-done | bytes 131104 | tf_op jit(solution)/shard_map/ppermute | solution.py:262
  170.9 0.9 fusion.1
  172.5 0.6 fusion.2
  (21 shorter events, 2.4 us)
Async XLA Ops:
  7.2 60.9 %all-gather.4.cloned.1.call-start = ((), (), s32[]{:S(2)}) async-start(), calls=%async_computation.6 | async-start | bytes 2654208 | tf_op jit(solution)/shard_map/all_gather | solution.py:205
  8.9 7.7 %collective-permute-start = (bf16[144,512]{1,0:T(8,128)(2,1)}, bf16[144,512]{1,0:T(8,128)(2,1)S(1)}, u32[]{:S(2)}, u32[]{:S(2)}) collective-permute-start(bf16[144,512]{1,0:T(8,128)(2,1)} %get-tuple-element.8), channel_id=1, source_target_pairs={{0,256},{32,288},{64,320},{96,352},{128,384},{160,416},{192,448},{... | collective-permute-start | bytes 442376 | tf_op jit(solution)/shard_map/ppermute | solution.py:204
  39.3 25.2 %all-to-all-start = ((bf16[4,4,128,512]{3,2,1,0:T(8,128)(2,1)}), bf16[4,4,128,512]{3,2,1,0:T(8,128)(2,1)S(1)}, u32[]{:S(2)}, u32[]{:S(2)}) async-start(bf16[4,4,128,512]{3,2,1,0:T(8,128)(2,1)} %broadcast_in_dim.2), calls=%async_computation | async-start | bytes 4194304 | tf_op jit(solution)/shard_map/all_to_all | solution.py:207
  44.1 119.1 %reduce-scatter.2.cloned.1.call-start = ((), (), s32[]{:S(2)}) async-start(), calls=%async_computation.5 | async-start | bytes 2359296 | tf_op jit(solution)/shard_map/reduce_scatter | solution.py:236
  64.5 8.0 %copy-start.2 = (bf16[4,4,128,512]{3,2,1,0:T(8,128)(2,1)}, bf16[4,4,128,512]{3,2,1,0:T(8,128)(2,1)S(1)}, u32[]{:S(2)}) copy-start(bf16[4,4,128,512]{3,2,1,0:T(8,128)(2,1)S(1)} %all-to-all-done) | copy-start | bytes 6291460
  68.1 1.7 copy-start
  69.8 0.7 copy-start.7
  70.5 29.0 %copy-start.8 = (s32[3,40]{1,0:T(4,128)S(1)}, s32[3,40]{1,0:T(4,128)}, u32[]{:S(2)}) copy-start(s32[3,40]{1,0:T(4,128)} %pair_lists.1.lists) | copy-start | bytes 1444
  99.4 1.6 copy-start.3
  101.0 7.2 %copy-start.1 = (bf16[16,144,512]{2,1,0:T(8,128)(2,1)S(1)}, bf16[16,144,512]{2,1,0:T(8,128)(2,1)}, u32[]{:S(2)}) copy-start(bf16[16,144,512]{2,1,0:T(8,128)(2,1)} %all-gather.4.cloned.1.call-done.kv) | copy-start | bytes 7077892
  105.5 1.4 copy-start.4
  106.9 1.3 copy-start.6
  108.3 1.6 copy-start.5
  136.4 12.5 %all-to-all-start.3 = ((bf16[4,128,256]{2,1,0:T(8,128)(2,1)}), bf16[4,128,256]{2,1,0:T(8,128)(2,1)S(1)}, u32[]{:S(2)}, u32[]{:S(2)}) async-start(bf16[4,128,256]{2,1,0:T(8,128)(2,1)} %reduce_sum.21), calls=%async_computation.3 | async-start | bytes 524288 | tf_op jit(solution)/shard_map/all_to_all | solution.py:258
  139.8 3.1 %collective-permute-start.1 = (f32[8,128]{1,0:T(8,128)S(1)}, f32[8,128]{1,0:T(8,128)S(1)}, u32[]{:S(2)}, u32[]{:S(2)}) collective-permute-start(f32[8,128]{1,0:T(8,128)S(1)} %get-tuple-element.11), channel_id=1, source_target_pairs={{0,1},{1,0},{2,3},{3,2},{4,5},{5,4},{6,7},{7,6},{8,9},{9,8},{10,11... | collective-permute-start | bytes 12296 | tf_op jit(solution)/shard_map/ppermute | solution.py:250
  164.1 6.9 %collective-permute-start.2 = (bf16[128,512]{1,0:T(8,128)(2,1)S(1)}, bf16[128,512]{1,0:T(8,128)(2,1)S(1)}, u32[]{:S(2)}, u32[]{:S(2)}) collective-permute-start(bf16[128,512]{1,0:T(8,128)(2,1)S(1)} %slice_bitcast_fusion), channel_id=1, source_target_pairs={{0,256},{32,288},{64,320},{96,352},{128,384},{160,416},{192,448},{... | collective-permute-start | bytes 393224 | tf_op jit(solution)/shard_map/ppermute | solution.py:262
Sparse Core Ops, SparseCore 0:
  18.4 49.6 all-gather.3
  108.4 54.7 reduce-scatter.1

commit v3 on v2

--- a/solution.py
+++ b/solution.py
@@ -27,7 +27,7 @@
 
 VMEM = pl.BlockSpec(memory_space=pltpu.VMEM)
 SMEM = pl.BlockSpec(memory_space=pltpu.SMEM)
-PARAMS = pltpu.CompilerParams(vmem_limit_bytes=40 * 1024 * 1024)
+PARAMS = pltpu.CompilerParams(vmem_limit_bytes=28 * 1024 * 1024)
 
 
 def dot(a, b, dims):
@@ -63,32 +63,48 @@
         lists[HEADS, head] = lax.fori_loop(0, GB, step, 0)
 
 
-def pair_of(lists, head, at, qg, kv):
-    both = lists[head, at]
-    row, col = both >> 4, both & 15
+def for_pairs(lists, work):
+    count = lists[HEADS, 0]
+
+    def fours(step, carry):
+        work([(head, 4 * step + u) for u in range(4) for head in range(HEADS)])
+        return carry
+
+    lax.fori_loop(0, count >> 2, fours, 0)
+
+    @pl.when((count & 2) != 0)
+    def _():
+        first = (count >> 2) * 4
+        work([(head, first + u) for u in range(2) for head in range(HEADS)])
+
+
+def blocks_at(ref, slot, head):
     first, second = head * DH, WIDE + head * DH
-    query, grad = qg[row, :, first : first + DH], qg[row, :, second : second + DH]
-    key, value = kv[col, :BLK, first : first + DH], kv[col, :BLK, second : second + DH]
-    scores = dot(key, query, ((1,), (1,))) * log2_scale
-    grad_scores = dot(value, grad, ((1,), (1,)))
-    return row, col, query, grad, scores, grad_scores
-
-
-def stat_kernel(lists, qg, kv, stats, top, total, delta):
+    return ref[slot, :BLK, first : first + DH], ref[slot, :BLK, second : second + DH]
+
+
+def stat_kernel(lists, qg, kv, stats, shifted, grad_scores, tops, top, total, delta):
     top[...] = jnp.full_like(top, neg_big)
     total[...] = jnp.zeros_like(total)
     delta[...] = jnp.zeros_like(delta)
 
-    def step(p, carry):
+    def work(pairs):
         found = []
-        for head in range(HEADS):
-            for u in range(2):
-                row, _, _, _, scores, grad_scores = pair_of(lists, head, 2 * p + u, qg, kv)
-                own_top = jnp.max(scores, axis=0, keepdims=True)
-                shifted = jnp.exp2(scores - own_top)
-                own_total = jnp.sum(shifted, axis=0, keepdims=True)
-                own_delta = jnp.sum(shifted * grad_scores, axis=0, keepdims=True)
-                found.append((head * GB + row, own_top, own_total, own_delta))
+        for head, at in pairs:
+            both = lists[head, at]
+            row, col = both >> 4, both & 15
+            query, grad = blocks_at(qg, row, head)
+            key, value = blocks_at(kv, col, head)
+            scores = dot(key, query, ((1,), (1,))) * log2_scale
+            product = dot(value, grad, ((1,), (1,)))
+            own_top = jnp.max(scores, axis=0, keepdims=True)
+            weights = jnp.exp2(scores - own_top)
+            shifted[head, at] = weights
+            grad_scores[head, at] = product
+            tops[head, at] = own_top
+            own_total = jnp.sum(weights, axis=0, keepdims=True)
+            own_delta = jnp.sum(weights * product, axis=0, keepdims=True)
+            found.append((head * GB + row, own_top, own_total, own_delta))
         for at, own_top, own_total, own_delta in found:
             old_top = top[at]
             new_top = jnp.maximum(old_top, own_top)
@@ -97,9 +113,8 @@
             top[at] = new_top
             total[at] = total[at] * old_weight + own_total * own_weight
             delta[at] = delta[at] * old_weight + own_delta * own_weight
-        return carry
-
-    lax.fori_loop(0, lists[HEADS, 0] // 2, step, 0)
+
+    for_pairs(lists, work)
     for at in range(SLOTS):
         stats[0, at : at + 1, :] = top[at]
         stats[0, SLOTS + at : SLOTS + at + 1, :] = total[at]
@@ -114,7 +129,9 @@
         stats[part] = own
 
 
-def key_kernel(lists, qg, kv, stats, kvout, dscores, latent, shift, delta, kacc, vacc):
+def key_kernel(
+    lists, qg, stats, shifted, grad_scores, own_tops, kvout, dscores, latent, shift, delta, kacc, vacc
+):
     tops = stats[0, :SLOTS]
     for part in range(1, GB):
         tops = jnp.maximum(tops, stats[part, :SLOTS])
@@ -135,23 +152,24 @@
     kacc[...] = jnp.zeros_like(kacc)
     vacc[...] = jnp.zeros_like(vacc)
 
-    def step(p, carry):
+    def work(pairs):
         found = []
-        for head in range(HEADS):
-            for u in range(2):
-                row, col, query, grad, scores, grad_scores = pair_of(lists, head, 2 * p + u, qg, kv)
-                rat, cat = head * GB + row, head * GB + col
-                weights = jnp.exp2(scores - shift[rat])
-                dscore = (weights * (grad_scores - delta[rat])).astype(jnp.bfloat16)
-                weights_low = weights.astype(jnp.bfloat16)
-                dscores[head, 2 * p + u] = dscore
-                found.append((cat, dot(dscore, query, ((1,), (0,))), dot(weights_low, grad, ((1,), (0,)))))
-        for cat, kterm, vterm in found:
-            kacc[cat] += kterm
-            vacc[cat] += vterm
-        return carry
-
-    lax.fori_loop(0, lists[HEADS, 0] // 2, step, 0)
+        for head, at in pairs:
+            both = lists[head, at]
+            row, col = both >> 4, both & 15
+            query, grad = blocks_at(qg, row, head)
+            scale = jnp.exp2(own_tops[head, at] - shift[head * GB + row])
+            weights = shifted[head, at] * scale
+            dscore = (weights * (grad_scores[head, at] - delta[head * GB + row])).astype(jnp.bfloat16)
+            dscores[head, at] = dscore
+            kterm = dot(dscore, query, ((1,), (0,)))
+            vterm = dot(weights.astype(jnp.bfloat16), grad, ((1,), (0,)))
+            found.append((head * GB + col, kterm, vterm))
+        for at, kterm, vterm in found:
+            kacc[at] += kterm
+            vacc[at] += vterm
+
+    for_pairs(lists, work)
     for slot in range(GB):
         for head in range(HEADS):
             first, second = head * DH, WIDE + head * DH
@@ -162,18 +180,16 @@
 def query_kernel(lists, kv, dscores, qout, qacc):
     qacc[...] = jnp.zeros_like(qacc)
 
-    def step(p, carry):
+    def work(pairs):
         found = []
-        for head in range(HEADS):
-            for u in range(2):
-                both = lists[head, 2 * p + u]
-                key = kv[both & 15, :BLK, head * DH : head * DH + DH]
-                found.append((head * GB + (both >> 4), dot(dscores[head, 2 * p + u], key, ((0,), (0,)))))
-        for rat, qterm in found:
-            qacc[rat] += qterm
-        return carry
-
-    lax.fori_loop(0, lists[HEADS, 0] // 2, step, 0)
+        for head, at in pairs:
+            both = lists[head, at]
+            key, _ = blocks_at(kv, both & 15, head)
+            found.append((head * GB + (both >> 4), dot(dscores[head, at], key, ((0,), (0,)))))
+        for at, qterm in found:
+            qacc[at] += qterm
+
+    for_pairs(lists, work)
     for slot in range(GB):
         for head in range(HEADS):
             qout[slot, :, head * DH : head * DH + DH] = qacc[head * GB + slot].astype(jnp.bfloat16)
@@ -210,11 +226,17 @@
 
     row_scratch = pltpu.VMEM((SLOTS, 1, DH), jnp.float32)
     block_scratch = pltpu.VMEM((SLOTS, BLK, DH), jnp.float32)
-    stats = pl.pallas_call(
+    by_pair = shape(HEADS, 2 * GB, BLK, BLK, dtype=jnp.float32)
+    stats, shifted, grad_scores, tops = pl.pallas_call(
         stat_kernel,
-        out_shape=shape(GB, STAT, DH, dtype=jnp.float32),
+        out_shape=(
+            shape(GB, STAT, DH, dtype=jnp.float32),
+            by_pair,
+            by_pair,
+            shape(HEADS, 2 * GB, 1, DH, dtype=jnp.float32),
+        ),
         in_specs=[SMEM, VMEM, VMEM],
-        out_specs=VMEM,
+        out_specs=(VMEM,) * 4,
         scratch_shapes=[row_scratch, row_scratch, row_scratch],
         compiler_params=PARAMS,
         name="row_stats",
@@ -227,12 +249,12 @@
             shape(HEADS, 2 * GB, BLK, BLK),
             shape(8, DH, dtype=jnp.float32),
         ),
-        in_specs=[SMEM, VMEM, VMEM, VMEM],
+        in_specs=[SMEM] + [VMEM] * 5,
         out_specs=(VMEM,) * 3,
         scratch_shapes=[row_scratch, row_scratch, block_scratch, block_scratch],
         compiler_params=PARAMS,
         name="key_value_grads",
-    )(lists, qg, kv, stats)
+    )(lists, qg, stats, shifted, grad_scores, tops)
     kvpart = lax.psum_scatter(
         kvpart.reshape(8, 2 * BLK, 2 * WIDE), "qb", scatter_dimension=0, axis_index_groups=Z_GROUPS
     )

time: 181 us -> 167 us (0.923)
  blocking collectives: 70.3 us -> 61.4 us
  Pallas kernels: 13.2 us -> 9.79 us
  waiting for transfers between devices: 45.7 us -> 43.2 us
    all_to_all x1, blocking collectives: 23.9 us -> 14.6 us  [body(): lax.all_to_all(qpart.reshape(4, 4, BLK, WIDE), 'kb', 0, 0, axis_index_gro...]
    pallas_call x1, Pallas kernels: 4.52 us -> 1.78 us  [body(): pl.pallas_call(key_kernel, out_shape=(shape(GB, BLK, 2 * WIDE), shape(HEA...]
    reduce_scatter x1, waiting for transfers between devices: 14.3 us -> 12.2 us  [body(): lax.psum_scatter(kvpart.reshape(8, 2 * BLK, 2 * WIDE), 'qb', scatter_dime...]
    unnamed x18 -> x14, local copies, waits for them, and re-layouts: 8.21 us -> 8.23 us
where the time goes in v3:
time: 167 us; the launch traced here: 166 us
  blocking collectives  61.4 us (37%)
  waiting for transfers between devices  43.2 us (26%)
  starting transfers between devices  17.2 us (10%)
  between operations  16.8 us (10%)
  local copies, waits for them, and re-layouts  12.3 us (7%)
  Pallas kernels  9.79 us (6%)
  other arithmetic  4.83 us (3%)
    all_to_all x1, blocking collectives, body(): stats = lax.all_to_all(stats, 'kb', 0, 0)  27.2 us
    all_gather x1, blocking collectives, body(): qg = lax.all_gather(qg, 'kb', axis_index_groups=Y_GROUPS)  19.5 us
    all_to_all x1, waiting for transfers between devices, body(): lax.all_to_all(jnp.broadcast_to(qg[None], (4, 4, BLK, 2 * WIDE)), 'kb', 0...  17.2 us
    all_to_all x1, blocking collectives, body(): lax.all_to_all(qpart.reshape(4, 4, BLK, WIDE), 'kb', 0, 0, axis_index_gro...  14.6 us
    reduce_scatter x1, waiting for transfers between devices, body(): lax.psum_scatter(kvpart.reshape(8, 2 * BLK, 2 * WIDE), 'qb', scatter_dime...  12.2 us
    unnamed x14, local copies, waits for them, and re-layouts  8.23 us
    all_to_all x1, starting transfers between devices, body(): lax.all_to_all(jnp.broadcast_to(qg[None], (4, 4, BLK, 2 * WIDE)), 'kb', 0...  4.77 us
    ppermute x1, waiting for transfers between devices, body(): far = lax.ppermute(kv, 'qb', Y_PAIRS)  4.2 us
  transfers between devices with their start and end apart: 7, of which 7 were waited for; matrix products, arithmetic and copies ran while one was open for 2% of the time, Pallas kernels for 3%

profile of v3, /device:TPU:6, one launch (start us, length us, event | category | flops | bytes accessed | tf_op | source)
XLA Modules:
  0.0 165.6 jit_solution(9679360123589888304)
XLA Ops:
  7.2 1.7 %pack.1 = (bf16[128,512]{1,0:T(8,128)(2,1)}, bf16[144,512]{1,0:T(8,128)(2,1)}) custom-call(bf16[1,128,256]{2,1,0:T(8,128)(2,1)} %queries.1, bf16[1,128,256]{2,1,0:T(8,128)(2,1)} %keys.1, bf16[1,128,256]{2,1,0:T(8,128)(2,1)} %values.1, bf16[1,128,256]{2,1,0:T(8,128)(2,1)} %out_grad.1, f32[1,128]{1,0:T(1,128)} %token_error.1), custom_call_target="tpu_custom_call" | custom-call | tf_op jit(solution)/shard_map/pack/pallas_call | solution.py:205
  8.9 3.5 %collective-permute-start = (bf16[144,512]{1,0:T(8,128)(2,1)}, bf16[144,512]{1,0:T(8,128)(2,1)S(1)}, u32[]{:S(2)}, u32[]{:S(2)}) collective-permute-start(bf16[144,512]{1,0:T(8,128)(2,1)} %get-tuple-element.12), channel_id=1, source_target_pairs={{0,256},{32,288},{64,320},{96,352},{128,384},{160,416},{192,448},{... | collective-permute-start | bytes 442376 | tf_op jit(solution)/shard_map/ppermute | solution.py:220
  12.4 4.2 %collective-permute-done = bf16[144,512]{1,0:T(8,128)(2,1)S(1)} collective-permute-done((bf16[144,512]{1,0:T(8,128)(2,1)}, bf16[144,512]{1,0:T(8,128)(2,1)S(1)}, u32[]{:S(2)}, u32[]{:S(2)}) %collective-permute-start) | collective-permute-done | bytes 147488 | tf_op jit(solution)/shard_map/ppermute | solution.py:220
  16.6 1.7 pad_maximum_fusion
  18.3 19.5 %all-gather.1 = bf16[512,512]{1,0:T(8,128)(2,1)S(1)} all-gather(bf16[128,512]{1,0:T(8,128)(2,1)} %get-tuple-element.13), channel_id=3, replica_groups={{0,8,16,24},{2,10,18,26},{4,12,20,28},{6,14,22,30},{1,9,17,25},{3,11,19..., dimensions={0}, use_global_device_ids=true | all-gather | bytes 655360 | tf_op jit(solution)/shard_map/all_gather | solution.py:222
  37.8 1.5 broadcast_in_dim.2
  39.3 4.8 %all-to-all-start = ((bf16[4,4,128,512]{3,2,1,0:T(8,128)(2,1)}), bf16[4,4,128,512]{3,2,1,0:T(8,128)(2,1)S(1)}, u32[]{:S(2)}, u32[]{:S(2)}) async-start(bf16[4,4,128,512]{3,2,1,0:T(8,128)(2,1)} %broadcast_in_dim.2), calls=%async_computation | async-start | bytes 4194304 | tf_op jit(solution)/shard_map/all_to_all | solution.py:223
  44.1 3.2 %pair_lists.1.lists = s32[3,40]{1,0:T(4,128)} custom-call(s32[2,16,16]{2,1,0:T(8,128)} %mask.1, s32[1]{0:T(128)} %bitcast.side), custom_call_target="tpu_custom_call" | custom-call | tf_op jit(solution)/shard_map/pair_lists/pallas_call | solution.py:213
  47.3 17.2 %all-to-all-done = bf16[4,4,128,512]{3,2,1,0:T(8,128)(2,1)S(1)} async-done(((bf16[4,4,128,512]{3,2,1,0:T(8,128)(2,1)}), bf16[4,4,128,512]{3,2,1,0:T(8,128)(2,1)S(1)}, u32[]{:S(2)}, u32[]{:S(2)}) %all-to-all-start) | async-done | bytes 2097184 | tf_op jit(solution)/shard_map/all_to_all | solution.py:223
  64.5 3.6 %all-gather.4.cloned.1.call-done.kv = bf16[16,144,512]{2,1,0:T(8,128)(2,1)} async-done(((bf16[2,144,512]{2,1,0:T(8,128)(2,1)}), bf16[16,144,512]{2,1,0:T(8,128)(2,1)}) %all-gather.4.cloned.1.call-update) | async-done | bytes 2359312 | tf_op jit(solution)/shard_map/all_gather | solution.py:221
  68.1 1.7 %copy-done = bf16[16,144,512]{2,1,0:T(8,128)(2,1)S(1)} copy-done((bf16[16,144,512]{2,1,0:T(8,128)(2,1)S(1)}, bf16[16,144,512]{2,1,0:T(8,128)(2,1)}, u32[]{:S(2)}) %copy-start) | copy-done | bytes 2359320
  69.8 0.7 copy-done.5
  70.5 1.7 %row_stats.1 = (f32[16,104,128]{2,1,0:T(8,128)S(1)}, f32[2,32,128,128]{3,2,1,0:T(8,128)S(1)}, f32[2,32,128,128]{3,2,1,0:T(8,128)S(1)}, f32[2,32,1,128]{3,2,1,0:T(1,128)S(1)}) custom-call(s32[3,40]{1,0:T(4,128)S(1)} %copy-done.5, bf16[16,128,512]{2,1,0:T(8,128)(2,1)S(1)} %bitcast.20, bf16[16,144,512]{2,1,0:T(8,128)(2,1)S(1)} %copy-done), custom_call_target="tpu_custom_call" | custom-call | tf_op jit(solution)/shard_map/row_stats/pallas_call | solution.py:230
  72.2 27.2 %all_to_all.20.stats = f32[16,104,128]{2,1,0:T(8,128)S(1)} all-to-all(f32[16,104,128]{2,1,0:T(8,128)S(1)} %get-tuple-element.14), channel_id=1, replica_groups=mesh['qb'=16,'kb'=16,'pair'=2] {'kb'}, dimensions={0} | all-to-all | bytes 1703936 | tf_op jit(solution)/shard_map/all_to_all | solution.py:244
  99.4 1.8 %key_value_grads.1 = (bf16[16,128,512]{2,1,0:T(8,128)(2,1)S(1)}, bf16[2,32,128,128]{3,2,1,0:T(8,128)(2,1)S(1)}, f32[8,128]{1,0:T(8,128)S(1)}) custom-call(s32[3,40]{1,0:T(4,128)S(1)} %copy-done.6, bf16[16,128,512]{2,1,0:T(8,128)(2,1)S(1)} %bitcast.21, f32[16,104,128]{2,1,0:T(8,128)S(1)} %all_to_all.20.stats, ...), custom_call_target="tpu_custom_call" | custom-call | tf_op jit(solution)/shard_map/key_value_grads/pallas_call | solution.py:245
  101.2 1.4 copy-done.2
  102.6 1.3 copy-done.4
  103.9 1.6 copy-done.3
  105.5 1.7 %copy-done.1 = bf16[16,144,512]{2,1,0:T(8,128)(2,1)S(1)} copy-done((bf16[16,144,512]{2,1,0:T(8,128)(2,1)S(1)}, bf16[16,144,512]{2,1,0:T(8,128)(2,1)}, u32[]{:S(2)}) %copy-start.1) | copy-done | bytes 2359320
  107.1 1.4 query_grads.1
  108.5 14.6 %all_to_all.21 = bf16[4,4,128,256]{3,2,1,0:T(8,128)(2,1)S(1)} all-to-all(bf16[4,4,128,256]{3,2,1,0:T(8,128)(2,1)S(1)} %bitcast.22), channel_id=1, replica_groups={{0,2,4,6},{8,10,12,14},{16,18,20,22},{24,26,28,30},{1,3,5,7},{9,11,13,1..., dimensions={0} | all-to-all | bytes 2097152 | tf_op jit(solution)/shard_map/all_to_all | solution.py:278
  123.2 0.9 reduce_sum.21
  124.1 3.4 %all-to-all-start.3 = ((bf16[4,128,256]{2,1,0:T(8,128)(2,1)}), bf16[4,128,256]{2,1,0:T(8,128)(2,1)S(1)}, u32[]{:S(2)}, u32[]{:S(2)}) async-start(bf16[4,128,256]{2,1,0:T(8,128)(2,1)} %reduce_sum.21), calls=%async_computation.3 | async-start | bytes 524288 | tf_op jit(solution)/shard_map/all_to_all | solution.py:280
  127.5 1.9 %collective-permute-start.1 = (f32[8,128]{1,0:T(8,128)S(1)}, f32[8,128]{1,0:T(8,128)S(1)}, u32[]{:S(2)}, u32[]{:S(2)}) collective-permute-start(f32[8,128]{1,0:T(8,128)S(1)} %get-tuple-element.19), channel_id=1, source_target_pairs={{0,1},{1,0},{2,3},{3,2},{4,5},{5,4},{6,7},{7,6},{8,9},{9,8},{10,11... | collective-permute-start | bytes 12296 | tf_op jit(solution)/shard_map/ppermute | solution.py:272
  133.8 2.8 %all-to-all-done.3 = bf16[4,128,256]{2,1,0:T(8,128)(2,1)S(1)} async-done(((bf16[4,128,256]{2,1,0:T(8,128)(2,1)}), bf16[4,128,256]{2,1,0:T(8,128)(2,1)S(1)}, u32[]{:S(2)}, u32[]{:S(2)}) %all-to-all-start.3) | async-done | bytes 262176 | tf_op jit(solution)/shard_map/all_to_all | solution.py:280
  136.6 12.2 %reduce-scatter.2.cloned.1.call-done = bf16[1,256,512]{2,1,0:T(8,128)(2,1)} async-done(((bf16[8,256,512]{2,1,0:T(8,128)(2,1)}), bf16[1,256,512]{2,1,0:T(8,128)(2,1)}) %reduce-scatter.2.cloned.1.call-update) | async-done | bytes 262160 | tf_op jit(solution)/shard_map/reduce_scatter | solution.py:258
  148.8 0.9 slice_bitcast_fusion
  149.7 3.6 %collective-permute-start.2 = (bf16[128,512]{1,0:T(8,128)(2,1)S(1)}, bf16[128,512]{1,0:T(8,128)(2,1)S(1)}, u32[]{:S(2)}, u32[]{:S(2)}) collective-permute-start(bf16[128,512]{1,0:T(8,128)(2,1)S(1)} %slice_bitcast_fusion), channel_id=1, source_target_pairs={{0,256},{32,288},{64,320},{96,352},{128,384},{160,416},{192,448},{... | collective-permute-start | bytes 393224 | tf_op jit(solution)/shard_map/ppermute | solution.py:284
  153.3 0.6 fusion.3
  154.0 2.6 %collective-permute-done.2 = bf16[128,512]{1,0:T(8,128)(2,1)S(1)} collective-permute-done((bf16[128,512]{1,0:T(8,128)(2,1)S(1)}, bf16[128,512]{1,0:T(8,128)(2,1)S(1)}, u32[]{:S(2)}, u32[]{:S(2)}) %collective-permute-start.2) | collective-permute-done | bytes 131104 | tf_op jit(solution)/shard_map/ppermute | solution.py:284
  156.6 0.9 fusion.1
  158.1 0.6 fusion.2
  (17 shorter events, 2.4 us)
Async XLA Ops:
  7.2 61.0 %all-gather.4.cloned.1.call-start = ((), (), s32[]{:S(2)}) async-start(), calls=%async_computation.6 | async-start | bytes 2654208 | tf_op jit(solution)/shard_map/all_gather | solution.py:221
  8.9 7.7 %collective-permute-start = (bf16[144,512]{1,0:T(8,128)(2,1)}, bf16[144,512]{1,0:T(8,128)(2,1)S(1)}, u32[]{:S(2)}, u32[]{:S(2)}) collective-permute-start(bf16[144,512]{1,0:T(8,128)(2,1)} %get-tuple-element.12), channel_id=1, source_target_pairs={{0,256},{32,288},{64,320},{96,352},{128,384},{160,416},{192,448},{... | collective-permute-start | bytes 442376 | tf_op jit(solution)/shard_map/ppermute | solution.py:220
  39.3 25.2 %all-to-all-start = ((bf16[4,4,128,512]{3,2,1,0:T(8,128)(2,1)}), bf16[4,4,128,512]{3,2,1,0:T(8,128)(2,1)S(1)}, u32[]{:S(2)}, u32[]{:S(2)}) async-start(bf16[4,4,128,512]{3,2,1,0:T(8,128)(2,1)} %broadcast_in_dim.2), calls=%async_computation | async-start | bytes 4194304 | tf_op jit(solution)/shard_map/all_to_all | solution.py:223
  44.1 104.7 %reduce-scatter.2.cloned.1.call-start = ((), (), s32[]{:S(2)}) async-start(), calls=%async_computation.5 | async-start | bytes 2359296 | tf_op jit(solution)/shard_map/reduce_scatter | solution.py:258
  68.1 1.7 %copy-start = (bf16[16,144,512]{2,1,0:T(8,128)(2,1)S(1)}, bf16[16,144,512]{2,1,0:T(8,128)(2,1)}, u32[]{:S(2)}) copy-start(bf16[16,144,512]{2,1,0:T(8,128)(2,1)} %all-gather.4.cloned.1.call-done.kv) | copy-start | bytes 7077892
  69.8 0.7 copy-start.5
  70.5 29.0 %copy-start.6 = (s32[3,40]{1,0:T(4,128)S(1)}, s32[3,40]{1,0:T(4,128)}, u32[]{:S(2)}) copy-start(s32[3,40]{1,0:T(4,128)} %pair_lists.1.lists) | copy-start | bytes 1444
  101.2 1.4 copy-start.2
  102.6 1.3 copy-start.4
  103.9 1.6 copy-start.3
  105.5 1.7 %copy-start.1 = (bf16[16,144,512]{2,1,0:T(8,128)(2,1)S(1)}, bf16[16,144,512]{2,1,0:T(8,128)(2,1)}, u32[]{:S(2)}) copy-start(bf16[16,144,512]{2,1,0:T(8,128)(2,1)} %all-gather.4.cloned.1.call-done.kv) | copy-start | bytes 7077892
  124.1 12.5 %all-to-all-start.3 = ((bf16[4,128,256]{2,1,0:T(8,128)(2,1)}), bf16[4,128,256]{2,1,0:T(8,128)(2,1)S(1)}, u32[]{:S(2)}, u32[]{:S(2)}) async-start(bf16[4,128,256]{2,1,0:T(8,128)(2,1)} %reduce_sum.21), calls=%async_computation.3 | async-start | bytes 524288 | tf_op jit(solution)/shard_map/all_to_all | solution.py:280
  127.5 3.1 %collective-permute-start.1 = (f32[8,128]{1,0:T(8,128)S(1)}, f32[8,128]{1,0:T(8,128)S(1)}, u32[]{:S(2)}, u32[]{:S(2)}) collective-permute-start(f32[8,128]{1,0:T(8,128)S(1)} %get-tuple-element.19), channel_id=1, source_target_pairs={{0,1},{1,0},{2,3},{3,2},{4,5},{5,4},{6,7},{7,6},{8,9},{9,8},{10,11... | collective-permute-start | bytes 12296 | tf_op jit(solution)/shard_map/ppermute | solution.py:272
  149.7 6.9 %collective-permute-start.2 = (bf16[128,512]{1,0:T(8,128)(2,1)S(1)}, bf16[128,512]{1,0:T(8,128)(2,1)S(1)}, u32[]{:S(2)}, u32[]{:S(2)}) collective-permute-start(bf16[128,512]{1,0:T(8,128)(2,1)S(1)} %slice_bitcast_fusion), channel_id=1, source_target_pairs={{0,256},{32,288},{64,320},{96,352},{128,384},{160,416},{192,448},{... | collective-permute-start | bytes 393224 | tf_op jit(solution)/shard_map/ppermute | solution.py:284
Sparse Core Ops, SparseCore 0:
  18.4 49.6 all-gather.3
  104.0 44.6 reduce-scatter.1

commit v4 on v3

--- a/solution.py
+++ b/solution.py
@@ -9,6 +9,7 @@
 HEADS = 2
 BLK = 128
 GB = 16
+TOKENS = 32768
 WIDE = HEADS * DH
 ROWS = BLK + 16
 SLOTS = HEADS * GB
@@ -23,11 +24,15 @@
 Y_GROUPS = [[x + 4 * y for y in range(4)] for x in range(4)]
 X_GROUPS = [[x + 4 * y for x in range(4)] for y in range(4)]
 Z_GROUPS = [[z + 8 * y for z in range(8)] for y in range(2)]
-Y_PAIRS = [(s, s ^ 8) for s in range(16)]
+Y_PAIRS = [[z, z + 8] for z in range(8)]
+Y_SWAP = [(s, s ^ 8) for s in range(16)]
 
 VMEM = pl.BlockSpec(memory_space=pltpu.VMEM)
 SMEM = pl.BlockSpec(memory_space=pltpu.SMEM)
-PARAMS = pltpu.CompilerParams(vmem_limit_bytes=28 * 1024 * 1024)
+
+
+def params(megabytes):
+    return pltpu.CompilerParams(vmem_limit_bytes=megabytes * 1024 * 1024)
 
 
 def dot(a, b, dims):
@@ -50,13 +55,13 @@
 
 
 def list_kernel(mask, side, lists):
-    flip = side[0]
+    lists[HEADS, 2] = side[0]
     for head in range(HEADS):
 
         def step(row, count):
             first = ((row & 3) * 4 + (row >> 2)) * GB
             for col in range(GB):
-                lists[head, count] = first + (2 * (col % 8) + ((col // 8) ^ flip))
+                lists[head, count] = first + 2 * (col % 8) + col // 8
                 count = jnp.minimum(count + mask[head, row, col], LIST - 1)
             return count
 
@@ -171,10 +176,11 @@
 
     for_pairs(lists, work)
     for slot in range(GB):
+        target = slot // 2 * 2 + ((slot & 1) ^ lists[HEADS, 2])
         for head in range(HEADS):
             first, second = head * DH, WIDE + head * DH
-            kvout[slot, :, first : first + DH] = kacc[head * GB + slot].astype(jnp.bfloat16)
-            kvout[slot, :, second : second + DH] = vacc[head * GB + slot].astype(jnp.bfloat16)
+            kvout[target, :, first : first + DH] = kacc[head * GB + slot].astype(jnp.bfloat16)
+            kvout[target, :, second : second + DH] = vacc[head * GB + slot].astype(jnp.bfloat16)
 
 
 def query_kernel(lists, kv, dscores, qout, qacc):
@@ -200,8 +206,6 @@
 
 
 def body(queries, keys, values, out_grad, token_error, block_mask):
-    pair_side = lax.axis_index("pair")
-    token_count = token_error.shape[1] * lax.axis_size("qb") * lax.axis_size("kb")
     qg, kv = pl.pallas_call(
         pack_kernel,
         out_shape=(shape(BLK, 2 * WIDE), shape(ROWS, 2 * WIDE)),
@@ -209,16 +213,15 @@
         out_specs=(VMEM, VMEM),
         name="pack",
     )(queries, keys, values, out_grad, token_error)
-    side = (lax.axis_index("qb") // 8).astype(jnp.int32).reshape(1)
     lists = pl.pallas_call(
         list_kernel,
         out_shape=shape(HEADS + 1, LIST, dtype=jnp.int32),
         in_specs=[SMEM, SMEM],
         out_specs=SMEM,
         name="pair_lists",
-    )(block_mask, side)
-    far = lax.ppermute(kv, "qb", Y_PAIRS)
-    kv = lax.all_gather(jnp.stack([kv, far]), "qb", axis_index_groups=Z_GROUPS).reshape(GB, ROWS, 2 * WIDE)
+    )(block_mask, (lax.axis_index("qb") // 8).astype(jnp.int32).reshape(1))
+    kv = lax.all_gather(kv, "qb", axis_index_groups=Y_PAIRS)
+    kv = lax.all_gather(kv, "qb", axis_index_groups=Z_GROUPS).reshape(GB, ROWS, 2 * WIDE)
     qg = lax.all_gather(qg, "kb", axis_index_groups=Y_GROUPS)
     qg = lax.all_to_all(
         jnp.broadcast_to(qg[None], (4, 4, BLK, 2 * WIDE)), "kb", 0, 0, axis_index_groups=X_GROUPS
@@ -238,7 +241,7 @@
         in_specs=[SMEM, VMEM, VMEM],
         out_specs=(VMEM,) * 4,
         scratch_shapes=[row_scratch, row_scratch, row_scratch],
-        compiler_params=PARAMS,
+        compiler_params=params(28),
         name="row_stats",
     )(lists, qg, kv)
     stats = lax.all_to_all(stats, "kb", 0, 0)
@@ -250,9 +253,9 @@
             shape(8, DH, dtype=jnp.float32),
         ),
         in_specs=[SMEM] + [VMEM] * 5,
-        out_specs=(VMEM,) * 3,
+        out_specs=(VMEM, VMEM, VMEM),
         scratch_shapes=[row_scratch, row_scratch, block_scratch, block_scratch],
-        compiler_params=PARAMS,
+        compiler_params=params(28),
         name="key_value_grads",
     )(lists, qg, stats, shifted, grad_scores, tops)
     kvpart = lax.psum_scatter(
@@ -264,14 +267,15 @@
         in_specs=[SMEM, VMEM, VMEM],
         out_specs=VMEM,
         scratch_shapes=[block_scratch],
-        compiler_params=PARAMS,
+        compiler_params=params(28),
         name="query_grads",
     )(lists, kv, dscores)
-
-    own_latent = latent[0, 0]
-    partner = lax.ppermute(latent, "pair", [(0, 1), (1, 0)])[0, 0]
-    winner_mean = jnp.where(pair_side == 0, own_latent, partner) / token_count
-    loser_mean = jnp.where(pair_side == 0, partner, own_latent) / token_count
+    partner = lax.ppermute(latent, "pair", [(0, 1), (1, 0)])
+    partner, qpart = lax.optimization_barrier((partner, qpart))
+    own, other = latent[0, 0], partner[0, 0]
+    pair_side = lax.axis_index("pair")
+    winner_mean = jnp.where(pair_side == 0, own, other) / TOKENS
+    loser_mean = jnp.where(pair_side == 0, other, own) / TOKENS
     keep_share = jax.nn.sigmoid(-beta_pref * (loser_mean - winner_mean))
     factor = jnp.where(pair_side == 0, 1.0 + beta_pref * keep_share, -beta_pref * keep_share)
 
@@ -281,10 +285,13 @@
     qsum = jnp.sum(qpart.astype(jnp.float32), axis=0, keepdims=True)
     query_grad = (qsum * (factor * score_scale)).astype(jnp.bfloat16)
 
-    far = lax.ppermute(kvpart[BLK:], "qb", Y_PAIRS)
-    kvsum = (kvpart[:BLK].astype(jnp.float32) + far.astype(jnp.float32))[None] * factor
-    key_grad = (kvsum[..., :WIDE] * score_scale).astype(jnp.bfloat16)
-    value_grad = kvsum[..., WIDE:].astype(jnp.bfloat16)
+    kvpart = kvpart.reshape(2 * BLK, 2 * WIDE)
+    far = lax.ppermute(kvpart[BLK:], "qb", Y_SWAP)
+    near = kvpart[:BLK]
+    ksum = near[None, :, :WIDE].astype(jnp.float32) + far[None, :, :WIDE].astype(jnp.float32)
+    vsum = near[None, :, WIDE:].astype(jnp.float32) + far[None, :, WIDE:].astype(jnp.float32)
+    key_grad = (ksum * (factor * score_scale)).astype(jnp.bfloat16)
+    value_grad = (vsum * factor).astype(jnp.bfloat16)
     return (query_grad, key_grad, value_grad)
 
 

time: 167 us -> 163 us (0.976)
  blocking collectives: 61.4 us -> 73.8 us
  waiting for transfers between devices: 43.2 us -> 36 us
  starting transfers between devices: 17.2 us -> 13.8 us
  other arithmetic: 4.83 us -> 2.28 us
  local copies, waits for them, and re-layouts: 12.3 us -> 10.2 us
    all_gather x0 -> x1, blocking collectives: none -> 7.96 us  [body(): kv = lax.all_gather(kv, 'qb', axis_index_groups=Y_PAIRS)]
    reduce_scatter x1, waiting for transfers between devices: 12.2 us -> 6.71 us  [body(): lax.psum_scatter(kvpart.reshape(8, 2 * BLK, 2 * WIDE), 'qb', scatter_dime...]
    all_to_all x1, blocking collectives: 14.6 us -> 19.7 us  [body(): lax.all_to_all(qpart.reshape(4, 4, BLK, WIDE), 'kb', 0, 0, axis_index_gro...]
    ppermute x3 -> x2, waiting for transfers between devices: 7.41 us -> 2.72 us  [the longest x1 2.71 us: body(): far = lax.ppermute(kvpart[BLK:], 'qb', Y_SWAP)]
    ppermute x3 -> x2, starting transfers between devices: 9 us -> 5.55 us  [the longest x1 3.5 us: body(): far = lax.ppermute(kvpart[BLK:], 'qb', Y_SWAP)]
    all_to_all x1, waiting for transfers between devices: 2.79 us -> 5.86 us  [body(): qpart = lax.all_to_all(qpart, 'kb', 0, 0, axis_index_groups=Y_GROUPS)]
  transfers between devices with their start and end apart: 7 -> 6, of which waited for: 7 -> 5; matrix products, arithmetic and copies ran while one was open for 2% -> 3% of each run, Pallas kernels for 3% -> 3%
where the time goes in v4:
time: 163 us
  blocking collectives  73.8 us (45%)
  waiting for transfers between devices  36 us (22%)
  between operations  16.8 us (10%)
  starting transfers between devices  13.8 us (8%)
  local copies, waits for them, and re-layouts  10.2 us (6%)
  Pallas kernels  9.67 us (6%)
  other arithmetic  2.28 us (1%)
    all_to_all x1, blocking collectives, body(): stats = lax.all_to_all(stats, 'kb', 0, 0)  27.2 us
    all_to_all x1, blocking collectives, body(): lax.all_to_all(qpart.reshape(4, 4, BLK, WIDE), 'kb', 0, 0, axis_index_gro...  19.7 us
    all_gather x1, blocking collectives, body(): qg = lax.all_gather(qg, 'kb', axis_index_groups=Y_GROUPS)  18.9 us
    all_to_all x1, waiting for transfers between devices, body(): lax.all_to_all(jnp.broadcast_to(qg[None], (4, 4, BLK, 2 * WIDE)), 'kb', 0...  16.1 us
    all_gather x1, blocking collectives, body(): kv = lax.all_gather(kv, 'qb', axis_index_groups=Y_PAIRS)  7.96 us
    reduce_scatter x1, waiting for transfers between devices, body(): lax.psum_scatter(kvpart.reshape(8, 2 * BLK, 2 * WIDE), 'qb', scatter_dime...  6.71 us
    unnamed x14, local copies, waits for them, and re-layouts  6.69 us
    all_to_all x1, waiting for transfers between devices, body(): qpart = lax.all_to_all(qpart, 'kb', 0, 0, axis_index_groups=Y_GROUPS)  5.86 us
  transfers between devices with their start and end apart: 6, of which 5 were waited for; matrix products, arithmetic and copies ran while one was open for 3% of the time, Pallas kernels for 3%

profile of v4, /device:TPU:6, one launch (start us, length us, event | category | flops | bytes accessed | tf_op | source)
XLA Modules:
  0.0 162.6 jit_solution(13920684000793657046)
XLA Ops:
  7.2 0.0 all-gather.5.cloned.1.call-start
  7.2 1.7 %pack.1 = (bf16[128,512]{1,0:T(8,128)(2,1)}, bf16[144,512]{1,0:T(8,128)(2,1)}) custom-call(bf16[1,128,256]{2,1,0:T(8,128)(2,1)} %queries.1, bf16[1,128,256]{2,1,0:T(8,128)(2,1)} %keys.1, bf16[1,128,256]{2,1,0:T(8,128)(2,1)} %values.1, bf16[1,128,256]{2,1,0:T(8,128)(2,1)} %out_grad.1, f32[1,128]{1,0:T(1,128)} %token_error.1), custom_call_target="tpu_custom_call" | custom-call | tf_op jit(solution)/shard_map/pack/pallas_call | solution.py:209
  8.9 8.0 %all-gather.1 = bf16[288,512]{1,0:T(8,128)(2,1)} all-gather(bf16[144,512]{1,0:T(8,128)(2,1)} %get-tuple-element.15), channel_id=3, replica_groups={{0,256},{32,288},{64,320},{96,352},{128,384},{160,416},{192,448},{224,4..., dimensions={0}, use_global_device_ids=true | all-gather | bytes 442368 | tf_op jit(solution)/shard_map/all_gather | solution.py:223
  16.9 0.0 all-gather.5.cloned.1.call-update
  16.9 18.9 %all-gather = bf16[512,512]{1,0:T(8,128)(2,1)S(1)} all-gather(bf16[128,512]{1,0:T(8,128)(2,1)} %get-tuple-element.14), channel_id=2, replica_groups={{0,8,16,24},{2,10,18,26},{4,12,20,28},{6,14,22,30},{1,9,17,25},{3,11,19..., dimensions={0}, use_global_device_ids=true | all-gather | bytes 655360 | tf_op jit(solution)/shard_map/all_gather | solution.py:225
  35.8 1.5 broadcast_in_dim.2
  37.3 4.8 %all-to-all-start = ((bf16[4,4,128,512]{3,2,1,0:T(8,128)(2,1)}), bf16[4,4,128,512]{3,2,1,0:T(8,128)(2,1)S(1)}, u32[]{:S(2)}, u32[]{:S(2)}) async-start(bf16[4,4,128,512]{3,2,1,0:T(8,128)(2,1)} %broadcast_in_dim.2), calls=%async_computation | async-start | bytes 4194304 | tf_op jit(solution)/shard_map/all_to_all | solution.py:226
  42.0 3.1 %pair_lists.1.lists = s32[3,40]{1,0:T(4,128)} custom-call(s32[2,16,16]{2,1,0:T(8,128)} %mask.1, s32[1]{0:T(128)} %bitcast.side), custom_call_target="tpu_custom_call" | custom-call | tf_op jit(solution)/shard_map/pair_lists/pallas_call | solution.py:216
  45.2 16.1 %all-to-all-done = bf16[4,4,128,512]{3,2,1,0:T(8,128)(2,1)S(1)} async-done(((bf16[4,4,128,512]{3,2,1,0:T(8,128)(2,1)}), bf16[4,4,128,512]{3,2,1,0:T(8,128)(2,1)S(1)}, u32[]{:S(2)}, u32[]{:S(2)}) %all-to-all-start) | async-done | bytes 2097184 | tf_op jit(solution)/shard_map/all_to_all | solution.py:226
  61.3 4.6 %all-gather.5.cloned.1.call-done.kv = bf16[16,144,512]{2,1,0:T(8,128)(2,1)} async-done(((bf16[2,144,512]{2,1,0:T(8,128)(2,1)}), bf16[16,144,512]{2,1,0:T(8,128)(2,1)}) %all-gather.5.cloned.1.call-update) | async-done | bytes 2359312 | tf_op jit(solution)/shard_map/all_gather | solution.py:224
  65.8 1.7 %copy-done = bf16[16,144,512]{2,1,0:T(8,128)(2,1)S(1)} copy-done((bf16[16,144,512]{2,1,0:T(8,128)(2,1)S(1)}, bf16[16,144,512]{2,1,0:T(8,128)(2,1)}, u32[]{:S(2)}) %copy-start) | copy-done | bytes 2359320
  67.5 0.7 copy-done.5
  68.2 1.7 %row_stats.1 = (f32[16,104,128]{2,1,0:T(8,128)S(1)}, f32[2,32,128,128]{3,2,1,0:T(8,128)S(1)}, f32[2,32,128,128]{3,2,1,0:T(8,128)S(1)}, f32[2,32,1,128]{3,2,1,0:T(1,128)S(1)}) custom-call(s32[3,40]{1,0:T(4,128)S(1)} %copy-done.5, bf16[16,128,512]{2,1,0:T(8,128)(2,1)S(1)} %bitcast.18, bf16[16,144,512]{2,1,0:T(8,128)(2,1)S(1)} %copy-done), custom_call_target="tpu_custom_call" | custom-call | tf_op jit(solution)/shard_map/row_stats/pallas_call | solution.py:233
  69.9 27.2 %all_to_all.20.stats = f32[16,104,128]{2,1,0:T(8,128)S(1)} all-to-all(f32[16,104,128]{2,1,0:T(8,128)S(1)} %get-tuple-element.16), channel_id=1, replica_groups=mesh['qb'=16,'kb'=16,'pair'=2] {'kb'}, dimensions={0} | all-to-all | bytes 1703936 | tf_op jit(solution)/shard_map/all_to_all | solution.py:247
  97.2 1.8 %key_value_grads.1 = (bf16[16,128,512]{2,1,0:T(8,128)(2,1)S(1)}, bf16[2,32,128,128]{3,2,1,0:T(8,128)(2,1)S(1)}, f32[8,128]{1,0:T(8,128)S(1)}) custom-call(s32[3,40]{1,0:T(4,128)S(1)} %copy-done.6, bf16[16,128,512]{2,1,0:T(8,128)(2,1)S(1)} %bitcast.19, f32[16,104,128]{2,1,0:T(8,128)S(1)} %all_to_all.20.stats, ...), custom_call_target="tpu_custom_call" | custom-call | tf_op jit(solution)/shard_map/key_value_grads/pallas_call | solution.py:248
  99.0 1.4 copy-done.2
  100.3 1.3 copy-done.4
  101.7 2.1 %collective-permute-start = (f32[8,128]{1,0:T(8,128)S(1)}, f32[8,128]{1,0:T(8,128)S(1)}, u32[]{:S(2)}, u32[]{:S(2)}) collective-permute-start(f32[8,128]{1,0:T(8,128)S(1)} %get-tuple-element.20), channel_id=1, source_target_pairs={{0,1},{1,0},{2,3},{3,2},{4,5},{5,4},{6,7},{7,6},{8,9},{9,8},{10,11... | collective-permute-start | bytes 12296 | tf_op jit(solution)/shard_map/ppermute | solution.py:273
  103.7 1.7 %copy-done.1 = bf16[16,144,512]{2,1,0:T(8,128)(2,1)S(1)} copy-done((bf16[16,144,512]{2,1,0:T(8,128)(2,1)S(1)}, bf16[16,144,512]{2,1,0:T(8,128)(2,1)}, u32[]{:S(2)}) %copy-start.1) | copy-done | bytes 2359320
  105.4 1.4 query_grads.1
  106.8 19.7 %all_to_all.21 = bf16[4,4,128,256]{3,2,1,0:T(8,128)(2,1)S(1)} all-to-all(bf16[4,4,128,256]{3,2,1,0:T(8,128)(2,1)S(1)} %bitcast.20), channel_id=1, replica_groups={{0,2,4,6},{8,10,12,14},{16,18,20,22},{24,26,28,30},{1,3,5,7},{9,11,13,1..., dimensions={0} | all-to-all | bytes 2097152 | tf_op jit(solution)/shard_map/all_to_all | solution.py:282
  126.5 0.9 reduce_sum.21
  127.4 3.4 %all-to-all-start.3 = ((bf16[4,128,256]{2,1,0:T(8,128)(2,1)}), bf16[4,128,256]{2,1,0:T(8,128)(2,1)S(1)}, u32[]{:S(2)}, u32[]{:S(2)}) async-start(bf16[4,128,256]{2,1,0:T(8,128)(2,1)} %reduce_sum.21), calls=%async_computation.3 | async-start | bytes 524288 | tf_op jit(solution)/shard_map/all_to_all | solution.py:284
  130.9 0.5 slice.31
  131.4 0.5 slice.30
  134.6 5.9 %all-to-all-done.3 = bf16[4,128,256]{2,1,0:T(8,128)(2,1)S(1)} async-done(((bf16[4,128,256]{2,1,0:T(8,128)(2,1)}), bf16[4,128,256]{2,1,0:T(8,128)(2,1)S(1)}, u32[]{:S(2)}, u32[]{:S(2)}) %all-to-all-start.3) | async-done | bytes 262176 | tf_op jit(solution)/shard_map/all_to_all | solution.py:284
  140.5 6.7 %reduce-scatter.2.cloned.1.call-done = bf16[1,256,512]{2,1,0:T(8,128)(2,1)} async-done(((bf16[8,256,512]{2,1,0:T(8,128)(2,1)}), bf16[1,256,512]{2,1,0:T(8,128)(2,1)}) %reduce-scatter.2.cloned.1.call-update) | async-done | bytes 262160 | tf_op jit(solution)/shard_map/reduce_scatter | solution.py:261
  147.2 1.0 slice_bitcast_fusion.1
  148.2 3.5 %collective-permute-start.1 = (bf16[128,512]{1,0:T(8,128)(2,1)S(1)}, bf16[128,512]{1,0:T(8,128)(2,1)S(1)}, u32[]{:S(2)}, u32[]{:S(2)}) collective-permute-start(bf16[128,512]{1,0:T(8,128)(2,1)S(1)} %get-tuple-element.28), channel_id=1, source_target_pairs={{0,256},{32,288},{64,320},{96,352},{128,384},{160,416},{192,448},{... | collective-permute-start | bytes 393224 | tf_op jit(solution)/shard_map/ppermute | solution.py:289
  151.7 0.6 fusion
  152.3 2.7 %collective-permute-done.1 = bf16[128,512]{1,0:T(8,128)(2,1)S(1)} collective-permute-done((bf16[128,512]{1,0:T(8,128)(2,1)S(1)}, bf16[128,512]{1,0:T(8,128)(2,1)S(1)}, u32[]{:S(2)}, u32[]{:S(2)}) %collective-permute-start.1) | collective-permute-done | bytes 131104 | tf_op jit(solution)/shard_map/ppermute | solution.py:289
  155.0 0.7 fusion.2
  (13 shorter events, 0.1 us)
Async XLA Ops:
  7.2 58.7 %all-gather.5.cloned.1.call-start = ((), (), s32[]{:S(2)}) async-start(), calls=%async_computation.6 | async-start | bytes 2654208 | tf_op jit(solution)/shard_map/all_gather | solution.py:224
  37.3 24.0 %all-to-all-start = ((bf16[4,4,128,512]{3,2,1,0:T(8,128)(2,1)}), bf16[4,4,128,512]{3,2,1,0:T(8,128)(2,1)S(1)}, u32[]{:S(2)}, u32[]{:S(2)}) async-start(bf16[4,4,128,512]{3,2,1,0:T(8,128)(2,1)} %broadcast_in_dim.2), calls=%async_computation | async-start | bytes 4194304 | tf_op jit(solution)/shard_map/all_to_all | solution.py:226
  42.0 105.1 %reduce-scatter.2.cloned.1.call-start = ((), (), s32[]{:S(2)}) async-start(), calls=%async_computation.5 | async-start | bytes 2359296 | tf_op jit(solution)/shard_map/reduce_scatter | solution.py:261
  65.8 1.7 %copy-start = (bf16[16,144,512]{2,1,0:T(8,128)(2,1)S(1)}, bf16[16,144,512]{2,1,0:T(8,128)(2,1)}, u32[]{:S(2)}) copy-start(bf16[16,144,512]{2,1,0:T(8,128)(2,1)} %all-gather.5.cloned.1.call-done.kv) | copy-start | bytes 7077892
  67.5 0.7 copy-start.5
  68.2 29.0 %copy-start.6 = (s32[3,40]{1,0:T(4,128)S(1)}, s32[3,40]{1,0:T(4,128)}, u32[]{:S(2)}) copy-start(s32[3,40]{1,0:T(4,128)} %pair_lists.1.lists) | copy-start | bytes 1444
  99.0 1.4 copy-start.2
  100.3 1.3 copy-start.4
  101.6 2.1 %copy-start.3 = (bf16[2,32,128,128]{3,2,1,0:T(8,128)(2,1)S(1)}, bf16[2,32,128,128]{3,2,1,0:T(8,128)(2,1)}, u32[]{:S(2)}) copy-start(bf16[2,32,128,128]{3,2,1,0:T(8,128)(2,1)} %copy-done.2) | copy-start | bytes 6291460
  101.7 5.1 %collective-permute-start = (f32[8,128]{1,0:T(8,128)S(1)}, f32[8,128]{1,0:T(8,128)S(1)}, u32[]{:S(2)}, u32[]{:S(2)}) collective-permute-start(f32[8,128]{1,0:T(8,128)S(1)} %get-tuple-element.20), channel_id=1, source_target_pairs={{0,1},{1,0},{2,3},{3,2},{4,5},{5,4},{6,7},{7,6},{8,9},{9,8},{10,11... | collective-permute-start | bytes 12296 | tf_op jit(solution)/shard_map/ppermute | solution.py:273
  103.7 1.7 %copy-start.1 = (bf16[16,144,512]{2,1,0:T(8,128)(2,1)S(1)}, bf16[16,144,512]{2,1,0:T(8,128)(2,1)}, u32[]{:S(2)}) copy-start(bf16[16,144,512]{2,1,0:T(8,128)(2,1)} %all-gather.5.cloned.1.call-done.kv) | copy-start | bytes 7077892
  127.4 13.0 %all-to-all-start.3 = ((bf16[4,128,256]{2,1,0:T(8,128)(2,1)}), bf16[4,128,256]{2,1,0:T(8,128)(2,1)S(1)}, u32[]{:S(2)}, u32[]{:S(2)}) async-start(bf16[4,128,256]{2,1,0:T(8,128)(2,1)} %reduce_sum.21), calls=%async_computation.3 | async-start | bytes 524288 | tf_op jit(solution)/shard_map/all_to_all | solution.py:284
  148.2 6.9 %collective-permute-start.1 = (bf16[128,512]{1,0:T(8,128)(2,1)S(1)}, bf16[128,512]{1,0:T(8,128)(2,1)S(1)}, u32[]{:S(2)}, u32[]{:S(2)}) collective-permute-start(bf16[128,512]{1,0:T(8,128)(2,1)S(1)} %get-tuple-element.28), channel_id=1, source_target_pairs={{0,256},{32,288},{64,320},{96,352},{128,384},{160,416},{192,448},{... | collective-permute-start | bytes 393224 | tf_op jit(solution)/shard_map/ppermute | solution.py:289
Sparse Core Ops, SparseCore 0:
  17.0 48.7 all-gather.4
  101.8 45.3 reduce-scatter.1

commit v5 on v4

--- a/solution.py
+++ b/solution.py
@@ -68,19 +68,23 @@
         lists[HEADS, head] = lax.fori_loop(0, GB, step, 0)
 
 
-def for_pairs(lists, work):
+def for_pairs(lists, work, most=4):
     count = lists[HEADS, 0]
-
-    def fours(step, carry):
-        work([(head, 4 * step + u) for u in range(4) for head in range(HEADS)])
+    whole = count // most
+
+    def several(step, carry):
+        work([(head, most * step + u) for u in range(most) for head in range(HEADS)])
         return carry
 
-    lax.fori_loop(0, count >> 2, fours, 0)
-
-    @pl.when((count & 2) != 0)
-    def _():
-        first = (count >> 2) * 4
-        work([(head, first + u) for u in range(2) for head in range(HEADS)])
+    lax.fori_loop(0, whole, several, 0)
+    first, rest = whole * most, most // 2
+    while rest >= 2:
+
+        @pl.when((count & rest) != 0)
+        def _(first=first, rest=rest):
+            work([(head, first + u) for u in range(rest) for head in range(HEADS)])
+
+        first, rest = first + (count & rest), rest // 2
 
 
 def blocks_at(ref, slot, head):
@@ -119,7 +123,7 @@
             total[at] = total[at] * old_weight + own_total * own_weight
             delta[at] = delta[at] * old_weight + own_delta * own_weight
 
-    for_pairs(lists, work)
+    for_pairs(lists, work, 8)
     for at in range(SLOTS):
         stats[0, at : at + 1, :] = top[at]
         stats[0, SLOTS + at : SLOTS + at + 1, :] = total[at]
@@ -135,7 +139,7 @@
 
 
 def key_kernel(
-    lists, qg, stats, shifted, grad_scores, own_tops, kvout, dscores, latent, shift, delta, kacc, vacc
+    lists, qg, stats, shifted, grad_scores, own_tops, kvout, latent, shift, delta, kacc, vacc
 ):
     tops = stats[0, :SLOTS]
     for part in range(1, GB):
@@ -166,7 +170,6 @@
             scale = jnp.exp2(own_tops[head, at] - shift[head * GB + row])
             weights = shifted[head, at] * scale
             dscore = (weights * (grad_scores[head, at] - delta[head * GB + row])).astype(jnp.bfloat16)
-            dscores[head, at] = dscore
             kterm = dot(dscore, query, ((1,), (0,)))
             vterm = dot(weights.astype(jnp.bfloat16), grad, ((1,), (0,)))
             found.append((head * GB + col, kterm, vterm))
@@ -183,7 +186,7 @@
             kvout[target, :, second : second + DH] = vacc[head * GB + slot].astype(jnp.bfloat16)
 
 
-def query_kernel(lists, kv, dscores, qout, qacc):
+def query_kernel(lists, kv, shifted, grad_scores, own_tops, shift, delta, qout, qacc):
     qacc[...] = jnp.zeros_like(qacc)
 
     def work(pairs):
@@ -191,7 +194,10 @@
         for head, at in pairs:
             both = lists[head, at]
             key, _ = blocks_at(kv, both & 15, head)
-            found.append((head * GB + (both >> 4), dot(dscores[head, at], key, ((0,), (0,)))))
+            row = head * GB + (both >> 4)
+            scale = jnp.exp2(own_tops[head, at] - shift[row])
+            dscore = shifted[head, at] * scale * (grad_scores[head, at] - delta[row])
+            found.append((row, dot(dscore.astype(jnp.bfloat16), key, ((0,), (0,)))))
         for at, qterm in found:
             qacc[at] += qterm
 
@@ -245,16 +251,17 @@
         name="row_stats",
     )(lists, qg, kv)
     stats = lax.all_to_all(stats, "kb", 0, 0)
-    kvpart, dscores, latent = pl.pallas_call(
+    kvpart, latent, shift, delta = pl.pallas_call(
         key_kernel,
         out_shape=(
             shape(GB, BLK, 2 * WIDE),
-            shape(HEADS, 2 * GB, BLK, BLK),
             shape(8, DH, dtype=jnp.float32),
+            shape(SLOTS, 1, DH, dtype=jnp.float32),
+            shape(SLOTS, 1, DH, dtype=jnp.float32),
         ),
         in_specs=[SMEM] + [VMEM] * 5,
-        out_specs=(VMEM, VMEM, VMEM),
-        scratch_shapes=[row_scratch, row_scratch, block_scratch, block_scratch],
+        out_specs=(VMEM,) * 4,
+        scratch_shapes=[block_scratch, block_scratch],
         compiler_params=params(28),
         name="key_value_grads",
     )(lists, qg, stats, shifted, grad_scores, tops)
@@ -264,14 +271,13 @@
     qpart = pl.pallas_call(
         query_kernel,
         out_shape=shape(GB, BLK, WIDE),
-        in_specs=[SMEM, VMEM, VMEM],
+        in_specs=[SMEM] + [VMEM] * 6,
         out_specs=VMEM,
         scratch_shapes=[block_scratch],
         compiler_params=params(28),
         name="query_grads",
-    )(lists, kv, dscores)
+    )(lists, kv, shifted, grad_scores, tops, shift, delta)
     partner = lax.ppermute(latent, "pair", [(0, 1), (1, 0)])
-    partner, qpart = lax.optimization_barrier((partner, qpart))
     own, other = latent[0, 0], partner[0, 0]
     pair_side = lax.axis_index("pair")
     winner_mean = jnp.where(pair_side == 0, own, other) / TOKENS

time: 163 us -> 162 us (level)
  blocking collectives: 73.8 us -> 69.2 us
  local copies, waits for them, and re-layouts: 10.2 us -> 13.3 us
    all_to_all x1, blocking collectives: 19.7 us -> 14.7 us  [body(): lax.all_to_all(qpart.reshape(4, 4, BLK, WIDE), 'kb', 0, 0, axis_index_gro...]
    all_to_all x1, waiting for transfers between devices: 5.86 us -> 2.79 us  [body(): qpart = lax.all_to_all(qpart, 'kb', 0, 0, axis_index_groups=Y_GROUPS)]
    unnamed x14 -> x18, local copies, waits for them, and re-layouts: 6.69 us -> 9.74 us
    reduce_scatter x1, waiting for transfers between devices: 6.71 us -> 9.17 us  [body(): lax.psum_scatter(kvpart.reshape(8, 2 * BLK, 2 * WIDE), 'qb', scatter_dime...]
  transfers between devices with their start and end apart: 6 -> 6, of which waited for: 5 -> 6; matrix products, arithmetic and copies ran while one was open for 3% -> 3% of each run, Pallas kernels for 3% -> 3%
where the time goes in v5:
time: 162 us; the launch traced here: 161 us
  blocking collectives  69.2 us (43%)
  waiting for transfers between devices  36.6 us (23%)
  between operations  16.8 us (10%)
  local copies, waits for them, and re-layouts  13.3 us (8%)
  starting transfers between devices  13 us (8%)
  Pallas kernels  9.58 us (6%)
  other arithmetic  2.26 us (1%)
    all_to_all x1, blocking collectives, body(): stats = lax.all_to_all(stats, 'kb', 0, 0)  27.7 us
    all_gather x1, blocking collectives, body(): qg = lax.all_gather(qg, 'kb', axis_index_groups=Y_GROUPS)  18.9 us
    all_to_all x1, waiting for transfers between devices, body(): lax.all_to_all(jnp.broadcast_to(qg[None], (4, 4, BLK, 2 * WIDE)), 'kb', 0...  16.1 us
    all_to_all x1, blocking collectives, body(): lax.all_to_all(qpart.reshape(4, 4, BLK, WIDE), 'kb', 0, 0, axis_index_gro...  14.7 us
    unnamed x18, local copies, waits for them, and re-layouts  9.74 us
    reduce_scatter x1, waiting for transfers between devices, body(): lax.psum_scatter(kvpart.reshape(8, 2 * BLK, 2 * WIDE), 'qb', scatter_dime...  9.17 us
    all_gather x1, blocking collectives, body(): kv = lax.all_gather(kv, 'qb', axis_index_groups=Y_PAIRS)  7.94 us
    all_to_all x1, starting transfers between devices, body(): lax.all_to_all(jnp.broadcast_to(qg[None], (4, 4, BLK, 2 * WIDE)), 'kb', 0...  4.77 us
  transfers between devices with their start and end apart: 6, of which 6 were waited for; matrix products, arithmetic and copies ran while one was open for 3% of the time, Pallas kernels for 3%

profile of v5, /device:TPU:6, one launch (start us, length us, event | category | flops | bytes accessed | tf_op | source)
XLA Modules:
  0.0 160.8 jit_solution(6690993244761238709)
XLA Ops:
  7.2 1.7 %pack.1 = (bf16[128,512]{1,0:T(8,128)(2,1)}, bf16[144,512]{1,0:T(8,128)(2,1)}) custom-call(bf16[1,128,256]{2,1,0:T(8,128)(2,1)} %queries.1, bf16[1,128,256]{2,1,0:T(8,128)(2,1)} %keys.1, bf16[1,128,256]{2,1,0:T(8,128)(2,1)} %values.1, bf16[1,128,256]{2,1,0:T(8,128)(2,1)} %out_grad.1, f32[1,128]{1,0:T(1,128)} %token_error.1), custom_call_target="tpu_custom_call" | custom-call | tf_op jit(solution)/shard_map/pack/pallas_call | solution.py:215
  8.9 7.9 %all-gather = bf16[288,512]{1,0:T(8,128)(2,1)} all-gather(bf16[144,512]{1,0:T(8,128)(2,1)} %get-tuple-element.13), channel_id=2, replica_groups={{0,256},{32,288},{64,320},{96,352},{128,384},{160,416},{192,448},{224,4..., dimensions={0}, use_global_device_ids=true | all-gather | bytes 442368 | tf_op jit(solution)/shard_map/all_gather | solution.py:229
  16.9 18.9 %all-gather.2 = bf16[512,512]{1,0:T(8,128)(2,1)S(1)} all-gather(bf16[128,512]{1,0:T(8,128)(2,1)} %get-tuple-element.14), channel_id=4, replica_groups={{0,8,16,24},{2,10,18,26},{4,12,20,28},{6,14,22,30},{1,9,17,25},{3,11,19..., dimensions={0}, use_global_device_ids=true | all-gather | bytes 655360 | tf_op jit(solution)/shard_map/all_gather | solution.py:231
  35.7 1.6 broadcast_in_dim.2
  37.3 4.8 %all-to-all-start = ((bf16[4,4,128,512]{3,2,1,0:T(8,128)(2,1)}), bf16[4,4,128,512]{3,2,1,0:T(8,128)(2,1)S(1)}, u32[]{:S(2)}, u32[]{:S(2)}) async-start(bf16[4,4,128,512]{3,2,1,0:T(8,128)(2,1)} %broadcast_in_dim.2), calls=%async_computation | async-start | bytes 4194304 | tf_op jit(solution)/shard_map/all_to_all | solution.py:232
  42.1 3.1 %pair_lists.1.lists = s32[3,40]{1,0:T(4,128)} custom-call(s32[2,16,16]{2,1,0:T(8,128)} %mask.1, s32[1]{0:T(128)} %bitcast.side), custom_call_target="tpu_custom_call" | custom-call | tf_op jit(solution)/shard_map/pair_lists/pallas_call | solution.py:222
  45.2 16.1 %all-to-all-done = bf16[4,4,128,512]{3,2,1,0:T(8,128)(2,1)S(1)} async-done(((bf16[4,4,128,512]{3,2,1,0:T(8,128)(2,1)}), bf16[4,4,128,512]{3,2,1,0:T(8,128)(2,1)S(1)}, u32[]{:S(2)}, u32[]{:S(2)}) %all-to-all-start) | async-done | bytes 2097184 | tf_op jit(solution)/shard_map/all_to_all | solution.py:232
  61.3 4.6 %all-gather.5.cloned.1.call-done.kv = bf16[16,144,512]{2,1,0:T(8,128)(2,1)} async-done(((bf16[2,144,512]{2,1,0:T(8,128)(2,1)}), bf16[16,144,512]{2,1,0:T(8,128)(2,1)}) %all-gather.5.cloned.1.call-update) | async-done | bytes 2359312 | tf_op jit(solution)/shard_map/all_gather | solution.py:230
  65.8 1.7 %copy-done.4 = bf16[16,144,512]{2,1,0:T(8,128)(2,1)S(1)} copy-done((bf16[16,144,512]{2,1,0:T(8,128)(2,1)S(1)}, bf16[16,144,512]{2,1,0:T(8,128)(2,1)}, u32[]{:S(2)}) %copy-start.4) | copy-done | bytes 2359320
  67.5 0.7 copy-done.7
  68.2 1.6 row_stats.1
  69.8 27.7 %all_to_all.20.stats = f32[16,104,128]{2,1,0:T(8,128)S(1)} all-to-all(f32[16,104,128]{2,1,0:T(8,128)S(1)} %get-tuple-element.18), channel_id=1, replica_groups=mesh['qb'=16,'kb'=16,'pair'=2] {'kb'}, dimensions={0} | all-to-all | bytes 1703936 | tf_op jit(solution)/shard_map/all_to_all | solution.py:253
  97.4 1.8 %key_value_grads.1 = (bf16[16,128,512]{2,1,0:T(8,128)(2,1)S(1)}, f32[8,128]{1,0:T(8,128)S(1)}, f32[32,1,128]{2,1,0:T(1,128)S(1)}, f32[32,1,128]{2,1,0:T(1,128)S(1)}) custom-call(s32[3,40]{1,0:T(4,128)S(1)} %copy-done.8, bf16[16,128,512]{2,1,0:T(8,128)(2,1)S(1)} %bitcast.19, f32[16,104,128]{2,1,0:T(8,128)S(1)} %all_to_all.20.stats, ...), custom_call_target="tpu_custom_call" | custom-call | tf_op jit(solution)/shard_map/key_value_grads/pallas_call | solution.py:254
  99.3 1.4 copy-done.6
  100.7 2.2 %copy-done.1 = f32[2,32,128,128]{3,2,1,0:T(8,128)S(1)} copy-done((f32[2,32,128,128]{3,2,1,0:T(8,128)S(1)}, f32[2,32,128,128]{3,2,1,0:T(8,128)}, u32[]{:S(2)}) %copy-start.1) | copy-done | bytes 4194328
  102.8 2.2 %copy-done.3 = f32[2,32,128,128]{3,2,1,0:T(8,128)S(1)} copy-done((f32[2,32,128,128]{3,2,1,0:T(8,128)S(1)}, f32[2,32,128,128]{3,2,1,0:T(8,128)}, u32[]{:S(2)}) %copy-start.3) | copy-done | bytes 4194328
  105.0 1.7 %copy-done.5 = bf16[16,144,512]{2,1,0:T(8,128)(2,1)S(1)} copy-done((bf16[16,144,512]{2,1,0:T(8,128)(2,1)S(1)}, bf16[16,144,512]{2,1,0:T(8,128)(2,1)}, u32[]{:S(2)}) %copy-start.5) | copy-done | bytes 2359320
  106.7 1.4 query_grads.1
  108.1 14.7 %all_to_all.21 = bf16[4,4,128,256]{3,2,1,0:T(8,128)(2,1)S(1)} all-to-all(bf16[4,4,128,256]{3,2,1,0:T(8,128)(2,1)S(1)} %bitcast.20), channel_id=1, replica_groups={{0,2,4,6},{8,10,12,14},{16,18,20,22},{24,26,28,30},{1,3,5,7},{9,11,13,1..., dimensions={0} | all-to-all | bytes 2097152 | tf_op jit(solution)/shard_map/all_to_all | solution.py:288
  122.9 0.9 reduce_sum.21
  123.8 3.4 %all-to-all-start.3 = ((bf16[4,128,256]{2,1,0:T(8,128)(2,1)}), bf16[4,128,256]{2,1,0:T(8,128)(2,1)S(1)}, u32[]{:S(2)}, u32[]{:S(2)}) async-start(bf16[4,128,256]{2,1,0:T(8,128)(2,1)} %reduce_sum.21), calls=%async_computation.3 | async-start | bytes 524288 | tf_op jit(solution)/shard_map/all_to_all | solution.py:290
  127.2 1.9 %collective-permute-start = (f32[8,128]{1,0:T(8,128)S(1)}, f32[8,128]{1,0:T(8,128)S(1)}, u32[]{:S(2)}, u32[]{:S(2)}) collective-permute-start(f32[8,128]{1,0:T(8,128)S(1)} %get-tuple-element.21), channel_id=1, source_target_pairs={{0,1},{1,0},{2,3},{3,2},{4,5},{5,4},{6,7},{7,6},{8,9},{9,8},{10,11... | collective-permute-start | bytes 12296 | tf_op jit(solution)/shard_map/ppermute | solution.py:280
  129.1 0.5 slice.31
  129.6 0.6 collective-permute-done
  130.2 0.5 slice.30
  133.4 2.8 %all-to-all-done.3 = bf16[4,128,256]{2,1,0:T(8,128)(2,1)S(1)} async-done(((bf16[4,128,256]{2,1,0:T(8,128)(2,1)}), bf16[4,128,256]{2,1,0:T(8,128)(2,1)S(1)}, u32[]{:S(2)}, u32[]{:S(2)}) %all-to-all-start.3) | async-done | bytes 262176 | tf_op jit(solution)/shard_map/all_to_all | solution.py:290
  136.3 9.2 %reduce-scatter.2.cloned.1.call-done = bf16[1,256,512]{2,1,0:T(8,128)(2,1)} async-done(((bf16[8,256,512]{2,1,0:T(8,128)(2,1)}), bf16[1,256,512]{2,1,0:T(8,128)(2,1)}) %reduce-scatter.2.cloned.1.call-update) | async-done | bytes 262160 | tf_op jit(solution)/shard_map/reduce_scatter | solution.py:268
  145.4 1.0 slice_bitcast_fusion.1
  146.4 2.9 %collective-permute-start.1 = (bf16[128,512]{1,0:T(8,128)(2,1)S(1)}, bf16[128,512]{1,0:T(8,128)(2,1)S(1)}, u32[]{:S(2)}, u32[]{:S(2)}) collective-permute-start(bf16[128,512]{1,0:T(8,128)(2,1)S(1)} %get-tuple-element.26), channel_id=1, source_target_pairs={{0,256},{32,288},{64,320},{96,352},{128,384},{160,416},{192,448},{... | collective-permute-start | bytes 393224 | tf_op jit(solution)/shard_map/ppermute | solution.py:295
  149.3 0.6 fusion
  150.0 3.3 %collective-permute-done.1 = bf16[128,512]{1,0:T(8,128)(2,1)S(1)} collective-permute-done((bf16[128,512]{1,0:T(8,128)(2,1)S(1)}, bf16[128,512]{1,0:T(8,128)(2,1)S(1)}, u32[]{:S(2)}, u32[]{:S(2)}) %collective-permute-start.1) | collective-permute-done | bytes 131104 | tf_op jit(solution)/shard_map/ppermute | solution.py:295
  153.3 0.7 fusion.2
  (17 shorter events, 0.1 us)
Async XLA Ops:
  7.2 58.7 %all-gather.5.cloned.1.call-start = ((), (), s32[]{:S(2)}) async-start(), calls=%async_computation.6 | async-start | bytes 2654208 | tf_op jit(solution)/shard_map/all_gather | solution.py:230
  37.3 24.0 %all-to-all-start = ((bf16[4,4,128,512]{3,2,1,0:T(8,128)(2,1)}), bf16[4,4,128,512]{3,2,1,0:T(8,128)(2,1)S(1)}, u32[]{:S(2)}, u32[]{:S(2)}) async-start(bf16[4,4,128,512]{3,2,1,0:T(8,128)(2,1)} %broadcast_in_dim.2), calls=%async_computation | async-start | bytes 4194304 | tf_op jit(solution)/shard_map/all_to_all | solution.py:232
  42.1 103.4 %reduce-scatter.2.cloned.1.call-start = ((), (), s32[]{:S(2)}) async-start(), calls=%async_computation.5 | async-start | bytes 2359296 | tf_op jit(solution)/shard_map/reduce_scatter | solution.py:268
  65.8 1.7 %copy-start.4 = (bf16[16,144,512]{2,1,0:T(8,128)(2,1)S(1)}, bf16[16,144,512]{2,1,0:T(8,128)(2,1)}, u32[]{:S(2)}) copy-start(bf16[16,144,512]{2,1,0:T(8,128)(2,1)} %all-gather.5.cloned.1.call-done.kv) | copy-start | bytes 7077892
  67.5 0.7 copy-start.7
  68.2 29.2 %copy-start.8 = (s32[3,40]{1,0:T(4,128)S(1)}, s32[3,40]{1,0:T(4,128)}, u32[]{:S(2)}) copy-start(s32[3,40]{1,0:T(4,128)} %pair_lists.1.lists) | copy-start | bytes 1444
  69.8 29.5 %copy-start = (f32[2,32,128,128]{3,2,1,0:T(8,128)}, f32[2,32,128,128]{3,2,1,0:T(8,128)S(1)}, u32[]{:S(2)}) copy-start(f32[2,32,128,128]{3,2,1,0:T(8,128)S(1)} %get-tuple-element.15.shifted) | copy-start | bytes 12582916
  69.8 29.5 %copy-start.2 = (f32[2,32,128,128]{3,2,1,0:T(8,128)}, f32[2,32,128,128]{3,2,1,0:T(8,128)S(1)}, u32[]{:S(2)}) copy-start(f32[2,32,128,128]{3,2,1,0:T(8,128)S(1)} %get-tuple-element.16.grad_scores) | copy-start | bytes 12582916
  99.3 1.4 copy-start.6
  100.6 2.2 %copy-start.1 = (f32[2,32,128,128]{3,2,1,0:T(8,128)S(1)}, f32[2,32,128,128]{3,2,1,0:T(8,128)}, u32[]{:S(2)}) copy-start(f32[2,32,128,128]{3,2,1,0:T(8,128)} %copy-done) | copy-start | bytes 12582916
  102.8 2.2 %copy-start.3 = (f32[2,32,128,128]{3,2,1,0:T(8,128)S(1)}, f32[2,32,128,128]{3,2,1,0:T(8,128)}, u32[]{:S(2)}) copy-start(f32[2,32,128,128]{3,2,1,0:T(8,128)} %copy-done.2) | copy-start | bytes 12582916
  105.0 1.7 %copy-start.5 = (bf16[16,144,512]{2,1,0:T(8,128)(2,1)S(1)}, bf16[16,144,512]{2,1,0:T(8,128)(2,1)}, u32[]{:S(2)}) copy-start(bf16[16,144,512]{2,1,0:T(8,128)(2,1)} %all-gather.5.cloned.1.call-done.kv) | copy-start | bytes 7077892
  123.8 12.5 %all-to-all-start.3 = ((bf16[4,128,256]{2,1,0:T(8,128)(2,1)}), bf16[4,128,256]{2,1,0:T(8,128)(2,1)S(1)}, u32[]{:S(2)}, u32[]{:S(2)}) async-start(bf16[4,128,256]{2,1,0:T(8,128)(2,1)} %reduce_sum.21), calls=%async_computation.3 | async-start | bytes 524288 | tf_op jit(solution)/shard_map/all_to_all | solution.py:290
  127.2 3.1 %collective-permute-start = (f32[8,128]{1,0:T(8,128)S(1)}, f32[8,128]{1,0:T(8,128)S(1)}, u32[]{:S(2)}, u32[]{:S(2)}) collective-permute-start(f32[8,128]{1,0:T(8,128)S(1)} %get-tuple-element.21), channel_id=1, source_target_pairs={{0,1},{1,0},{2,3},{3,2},{4,5},{5,4},{6,7},{7,6},{8,9},{9,8},{10,11... | collective-permute-start | bytes 12296 | tf_op jit(solution)/shard_map/ppermute | solution.py:280
  146.4 6.9 %collective-permute-start.1 = (bf16[128,512]{1,0:T(8,128)(2,1)S(1)}, bf16[128,512]{1,0:T(8,128)(2,1)S(1)}, u32[]{:S(2)}, u32[]{:S(2)}) collective-permute-start(bf16[128,512]{1,0:T(8,128)(2,1)S(1)} %get-tuple-element.26), channel_id=1, source_target_pairs={{0,256},{32,288},{64,320},{96,352},{128,384},{160,416},{192,448},{... | collective-permute-start | bytes 393224 | tf_op jit(solution)/shard_map/ppermute | solution.py:295
Sparse Core Ops, SparseCore 0:
  17.0 48.7 all-gather.4
  100.8 44.6 reduce-scatter.1

commit v6 on v5

--- a/solution.py
+++ b/solution.py
@@ -134,20 +134,39 @@
     sums = jnp.sum(sums, axis=0, keepdims=True)
     stats[0, 3 * SLOTS :, :] = jnp.broadcast_to(sums, (8, DH))
     own = stats[0]
-    for part in range(1, GB):
+    for part in range(1, 4):
         stats[part] = own
+
+
+def merge_kernel(stats, merged):
+    tops = stats[0, :SLOTS]
+    for part in range(1, 4):
+        tops = jnp.maximum(tops, stats[part, :SLOTS])
+    totals = jnp.zeros_like(tops)
+    deltas = jnp.zeros_like(tops)
+    sums = jnp.zeros((8, DH), jnp.float32)
+    for part in range(4):
+        weight = jnp.exp2(stats[part, :SLOTS] - tops)
+        totals = totals + stats[part, SLOTS : 2 * SLOTS] * weight
+        deltas = deltas + stats[part, 2 * SLOTS : 3 * SLOTS] * weight
+        sums = sums + stats[part, 3 * SLOTS :]
+    for part in range(4):
+        merged[part, :SLOTS] = tops
+        merged[part, SLOTS : 2 * SLOTS] = totals
+        merged[part, 2 * SLOTS : 3 * SLOTS] = deltas
+        merged[part, 3 * SLOTS :] = sums
 
 
 def key_kernel(
     lists, qg, stats, shifted, grad_scores, own_tops, kvout, latent, shift, delta, kacc, vacc
 ):
     tops = stats[0, :SLOTS]
-    for part in range(1, GB):
+    for part in range(1, 4):
         tops = jnp.maximum(tops, stats[part, :SLOTS])
     totals = jnp.zeros_like(tops)
     deltas = jnp.zeros_like(tops)
     sums = jnp.zeros((8, DH), jnp.float32)
-    for part in range(GB):
+    for part in range(4):
         weight = jnp.exp2(stats[part, :SLOTS] - tops)
         totals = totals + stats[part, SLOTS : 2 * SLOTS] * weight
         deltas = deltas + stats[part, 2 * SLOTS : 3 * SLOTS] * weight
@@ -224,6 +243,7 @@
         out_shape=shape(HEADS + 1, LIST, dtype=jnp.int32),
         in_specs=[SMEM, SMEM],
         out_specs=SMEM,
+        compiler_params=params(4),
         name="pair_lists",
     )(block_mask, (lax.axis_index("qb") // 8).astype(jnp.int32).reshape(1))
     kv = lax.all_gather(kv, "qb", axis_index_groups=Y_PAIRS)
@@ -239,7 +259,7 @@
     stats, shifted, grad_scores, tops = pl.pallas_call(
         stat_kernel,
         out_shape=(
-            shape(GB, STAT, DH, dtype=jnp.float32),
+            shape(4, STAT, DH, dtype=jnp.float32),
             by_pair,
             by_pair,
             shape(HEADS, 2 * GB, 1, DH, dtype=jnp.float32),
@@ -250,7 +270,16 @@
         compiler_params=params(28),
         name="row_stats",
     )(lists, qg, kv)
-    stats = lax.all_to_all(stats, "kb", 0, 0)
+    stats = lax.all_to_all(stats, "kb", 0, 0, axis_index_groups=X_GROUPS)
+    stats = pl.pallas_call(
+        merge_kernel,
+        out_shape=shape(4, STAT, DH, dtype=jnp.float32),
+        in_specs=[VMEM],
+        out_specs=VMEM,
+        compiler_params=params(4),
+        name="merge_stats",
+    )(stats)
+    stats = lax.all_to_all(stats, "kb", 0, 0, axis_index_groups=Y_GROUPS)
     kvpart, latent, shift, delta = pl.pallas_call(
         key_kernel,
         out_shape=(

time: 162 us -> 156 us (0.963)
  waiting for transfers between devices: 36.6 us -> 31.7 us
    reduce_scatter x1, waiting for transfers between devices: 9.17 us -> 4.85 us  [body(): lax.psum_scatter(kvpart.reshape(8, 2 * BLK, 2 * WIDE), 'qb', scatter_dime...]
    all_to_all x1 -> x2, blocking collectives: 27.7 us -> 24.9 us  [the longest x1 15 us: body(): stats = lax.all_to_all(stats, 'kb', 0, 0, axis_index_groups=Y_GROUPS)]
    all_to_all x1, blocking collectives: 14.7 us -> 16.8 us  [body(): lax.all_to_all(qpart.reshape(4, 4, BLK, WIDE), 'kb', 0, 0, axis_index_gro...]
    unnamed x18 -> x16, local copies, waits for them, and re-layouts: 9.74 us -> 9.07 us
where the time goes in v6:
time: 156 us; the launch traced here: 155 us
  blocking collectives  68.6 us (44%)
  waiting for transfers between devices  31.7 us (20%)
  between operations  16.8 us (11%)
  starting transfers between devices  13.7 us (9%)
  local copies, waits for them, and re-layouts  12.6 us (8%)
  Pallas kernels  9.41 us (6%)
  other arithmetic  2.27 us (1%)
    all_gather x1, blocking collectives, body(): qg = lax.all_gather(qg, 'kb', axis_index_groups=Y_GROUPS)  18.9 us
    all_to_all x1, blocking collectives, body(): lax.all_to_all(qpart.reshape(4, 4, BLK, WIDE), 'kb', 0, 0, axis_index_gro...  16.8 us
    all_to_all x1, waiting for transfers between devices, body(): lax.all_to_all(jnp.broadcast_to(qg[None], (4, 4, BLK, 2 * WIDE)), 'kb', 0...  16.2 us
    all_to_all x1, blocking collectives, body(): stats = lax.all_to_all(stats, 'kb', 0, 0, axis_index_groups=Y_GROUPS)  15 us
    all_to_all x1, blocking collectives, body(): stats = lax.all_to_all(stats, 'kb', 0, 0, axis_index_groups=X_GROUPS)  9.94 us
    unnamed x16, local copies, waits for them, and re-layouts  9.07 us
    all_gather x1, blocking collectives, body(): kv = lax.all_gather(kv, 'qb', axis_index_groups=Y_PAIRS)  7.95 us
    all_to_all x1, starting transfers between devices, body(): lax.all_to_all(jnp.broadcast_to(qg[None], (4, 4, BLK, 2 * WIDE)), 'kb', 0...  4.9 us
  transfers between devices with their start and end apart: 6, of which 6 were waited for; matrix products, arithmetic and copies ran while one was open for 3% of the time, Pallas kernels for 3%

profile of v6, /device:TPU:6, one launch (start us, length us, event | category | flops | bytes accessed | tf_op | source)
XLA Modules:
  0.0 155.1 jit_solution(11539991458017138706)
XLA Ops:
  7.2 1.7 %pack.1 = (bf16[128,512]{1,0:T(8,128)(2,1)}, bf16[144,512]{1,0:T(8,128)(2,1)}) custom-call(bf16[1,128,256]{2,1,0:T(8,128)(2,1)} %queries.1, bf16[1,128,256]{2,1,0:T(8,128)(2,1)} %keys.1, bf16[1,128,256]{2,1,0:T(8,128)(2,1)} %values.1, bf16[1,128,256]{2,1,0:T(8,128)(2,1)} %out_grad.1, f32[1,128]{1,0:T(1,128)} %token_error.1), custom_call_target="tpu_custom_call" | custom-call | tf_op jit(solution)/shard_map/pack/pallas_call | solution.py:234
  8.9 8.0 %all-gather = bf16[288,512]{1,0:T(8,128)(2,1)} all-gather(bf16[144,512]{1,0:T(8,128)(2,1)} %get-tuple-element.13), channel_id=2, replica_groups={{0,256},{32,288},{64,320},{96,352},{128,384},{160,416},{192,448},{224,4..., dimensions={0}, use_global_device_ids=true | all-gather | bytes 442368 | tf_op jit(solution)/shard_map/all_gather | solution.py:249
  16.9 18.9 %all-gather.2 = bf16[512,512]{1,0:T(8,128)(2,1)S(1)} all-gather(bf16[128,512]{1,0:T(8,128)(2,1)} %get-tuple-element.14), channel_id=4, replica_groups={{0,8,16,24},{2,10,18,26},{4,12,20,28},{6,14,22,30},{1,9,17,25},{3,11,19..., dimensions={0}, use_global_device_ids=true | all-gather | bytes 655360 | tf_op jit(solution)/shard_map/all_gather | solution.py:251
  35.8 1.5 broadcast_in_dim.2
  37.3 4.9 %all-to-all-start = ((bf16[4,4,128,512]{3,2,1,0:T(8,128)(2,1)}), bf16[4,4,128,512]{3,2,1,0:T(8,128)(2,1)S(1)}, u32[]{:S(2)}, u32[]{:S(2)}) async-start(bf16[4,4,128,512]{3,2,1,0:T(8,128)(2,1)} %broadcast_in_dim.2), calls=%async_computation | async-start | bytes 4194304 | tf_op jit(solution)/shard_map/all_to_all | solution.py:252
  42.2 3.0 %pair_lists.1.lists = s32[3,40]{1,0:T(4,128)S(1)} custom-call(s32[2,16,16]{2,1,0:T(8,128)S(1)} %copy-done.7, s32[1]{0:T(128)} %bitcast.side), custom_call_target="tpu_custom_call" | custom-call | tf_op jit(solution)/shard_map/pair_lists/pallas_call | solution.py:241
  45.2 16.2 %all-to-all-done = bf16[4,4,128,512]{3,2,1,0:T(8,128)(2,1)S(1)} async-done(((bf16[4,4,128,512]{3,2,1,0:T(8,128)(2,1)}), bf16[4,4,128,512]{3,2,1,0:T(8,128)(2,1)S(1)}, u32[]{:S(2)}, u32[]{:S(2)}) %all-to-all-start) | async-done | bytes 2097184 | tf_op jit(solution)/shard_map/all_to_all | solution.py:252
  61.5 4.4 %all-gather.5.cloned.1.call-done.kv = bf16[16,144,512]{2,1,0:T(8,128)(2,1)} async-done(((bf16[2,144,512]{2,1,0:T(8,128)(2,1)}), bf16[16,144,512]{2,1,0:T(8,128)(2,1)}) %all-gather.5.cloned.1.call-update) | async-done | bytes 2359312 | tf_op jit(solution)/shard_map/all_gather | solution.py:250
  65.8 1.7 %copy-done.4 = bf16[16,144,512]{2,1,0:T(8,128)(2,1)S(1)} copy-done((bf16[16,144,512]{2,1,0:T(8,128)(2,1)S(1)}, bf16[16,144,512]{2,1,0:T(8,128)(2,1)}, u32[]{:S(2)}) %copy-start.4) | copy-done | bytes 2359320
  67.5 1.5 row_stats.1
  69.0 9.9 %all_to_all.25.stats = f32[4,104,128]{2,1,0:T(8,128)S(1)} all-to-all(f32[4,104,128]{2,1,0:T(8,128)S(1)} %get-tuple-element.18), channel_id=1, replica_groups={{0,2,4,6},{8,10,12,14},{16,18,20,22},{24,26,28,30},{1,3,5,7},{9,11,13,1..., dimensions={0} | all-to-all | bytes 425984 | tf_op jit(solution)/shard_map/all_to_all | solution.py:273
  79.0 15.0 %all_to_all.26.stats = f32[4,104,128]{2,1,0:T(8,128)S(1)} all-to-all(f32[4,104,128]{2,1,0:T(8,128)S(1)} %merge_stats.1), channel_id=1, replica_groups={{0,8,16,24},{2,10,18,26},{4,12,20,28},{6,14,22,30},{1,9,17,25},{3,11,19..., dimensions={0} | all-to-all | bytes 425984 | tf_op jit(solution)/shard_map/all_to_all | solution.py:282
  94.0 1.7 %key_value_grads.1 = (bf16[16,128,512]{2,1,0:T(8,128)(2,1)S(1)}, f32[8,128]{1,0:T(8,128)S(1)}, f32[32,1,128]{2,1,0:T(1,128)S(1)}, f32[32,1,128]{2,1,0:T(1,128)S(1)}) custom-call(s32[3,40]{1,0:T(4,128)S(1)} %pair_lists.1.lists, bf16[16,128,512]{2,1,0:T(8,128)(2,1)S(1)} %bitcast.19, f32[4,104,128]{2,1,0:T(8,128)S(1)} %all_to_all.26.stats, ...), custom_call_target="tpu_custom_call" | custom-call | tf_op jit(solution)/shard_map/key_value_grads/pallas_call | solution.py:283
  95.8 1.4 copy-done.6
  97.1 2.2 %copy-done.1 = f32[2,32,128,128]{3,2,1,0:T(8,128)S(1)} copy-done((f32[2,32,128,128]{3,2,1,0:T(8,128)S(1)}, f32[2,32,128,128]{3,2,1,0:T(8,128)}, u32[]{:S(2)}) %copy-start.1) | copy-done | bytes 4194328
  99.3 2.2 %copy-done.3 = f32[2,32,128,128]{3,2,1,0:T(8,128)S(1)} copy-done((f32[2,32,128,128]{3,2,1,0:T(8,128)S(1)}, f32[2,32,128,128]{3,2,1,0:T(8,128)}, u32[]{:S(2)}) %copy-start.3) | copy-done | bytes 4194328
  101.5 1.7 %copy-done.5 = bf16[16,144,512]{2,1,0:T(8,128)(2,1)S(1)} copy-done((bf16[16,144,512]{2,1,0:T(8,128)(2,1)S(1)}, bf16[16,144,512]{2,1,0:T(8,128)(2,1)}, u32[]{:S(2)}) %copy-start.5) | copy-done | bytes 2359320
  103.2 1.4 query_grads.1
  104.6 16.8 %all_to_all.27 = bf16[4,4,128,256]{3,2,1,0:T(8,128)(2,1)S(1)} all-to-all(bf16[4,4,128,256]{3,2,1,0:T(8,128)(2,1)S(1)} %bitcast.20), channel_id=1, replica_groups={{0,2,4,6},{8,10,12,14},{16,18,20,22},{24,26,28,30},{1,3,5,7},{9,11,13,1..., dimensions={0} | all-to-all | bytes 2097152 | tf_op jit(solution)/shard_map/all_to_all | solution.py:317
  121.4 0.9 reduce_sum.21
  122.3 3.4 %all-to-all-start.4 = ((bf16[4,128,256]{2,1,0:T(8,128)(2,1)}), bf16[4,128,256]{2,1,0:T(8,128)(2,1)S(1)}, u32[]{:S(2)}, u32[]{:S(2)}) async-start(bf16[4,128,256]{2,1,0:T(8,128)(2,1)} %reduce_sum.21), calls=%async_computation.4 | async-start | bytes 524288 | tf_op jit(solution)/shard_map/all_to_all | solution.py:319
  125.8 1.9 %collective-permute-start = (f32[8,128]{1,0:T(8,128)S(1)}, f32[8,128]{1,0:T(8,128)S(1)}, u32[]{:S(2)}, u32[]{:S(2)}) collective-permute-start(f32[8,128]{1,0:T(8,128)S(1)} %get-tuple-element.21), channel_id=1, source_target_pairs={{0,1},{1,0},{2,3},{3,2},{4,5},{5,4},{6,7},{7,6},{8,9},{9,8},{10,11... | collective-permute-start | bytes 12296 | tf_op jit(solution)/shard_map/ppermute | solution.py:309
  127.7 0.5 slice.31
  128.2 0.6 collective-permute-done
  128.8 0.5 slice.30
  132.0 2.8 %all-to-all-done.4 = bf16[4,128,256]{2,1,0:T(8,128)(2,1)S(1)} async-done(((bf16[4,128,256]{2,1,0:T(8,128)(2,1)}), bf16[4,128,256]{2,1,0:T(8,128)(2,1)S(1)}, u32[]{:S(2)}, u32[]{:S(2)}) %all-to-all-start.4) | async-done | bytes 262176 | tf_op jit(solution)/shard_map/all_to_all | solution.py:319
  134.8 4.9 %reduce-scatter.2.cloned.1.call-done = bf16[1,256,512]{2,1,0:T(8,128)(2,1)} async-done(((bf16[8,256,512]{2,1,0:T(8,128)(2,1)}), bf16[1,256,512]{2,1,0:T(8,128)(2,1)}) %reduce-scatter.2.cloned.1.call-update) | async-done | bytes 262160 | tf_op jit(solution)/shard_map/reduce_scatter | solution.py:297
  139.7 1.0 slice_bitcast_fusion.1
  140.7 3.4 %collective-permute-start.1 = (bf16[128,512]{1,0:T(8,128)(2,1)S(1)}, bf16[128,512]{1,0:T(8,128)(2,1)S(1)}, u32[]{:S(2)}, u32[]{:S(2)}) collective-permute-start(bf16[128,512]{1,0:T(8,128)(2,1)S(1)} %get-tuple-element.26), channel_id=1, source_target_pairs={{0,256},{32,288},{64,320},{96,352},{128,384},{160,416},{192,448},{... | collective-permute-start | bytes 393224 | tf_op jit(solution)/shard_map/ppermute | solution.py:324
  144.1 0.6 fusion
  144.7 2.8 %collective-permute-done.1 = bf16[128,512]{1,0:T(8,128)(2,1)S(1)} collective-permute-done((bf16[128,512]{1,0:T(8,128)(2,1)S(1)}, bf16[128,512]{1,0:T(8,128)(2,1)S(1)}, u32[]{:S(2)}, u32[]{:S(2)}) %collective-permute-start.1) | collective-permute-done | bytes 131104 | tf_op jit(solution)/shard_map/ppermute | solution.py:324
  147.5 0.7 fusion.2
  (17 shorter events, 0.2 us)
Async XLA Ops:
  7.2 58.7 %all-gather.5.cloned.1.call-start = ((), (), s32[]{:S(2)}) async-start(), calls=%async_computation.7 | async-start | bytes 2654208 | tf_op jit(solution)/shard_map/all_gather | solution.py:250
  37.3 4.9 %copy-start.7 = (s32[2,16,16]{2,1,0:T(8,128)S(1)}, s32[2,16,16]{2,1,0:T(8,128)}, u32[]{:S(2)}) copy-start(s32[2,16,16]{2,1,0:T(8,128)} %mask.1) | copy-start | bytes 6148
  37.3 24.1 %all-to-all-start = ((bf16[4,4,128,512]{3,2,1,0:T(8,128)(2,1)}), bf16[4,4,128,512]{3,2,1,0:T(8,128)(2,1)S(1)}, u32[]{:S(2)}, u32[]{:S(2)}) async-start(bf16[4,4,128,512]{3,2,1,0:T(8,128)(2,1)} %broadcast_in_dim.2), calls=%async_computation | async-start | bytes 4194304 | tf_op jit(solution)/shard_map/all_to_all | solution.py:252
  42.2 97.5 %reduce-scatter.2.cloned.1.call-start = ((), (), s32[]{:S(2)}) async-start(), calls=%async_computation.6 | async-start | bytes 2359296 | tf_op jit(solution)/shard_map/reduce_scatter | solution.py:297
  65.8 1.7 %copy-start.4 = (bf16[16,144,512]{2,1,0:T(8,128)(2,1)S(1)}, bf16[16,144,512]{2,1,0:T(8,128)(2,1)}, u32[]{:S(2)}) copy-start(bf16[16,144,512]{2,1,0:T(8,128)(2,1)} %all-gather.5.cloned.1.call-done.kv) | copy-start | bytes 7077892
  69.0 26.7 %copy-start = (f32[2,32,128,128]{3,2,1,0:T(8,128)}, f32[2,32,128,128]{3,2,1,0:T(8,128)S(1)}, u32[]{:S(2)}) copy-start(f32[2,32,128,128]{3,2,1,0:T(8,128)S(1)} %get-tuple-element.15.shifted) | copy-start | bytes 12582916
  69.0 26.7 %copy-start.2 = (f32[2,32,128,128]{3,2,1,0:T(8,128)}, f32[2,32,128,128]{3,2,1,0:T(8,128)S(1)}, u32[]{:S(2)}) copy-start(f32[2,32,128,128]{3,2,1,0:T(8,128)S(1)} %get-tuple-element.16.grad_scores) | copy-start | bytes 12582916
  95.7 1.4 copy-start.6
  97.1 2.2 %copy-start.1 = (f32[2,32,128,128]{3,2,1,0:T(8,128)S(1)}, f32[2,32,128,128]{3,2,1,0:T(8,128)}, u32[]{:S(2)}) copy-start(f32[2,32,128,128]{3,2,1,0:T(8,128)} %copy-done) | copy-start | bytes 12582916
  99.3 2.2 %copy-start.3 = (f32[2,32,128,128]{3,2,1,0:T(8,128)S(1)}, f32[2,32,128,128]{3,2,1,0:T(8,128)}, u32[]{:S(2)}) copy-start(f32[2,32,128,128]{3,2,1,0:T(8,128)} %copy-done.2) | copy-start | bytes 12582916
  101.5 1.7 %copy-start.5 = (bf16[16,144,512]{2,1,0:T(8,128)(2,1)S(1)}, bf16[16,144,512]{2,1,0:T(8,128)(2,1)}, u32[]{:S(2)}) copy-start(bf16[16,144,512]{2,1,0:T(8,128)(2,1)} %all-gather.5.cloned.1.call-done.kv) | copy-start | bytes 7077892
  122.3 12.5 %all-to-all-start.4 = ((bf16[4,128,256]{2,1,0:T(8,128)(2,1)}), bf16[4,128,256]{2,1,0:T(8,128)(2,1)S(1)}, u32[]{:S(2)}, u32[]{:S(2)}) async-start(bf16[4,128,256]{2,1,0:T(8,128)(2,1)} %reduce_sum.21), calls=%async_computation.4 | async-start | bytes 524288 | tf_op jit(solution)/shard_map/all_to_all | solution.py:319
  125.8 3.1 %collective-permute-start = (f32[8,128]{1,0:T(8,128)S(1)}, f32[8,128]{1,0:T(8,128)S(1)}, u32[]{:S(2)}, u32[]{:S(2)}) collective-permute-start(f32[8,128]{1,0:T(8,128)S(1)} %get-tuple-element.21), channel_id=1, source_target_pairs={{0,1},{1,0},{2,3},{3,2},{4,5},{5,4},{6,7},{7,6},{8,9},{9,8},{10,11... | collective-permute-start | bytes 12296 | tf_op jit(solution)/shard_map/ppermute | solution.py:309
  140.7 6.9 %collective-permute-start.1 = (bf16[128,512]{1,0:T(8,128)(2,1)S(1)}, bf16[128,512]{1,0:T(8,128)(2,1)S(1)}, u32[]{:S(2)}, u32[]{:S(2)}) collective-permute-start(bf16[128,512]{1,0:T(8,128)(2,1)S(1)} %get-tuple-element.26), channel_id=1, source_target_pairs={{0,256},{32,288},{64,320},{96,352},{128,384},{160,416},{192,448},{... | collective-permute-start | bytes 393224 | tf_op jit(solution)/shard_map/ppermute | solution.py:324
Sparse Core Ops, SparseCore 0:
  17.0 48.7 all-gather.4
  97.3 42.3 reduce-scatter.1

commit v7 on v6

--- a/solution.py
+++ b/solution.py
@@ -52,6 +52,14 @@
     kv_ref[:BLK, :WIDE] = keys[0]
     kv_ref[:BLK, WIDE:] = values[0]
     kv_ref[BLK:, :] = sums.astype(jnp.bfloat16)
+
+
+def copies_kernel(source, target, sems):
+    copies = [pltpu.make_async_copy(source, target.at[at], sems.at[at]) for at in range(4)]
+    for copy in copies:
+        copy.start()
+    for copy in copies:
+        copy.wait()
 
 
 def list_kernel(mask, side, lists):
@@ -249,9 +257,16 @@
     kv = lax.all_gather(kv, "qb", axis_index_groups=Y_PAIRS)
     kv = lax.all_gather(kv, "qb", axis_index_groups=Z_GROUPS).reshape(GB, ROWS, 2 * WIDE)
     qg = lax.all_gather(qg, "kb", axis_index_groups=Y_GROUPS)
-    qg = lax.all_to_all(
-        jnp.broadcast_to(qg[None], (4, 4, BLK, 2 * WIDE)), "kb", 0, 0, axis_index_groups=X_GROUPS
-    ).reshape(GB, BLK, 2 * WIDE)
+    qg = pl.pallas_call(
+        copies_kernel,
+        out_shape=shape(4, 4, BLK, 2 * WIDE),
+        in_specs=[VMEM],
+        out_specs=pl.BlockSpec(memory_space=pl.ANY),
+        scratch_shapes=[pltpu.SemaphoreType.DMA((4,))],
+        compiler_params=params(4),
+        name="four_copies",
+    )(qg)
+    qg = lax.all_to_all(qg, "kb", 0, 0, axis_index_groups=X_GROUPS).reshape(GB, BLK, 2 * WIDE)
 
     row_scratch = pltpu.VMEM((SLOTS, 1, DH), jnp.float32)
     block_scratch = pltpu.VMEM((SLOTS, BLK, DH), jnp.float32)

time: 156 us -> 155 us (level)
    unnamed x16 -> x18, local copies, waits for them, and re-layouts: 9.07 us -> 10.4 us
  transfers between devices with their start and end apart: 6 -> 6, of which waited for: 6 -> 6; matrix products, arithmetic and copies ran while one was open for 3% -> 2% of each run, Pallas kernels for 3% -> 3%
where the time goes in v7:
time: 155 us; the launch traced here: 154 us
  blocking collectives  68.5 us (44%)
  waiting for transfers between devices  30.8 us (20%)
  between operations  16.9 us (11%)
  starting transfers between devices  13.7 us (9%)
  local copies, waits for them, and re-layouts  12.4 us (8%)
  Pallas kernels  9.62 us (6%)
  other arithmetic  2.26 us (1%)
    all_gather x1, blocking collectives, body(): qg = lax.all_gather(qg, 'kb', axis_index_groups=Y_GROUPS)  18.9 us
    all_to_all x1, blocking collectives, body(): lax.all_to_all(qpart.reshape(4, 4, BLK, WIDE), 'kb', 0, 0, axis_index_gro...  16.8 us
    all_to_all x1, waiting for transfers between devices, body(): lax.all_to_all(qg, 'kb', 0, 0, axis_index_groups=X_GROUPS)  16.2 us
    all_to_all x1, blocking collectives, body(): stats = lax.all_to_all(stats, 'kb', 0, 0, axis_index_groups=Y_GROUPS)  15 us
    unnamed x18, local copies, waits for them, and re-layouts  10.4 us
    all_to_all x1, blocking collectives, body(): stats = lax.all_to_all(stats, 'kb', 0, 0, axis_index_groups=X_GROUPS)  9.93 us
    all_gather x1, blocking collectives, body(): kv = lax.all_gather(kv, 'qb', axis_index_groups=Y_PAIRS)  7.94 us
    all_to_all x1, starting transfers between devices, body(): lax.all_to_all(qg, 'kb', 0, 0, axis_index_groups=X_GROUPS)  4.9 us
  transfers between devices with their start and end apart: 6, of which 6 were waited for; matrix products, arithmetic and copies ran while one was open for 2% of the time, Pallas kernels for 3%

profile of v7, /device:TPU:6, one launch (start us, length us, event | category | flops | bytes accessed | tf_op | source)
XLA Modules:
  0.0 154.2 jit_solution(3249408799669236052)
XLA Ops:
  7.2 1.7 %pack.1 = (bf16[128,512]{1,0:T(8,128)(2,1)}, bf16[144,512]{1,0:T(8,128)(2,1)}) custom-call(bf16[1,128,256]{2,1,0:T(8,128)(2,1)} %queries.1, bf16[1,128,256]{2,1,0:T(8,128)(2,1)} %keys.1, bf16[1,128,256]{2,1,0:T(8,128)(2,1)} %values.1, bf16[1,128,256]{2,1,0:T(8,128)(2,1)} %out_grad.1, f32[1,128]{1,0:T(1,128)} %token_error.1), custom_call_target="tpu_custom_call" | custom-call | tf_op jit(solution)/shard_map/pack/pallas_call | solution.py:242
  8.9 7.9 %all-gather = bf16[288,512]{1,0:T(8,128)(2,1)} all-gather(bf16[144,512]{1,0:T(8,128)(2,1)} %get-tuple-element.13), channel_id=2, replica_groups={{0,256},{32,288},{64,320},{96,352},{128,384},{160,416},{192,448},{224,4..., dimensions={0}, use_global_device_ids=true | all-gather | bytes 442368 | tf_op jit(solution)/shard_map/all_gather | solution.py:257
  16.9 18.9 %all-gather.2 = bf16[512,512]{1,0:T(8,128)(2,1)S(1)} all-gather(bf16[128,512]{1,0:T(8,128)(2,1)} %get-tuple-element.14), channel_id=4, replica_groups={{0,8,16,24},{2,10,18,26},{4,12,20,28},{6,14,22,30},{1,9,17,25},{3,11,19..., dimensions={0}, use_global_device_ids=true | all-gather | bytes 655360 | tf_op jit(solution)/shard_map/all_gather | solution.py:259
  36.0 1.3 copy-done.6
  37.3 4.9 %all-to-all-start = ((bf16[4,4,128,512]{3,2,1,0:T(8,128)(2,1)}), bf16[4,4,128,512]{3,2,1,0:T(8,128)(2,1)S(1)}, u32[]{:S(2)}, u32[]{:S(2)}) async-start(bf16[4,4,128,512]{3,2,1,0:T(8,128)(2,1)} %copy-done.6), calls=%async_computation | async-start | bytes 4194304 | tf_op jit(solution)/shard_map/all_to_all | solution.py:269
  42.2 3.0 %pair_lists.1.lists = s32[3,40]{1,0:T(4,128)S(1)} custom-call(s32[2,16,16]{2,1,0:T(8,128)S(1)} %copy-done.8, s32[1]{0:T(128)} %bitcast.side), custom_call_target="tpu_custom_call" | custom-call | tf_op jit(solution)/shard_map/pair_lists/pallas_call | solution.py:249
  45.2 16.2 %all-to-all-done = bf16[4,4,128,512]{3,2,1,0:T(8,128)(2,1)S(1)} async-done(((bf16[4,4,128,512]{3,2,1,0:T(8,128)(2,1)}), bf16[4,4,128,512]{3,2,1,0:T(8,128)(2,1)S(1)}, u32[]{:S(2)}, u32[]{:S(2)}) %all-to-all-start) | async-done | bytes 2097184 | tf_op jit(solution)/shard_map/all_to_all | solution.py:269
  61.4 4.4 %all-gather.5.cloned.1.call-done.kv = bf16[16,144,512]{2,1,0:T(8,128)(2,1)} async-done(((bf16[2,144,512]{2,1,0:T(8,128)(2,1)}), bf16[16,144,512]{2,1,0:T(8,128)(2,1)}) %all-gather.5.cloned.1.call-update) | async-done | bytes 2359312 | tf_op jit(solution)/shard_map/all_gather | solution.py:258
  65.8 1.7 %copy-done.4 = bf16[16,144,512]{2,1,0:T(8,128)(2,1)S(1)} copy-done((bf16[16,144,512]{2,1,0:T(8,128)(2,1)S(1)}, bf16[16,144,512]{2,1,0:T(8,128)(2,1)}, u32[]{:S(2)}) %copy-start.4) | copy-done | bytes 2359320
  67.5 1.5 row_stats.1
  69.1 9.9 %all_to_all.25.stats = f32[4,104,128]{2,1,0:T(8,128)S(1)} all-to-all(f32[4,104,128]{2,1,0:T(8,128)S(1)} %get-tuple-element.18), channel_id=1, replica_groups={{0,2,4,6},{8,10,12,14},{16,18,20,22},{24,26,28,30},{1,3,5,7},{9,11,13,1..., dimensions={0} | all-to-all | bytes 425984 | tf_op jit(solution)/shard_map/all_to_all | solution.py:288
  79.0 15.0 %all_to_all.26.stats = f32[4,104,128]{2,1,0:T(8,128)S(1)} all-to-all(f32[4,104,128]{2,1,0:T(8,128)S(1)} %merge_stats.1), channel_id=1, replica_groups={{0,8,16,24},{2,10,18,26},{4,12,20,28},{6,14,22,30},{1,9,17,25},{3,11,19..., dimensions={0} | all-to-all | bytes 425984 | tf_op jit(solution)/shard_map/all_to_all | solution.py:297
  94.0 1.7 %key_value_grads.1 = (bf16[16,128,512]{2,1,0:T(8,128)(2,1)S(1)}, f32[8,128]{1,0:T(8,128)S(1)}, f32[32,1,128]{2,1,0:T(1,128)S(1)}, f32[32,1,128]{2,1,0:T(1,128)S(1)}) custom-call(s32[3,40]{1,0:T(4,128)S(1)} %pair_lists.1.lists, bf16[16,128,512]{2,1,0:T(8,128)(2,1)S(1)} %bitcast.19, f32[4,104,128]{2,1,0:T(8,128)S(1)} %all_to_all.26.stats, ...), custom_call_target="tpu_custom_call" | custom-call | tf_op jit(solution)/shard_map/key_value_grads/pallas_call | solution.py:298
  95.8 1.4 copy-done.7
  97.1 2.2 %copy-done.1 = f32[2,32,128,128]{3,2,1,0:T(8,128)S(1)} copy-done((f32[2,32,128,128]{3,2,1,0:T(8,128)S(1)}, f32[2,32,128,128]{3,2,1,0:T(8,128)}, u32[]{:S(2)}) %copy-start.1) | copy-done | bytes 4194328
  99.3 2.2 %copy-done.3 = f32[2,32,128,128]{3,2,1,0:T(8,128)S(1)} copy-done((f32[2,32,128,128]{3,2,1,0:T(8,128)S(1)}, f32[2,32,128,128]{3,2,1,0:T(8,128)}, u32[]{:S(2)}) %copy-start.3) | copy-done | bytes 4194328
  101.5 1.7 %copy-done.5 = bf16[16,144,512]{2,1,0:T(8,128)(2,1)S(1)} copy-done((bf16[16,144,512]{2,1,0:T(8,128)(2,1)S(1)}, bf16[16,144,512]{2,1,0:T(8,128)(2,1)}, u32[]{:S(2)}) %copy-start.5) | copy-done | bytes 2359320
  103.2 1.4 query_grads.1
  104.6 16.8 %all_to_all.27 = bf16[4,4,128,256]{3,2,1,0:T(8,128)(2,1)S(1)} all-to-all(bf16[4,4,128,256]{3,2,1,0:T(8,128)(2,1)S(1)} %bitcast.20), channel_id=1, replica_groups={{0,2,4,6},{8,10,12,14},{16,18,20,22},{24,26,28,30},{1,3,5,7},{9,11,13,1..., dimensions={0} | all-to-all | bytes 2097152 | tf_op jit(solution)/shard_map/all_to_all | solution.py:332
  121.5 0.9 reduce_sum.21
  122.3 3.4 %all-to-all-start.4 = ((bf16[4,128,256]{2,1,0:T(8,128)(2,1)}), bf16[4,128,256]{2,1,0:T(8,128)(2,1)S(1)}, u32[]{:S(2)}, u32[]{:S(2)}) async-start(bf16[4,128,256]{2,1,0:T(8,128)(2,1)} %reduce_sum.21), calls=%async_computation.4 | async-start | bytes 524288 | tf_op jit(solution)/shard_map/all_to_all | solution.py:334
  125.8 1.9 %collective-permute-start = (f32[8,128]{1,0:T(8,128)S(1)}, f32[8,128]{1,0:T(8,128)S(1)}, u32[]{:S(2)}, u32[]{:S(2)}) collective-permute-start(f32[8,128]{1,0:T(8,128)S(1)} %get-tuple-element.21), channel_id=1, source_target_pairs={{0,1},{1,0},{2,3},{3,2},{4,5},{5,4},{6,7},{7,6},{8,9},{9,8},{10,11... | collective-permute-start | bytes 12296 | tf_op jit(solution)/shard_map/ppermute | solution.py:324
  127.7 0.5 slice.31
  128.2 0.6 collective-permute-done
  128.8 0.5 slice.30
  132.0 2.8 %all-to-all-done.4 = bf16[4,128,256]{2,1,0:T(8,128)(2,1)S(1)} async-done(((bf16[4,128,256]{2,1,0:T(8,128)(2,1)}), bf16[4,128,256]{2,1,0:T(8,128)(2,1)S(1)}, u32[]{:S(2)}, u32[]{:S(2)}) %all-to-all-start.4) | async-done | bytes 262176 | tf_op jit(solution)/shard_map/all_to_all | solution.py:334
  134.8 4.0 %reduce-scatter.2.cloned.1.call-done = bf16[1,256,512]{2,1,0:T(8,128)(2,1)} async-done(((bf16[8,256,512]{2,1,0:T(8,128)(2,1)}), bf16[1,256,512]{2,1,0:T(8,128)(2,1)}) %reduce-scatter.2.cloned.1.call-update) | async-done | bytes 262160 | tf_op jit(solution)/shard_map/reduce_scatter | solution.py:312
  138.8 1.0 slice_bitcast_fusion.1
  139.8 3.5 %collective-permute-start.1 = (bf16[128,512]{1,0:T(8,128)(2,1)S(1)}, bf16[128,512]{1,0:T(8,128)(2,1)S(1)}, u32[]{:S(2)}, u32[]{:S(2)}) collective-permute-start(bf16[128,512]{1,0:T(8,128)(2,1)S(1)} %get-tuple-element.26), channel_id=1, source_target_pairs={{0,256},{32,288},{64,320},{96,352},{128,384},{160,416},{192,448},{... | collective-permute-start | bytes 393224 | tf_op jit(solution)/shard_map/ppermute | solution.py:339
  143.3 0.6 fusion
  144.0 2.7 %collective-permute-done.1 = bf16[128,512]{1,0:T(8,128)(2,1)S(1)} collective-permute-done((bf16[128,512]{1,0:T(8,128)(2,1)S(1)}, bf16[128,512]{1,0:T(8,128)(2,1)S(1)}, u32[]{:S(2)}, u32[]{:S(2)}) %collective-permute-start.1) | collective-permute-done | bytes 131104 | tf_op jit(solution)/shard_map/ppermute | solution.py:339
  146.7 0.7 fusion.2
  (19 shorter events, 0.3 us)
Async XLA Ops:
  7.2 58.7 %all-gather.5.cloned.1.call-start = ((), (), s32[]{:S(2)}) async-start(), calls=%async_computation.7 | async-start | bytes 2654208 | tf_op jit(solution)/shard_map/all_gather | solution.py:258
  35.9 1.3 copy-start.6
  37.3 4.9 %copy-start.8 = (s32[2,16,16]{2,1,0:T(8,128)S(1)}, s32[2,16,16]{2,1,0:T(8,128)}, u32[]{:S(2)}) copy-start(s32[2,16,16]{2,1,0:T(8,128)} %mask.1) | copy-start | bytes 6148
  37.3 24.1 %all-to-all-start = ((bf16[4,4,128,512]{3,2,1,0:T(8,128)(2,1)}), bf16[4,4,128,512]{3,2,1,0:T(8,128)(2,1)S(1)}, u32[]{:S(2)}, u32[]{:S(2)}) async-start(bf16[4,4,128,512]{3,2,1,0:T(8,128)(2,1)} %copy-done.6), calls=%async_computation | async-start | bytes 4194304 | tf_op jit(solution)/shard_map/all_to_all | solution.py:269
  42.2 96.6 %reduce-scatter.2.cloned.1.call-start = ((), (), s32[]{:S(2)}) async-start(), calls=%async_computation.6 | async-start | bytes 2359296 | tf_op jit(solution)/shard_map/reduce_scatter | solution.py:312
  65.8 1.7 %copy-start.4 = (bf16[16,144,512]{2,1,0:T(8,128)(2,1)S(1)}, bf16[16,144,512]{2,1,0:T(8,128)(2,1)}, u32[]{:S(2)}) copy-start(bf16[16,144,512]{2,1,0:T(8,128)(2,1)} %all-gather.5.cloned.1.call-done.kv) | copy-start | bytes 7077892
  69.0 26.7 %copy-start = (f32[2,32,128,128]{3,2,1,0:T(8,128)}, f32[2,32,128,128]{3,2,1,0:T(8,128)S(1)}, u32[]{:S(2)}) copy-start(f32[2,32,128,128]{3,2,1,0:T(8,128)S(1)} %get-tuple-element.15.shifted) | copy-start | bytes 12582916
  69.0 26.7 %copy-start.2 = (f32[2,32,128,128]{3,2,1,0:T(8,128)}, f32[2,32,128,128]{3,2,1,0:T(8,128)S(1)}, u32[]{:S(2)}) copy-start(f32[2,32,128,128]{3,2,1,0:T(8,128)S(1)} %get-tuple-element.16.grad_scores) | copy-start | bytes 12582916
  95.7 1.4 copy-start.7
  97.1 2.2 %copy-start.1 = (f32[2,32,128,128]{3,2,1,0:T(8,128)S(1)}, f32[2,32,128,128]{3,2,1,0:T(8,128)}, u32[]{:S(2)}) copy-start(f32[2,32,128,128]{3,2,1,0:T(8,128)} %copy-done) | copy-start | bytes 12582916
  99.3 2.2 %copy-start.3 = (f32[2,32,128,128]{3,2,1,0:T(8,128)S(1)}, f32[2,32,128,128]{3,2,1,0:T(8,128)}, u32[]{:S(2)}) copy-start(f32[2,32,128,128]{3,2,1,0:T(8,128)} %copy-done.2) | copy-start | bytes 12582916
  101.5 1.7 %copy-start.5 = (bf16[16,144,512]{2,1,0:T(8,128)(2,1)S(1)}, bf16[16,144,512]{2,1,0:T(8,128)(2,1)}, u32[]{:S(2)}) copy-start(bf16[16,144,512]{2,1,0:T(8,128)(2,1)} %all-gather.5.cloned.1.call-done.kv) | copy-start | bytes 7077892
  122.3 12.5 %all-to-all-start.4 = ((bf16[4,128,256]{2,1,0:T(8,128)(2,1)}), bf16[4,128,256]{2,1,0:T(8,128)(2,1)S(1)}, u32[]{:S(2)}, u32[]{:S(2)}) async-start(bf16[4,128,256]{2,1,0:T(8,128)(2,1)} %reduce_sum.21), calls=%async_computation.4 | async-start | bytes 524288 | tf_op jit(solution)/shard_map/all_to_all | solution.py:334
  125.8 3.1 %collective-permute-start = (f32[8,128]{1,0:T(8,128)S(1)}, f32[8,128]{1,0:T(8,128)S(1)}, u32[]{:S(2)}, u32[]{:S(2)}) collective-permute-start(f32[8,128]{1,0:T(8,128)S(1)} %get-tuple-element.21), channel_id=1, source_target_pairs={{0,1},{1,0},{2,3},{3,2},{4,5},{5,4},{6,7},{7,6},{8,9},{9,8},{10,11... | collective-permute-start | bytes 12296 | tf_op jit(solution)/shard_map/ppermute | solution.py:324
  139.8 6.9 %collective-permute-start.1 = (bf16[128,512]{1,0:T(8,128)(2,1)S(1)}, bf16[128,512]{1,0:T(8,128)(2,1)S(1)}, u32[]{:S(2)}, u32[]{:S(2)}) collective-permute-start(bf16[128,512]{1,0:T(8,128)(2,1)S(1)} %get-tuple-element.26), channel_id=1, source_target_pairs={{0,256},{32,288},{64,320},{96,352},{128,384},{160,416},{192,448},{... | collective-permute-start | bytes 393224 | tf_op jit(solution)/shard_map/ppermute | solution.py:339
Sparse Core Ops, SparseCore 0:
  17.0 48.7 all-gather.4
  97.3 41.5 reduce-scatter.1

commit v8 on v7

--- a/solution.py
+++ b/solution.py
@@ -166,7 +166,7 @@
 
 
 def key_kernel(
-    lists, qg, stats, shifted, grad_scores, own_tops, kvout, latent, shift, delta, kacc, vacc
+    lists, qg, stats, shifted, grad_scores, own_tops, spare, kvout, latent, shift, delta, kacc, vacc
 ):
     tops = stats[0, :SLOTS]
     for part in range(1, 4):
@@ -266,6 +266,7 @@
         compiler_params=params(4),
         name="four_copies",
     )(qg)
+    spare = qg.reshape(GB, BLK, 2 * WIDE)
     qg = lax.all_to_all(qg, "kb", 0, 0, axis_index_groups=X_GROUPS).reshape(GB, BLK, 2 * WIDE)
 
     row_scratch = pltpu.VMEM((SLOTS, 1, DH), jnp.float32)
@@ -303,12 +304,13 @@
             shape(SLOTS, 1, DH, dtype=jnp.float32),
             shape(SLOTS, 1, DH, dtype=jnp.float32),
         ),
-        in_specs=[SMEM] + [VMEM] * 5,
+        in_specs=[SMEM] + [VMEM] * 5 + [pl.BlockSpec(memory_space=pl.ANY)],
+        input_output_aliases={6: 0},
         out_specs=(VMEM,) * 4,
         scratch_shapes=[block_scratch, block_scratch],
         compiler_params=params(28),
         name="key_value_grads",
-    )(lists, qg, stats, shifted, grad_scores, tops)
+    )(lists, qg, stats, shifted, grad_scores, tops, spare)
     kvpart = lax.psum_scatter(
         kvpart.reshape(8, 2 * BLK, 2 * WIDE), "qb", scatter_dimension=0, axis_index_groups=Z_GROUPS
     )

time: 155 us -> 155 us (level)
  local copies, waits for them, and re-layouts: 12.4 us -> 9.72 us
  Pallas kernels: 9.62 us -> 12.1 us
    unnamed x18 -> x14, local copies, waits for them, and re-layouts: 10.4 us -> 7.71 us
  transfers between devices with their start and end apart: 6 -> 6, of which waited for: 6 -> 6; matrix products, arithmetic and copies ran while one was open for 2% -> 2% of each run, Pallas kernels for 3% -> 4%
where the time goes in v8:
time: 155 us; the launch traced here: 154 us
  blocking collectives  68.6 us (44%)
  waiting for transfers between devices  31 us (20%)
  between operations  16.8 us (11%)
  starting transfers between devices  13.4 us (9%)
  Pallas kernels  12.1 us (8%)
  local copies, waits for them, and re-layouts  9.72 us (6%)
  other arithmetic  2.27 us (1%)
    all_gather x1, blocking collectives, body(): qg = lax.all_gather(qg, 'kb', axis_index_groups=Y_GROUPS)  18.9 us
    all_to_all x1, blocking collectives, body(): lax.all_to_all(qpart.reshape(4, 4, BLK, WIDE), 'kb', 0, 0, axis_index_gro...  16.8 us
    all_to_all x1, waiting for transfers between devices, body(): lax.all_to_all(qg, 'kb', 0, 0, axis_index_groups=X_GROUPS)  16.2 us
    all_to_all x1, blocking collectives, body(): stats = lax.all_to_all(stats, 'kb', 0, 0, axis_index_groups=Y_GROUPS)  15 us
    all_to_all x1, blocking collectives, body(): stats = lax.all_to_all(stats, 'kb', 0, 0, axis_index_groups=X_GROUPS)  9.94 us
    all_gather x1, blocking collectives, body(): kv = lax.all_gather(kv, 'qb', axis_index_groups=Y_PAIRS)  7.93 us
    unnamed x14, local copies, waits for them, and re-layouts  7.71 us
    all_to_all x1, starting transfers between devices, body(): lax.all_to_all(qg, 'kb', 0, 0, axis_index_groups=X_GROUPS)  4.78 us
  transfers between devices with their start and end apart: 6, of which 6 were waited for; matrix products, arithmetic and copies ran while one was open for 2% of the time, Pallas kernels for 4%

profile of v8, /device:TPU:6, one launch (start us, length us, event | category | flops | bytes accessed | tf_op | source)
XLA Modules:
  0.0 153.9 jit_solution(17795474238546758132)
XLA Ops:
  7.2 0.0 all-gather.5.cloned.1.call-start
  7.2 1.7 %pack.1 = (bf16[128,512]{1,0:T(8,128)(2,1)}, bf16[144,512]{1,0:T(8,128)(2,1)}) custom-call(bf16[1,128,256]{2,1,0:T(8,128)(2,1)} %queries.1, bf16[1,128,256]{2,1,0:T(8,128)(2,1)} %keys.1, bf16[1,128,256]{2,1,0:T(8,128)(2,1)} %values.1, bf16[1,128,256]{2,1,0:T(8,128)(2,1)} %out_grad.1, f32[1,128]{1,0:T(1,128)} %token_error.1), custom_call_target="tpu_custom_call" | custom-call | tf_op jit(solution)/shard_map/pack/pallas_call | solution.py:242
  8.9 7.9 %all-gather = bf16[288,512]{1,0:T(8,128)(2,1)} all-gather(bf16[144,512]{1,0:T(8,128)(2,1)} %get-tuple-element.13), channel_id=2, replica_groups={{0,256},{32,288},{64,320},{96,352},{128,384},{160,416},{192,448},{224,4..., dimensions={0}, use_global_device_ids=true | all-gather | bytes 442368 | tf_op jit(solution)/shard_map/all_gather | solution.py:257
  16.8 18.9 %all-gather.2 = bf16[512,512]{1,0:T(8,128)(2,1)S(1)} all-gather(bf16[128,512]{1,0:T(8,128)(2,1)} %get-tuple-element.14), channel_id=4, replica_groups={{0,8,16,24},{2,10,18,26},{4,12,20,28},{6,14,22,30},{1,9,17,25},{3,11,19..., dimensions={0}, use_global_device_ids=true | all-gather | bytes 655360 | tf_op jit(solution)/shard_map/all_gather | solution.py:259
  35.7 1.4 four_copies.1
  37.2 4.8 %all-to-all-start = ((bf16[4,4,128,512]{3,2,1,0:T(8,128)(2,1)}), bf16[4,4,128,512]{3,2,1,0:T(8,128)(2,1)S(1)}, u32[]{:S(2)}, u32[]{:S(2)}) async-start(bf16[4,4,128,512]{3,2,1,0:T(8,128)(2,1)} %four_copies.1), calls=%async_computation | async-start | bytes 4194304 | tf_op jit(solution)/shard_map/all_to_all | solution.py:270
  41.9 3.0 %pair_lists.1.lists = s32[3,40]{1,0:T(4,128)S(1)} custom-call(s32[2,16,16]{2,1,0:T(8,128)S(1)} %copy-done.6, s32[1]{0:T(128)} %bitcast.side), custom_call_target="tpu_custom_call" | custom-call | tf_op jit(solution)/shard_map/pair_lists/pallas_call | solution.py:249
  45.0 16.2 %all-to-all-done = bf16[4,4,128,512]{3,2,1,0:T(8,128)(2,1)S(1)} async-done(((bf16[4,4,128,512]{3,2,1,0:T(8,128)(2,1)}), bf16[4,4,128,512]{3,2,1,0:T(8,128)(2,1)S(1)}, u32[]{:S(2)}, u32[]{:S(2)}) %all-to-all-start) | async-done | bytes 2097184 | tf_op jit(solution)/shard_map/all_to_all | solution.py:270
  61.1 4.7 %all-gather.5.cloned.1.call-done.kv = bf16[16,144,512]{2,1,0:T(8,128)(2,1)} async-done(((bf16[2,144,512]{2,1,0:T(8,128)(2,1)}), bf16[16,144,512]{2,1,0:T(8,128)(2,1)}) %all-gather.5.cloned.1.call-update) | async-done | bytes 2359312 | tf_op jit(solution)/shard_map/all_gather | solution.py:258
  65.8 1.7 %copy-done.4 = bf16[16,144,512]{2,1,0:T(8,128)(2,1)S(1)} copy-done((bf16[16,144,512]{2,1,0:T(8,128)(2,1)S(1)}, bf16[16,144,512]{2,1,0:T(8,128)(2,1)}, u32[]{:S(2)}) %copy-start.4) | copy-done | bytes 2359320
  67.5 1.5 row_stats.1
  69.0 9.9 %all_to_all.25.stats = f32[4,104,128]{2,1,0:T(8,128)S(1)} all-to-all(f32[4,104,128]{2,1,0:T(8,128)S(1)} %get-tuple-element.18), channel_id=1, replica_groups={{0,2,4,6},{8,10,12,14},{16,18,20,22},{24,26,28,30},{1,3,5,7},{9,11,13,1..., dimensions={0} | all-to-all | bytes 425984 | tf_op jit(solution)/shard_map/all_to_all | solution.py:289
  79.0 15.0 %all_to_all.26.stats = f32[4,104,128]{2,1,0:T(8,128)S(1)} all-to-all(f32[4,104,128]{2,1,0:T(8,128)S(1)} %merge_stats.1), channel_id=1, replica_groups={{0,8,16,24},{2,10,18,26},{4,12,20,28},{6,14,22,30},{1,9,17,25},{3,11,19..., dimensions={0} | all-to-all | bytes 425984 | tf_op jit(solution)/shard_map/all_to_all | solution.py:298
  93.9 3.1 %key_value_grads.1 = (bf16[16,128,512]{2,1,0:T(8,128)(2,1)}, f32[8,128]{1,0:T(8,128)S(1)}, f32[32,1,128]{2,1,0:T(1,128)S(1)}, f32[32,1,128]{2,1,0:T(1,128)S(1)}) custom-call(s32[3,40]{1,0:T(4,128)S(1)} %pair_lists.1.lists, bf16[16,128,512]{2,1,0:T(8,128)(2,1)S(1)} %bitcast.20, f32[4,104,128]{2,1,0:T(8,128)S(1)} %all_to_all.26.stats, ...), custom_call_target="tpu_custom_call", output_to_operand_aliasing={{0}: (6, {})} | custom-call | tf_op jit(solution)/shard_map/key_value_grads/pallas_call | solution.py:299
  97.1 2.2 %copy-done.1 = f32[2,32,128,128]{3,2,1,0:T(8,128)S(1)} copy-done((f32[2,32,128,128]{3,2,1,0:T(8,128)S(1)}, f32[2,32,128,128]{3,2,1,0:T(8,128)}, u32[]{:S(2)}) %copy-start.1) | copy-done | bytes 4194328
  99.3 2.2 %copy-done.3 = f32[2,32,128,128]{3,2,1,0:T(8,128)S(1)} copy-done((f32[2,32,128,128]{3,2,1,0:T(8,128)S(1)}, f32[2,32,128,128]{3,2,1,0:T(8,128)}, u32[]{:S(2)}) %copy-start.3) | copy-done | bytes 4194328
  101.4 1.7 %copy-done.5 = bf16[16,144,512]{2,1,0:T(8,128)(2,1)S(1)} copy-done((bf16[16,144,512]{2,1,0:T(8,128)(2,1)S(1)}, bf16[16,144,512]{2,1,0:T(8,128)(2,1)}, u32[]{:S(2)}) %copy-start.5) | copy-done | bytes 2359320
  103.1 1.4 query_grads.1
  104.5 16.8 %all_to_all.27 = bf16[4,4,128,256]{3,2,1,0:T(8,128)(2,1)S(1)} all-to-all(bf16[4,4,128,256]{3,2,1,0:T(8,128)(2,1)S(1)} %bitcast.21), channel_id=1, replica_groups={{0,2,4,6},{8,10,12,14},{16,18,20,22},{24,26,28,30},{1,3,5,7},{9,11,13,1..., dimensions={0} | all-to-all | bytes 2097152 | tf_op jit(solution)/shard_map/all_to_all | solution.py:334
  121.4 0.9 reduce_sum.21
  122.3 3.4 %all-to-all-start.4 = ((bf16[4,128,256]{2,1,0:T(8,128)(2,1)}), bf16[4,128,256]{2,1,0:T(8,128)(2,1)S(1)}, u32[]{:S(2)}, u32[]{:S(2)}) async-start(bf16[4,128,256]{2,1,0:T(8,128)(2,1)} %reduce_sum.21), calls=%async_computation.4 | async-start | bytes 524288 | tf_op jit(solution)/shard_map/all_to_all | solution.py:336
  125.7 1.9 %collective-permute-start = (f32[8,128]{1,0:T(8,128)S(1)}, f32[8,128]{1,0:T(8,128)S(1)}, u32[]{:S(2)}, u32[]{:S(2)}) collective-permute-start(f32[8,128]{1,0:T(8,128)S(1)} %get-tuple-element.21), channel_id=1, source_target_pairs={{0,1},{1,0},{2,3},{3,2},{4,5},{5,4},{6,7},{7,6},{8,9},{9,8},{10,11... | collective-permute-start | bytes 12296 | tf_op jit(solution)/shard_map/ppermute | solution.py:326
  127.6 0.5 slice.31
  128.1 0.6 collective-permute-done
  128.8 0.5 slice.30
  131.9 2.8 %all-to-all-done.4 = bf16[4,128,256]{2,1,0:T(8,128)(2,1)S(1)} async-done(((bf16[4,128,256]{2,1,0:T(8,128)(2,1)}), bf16[4,128,256]{2,1,0:T(8,128)(2,1)S(1)}, u32[]{:S(2)}, u32[]{:S(2)}) %all-to-all-start.4) | async-done | bytes 262176 | tf_op jit(solution)/shard_map/all_to_all | solution.py:336
  134.8 3.8 %reduce-scatter.2.cloned.1.call-done = bf16[1,256,512]{2,1,0:T(8,128)(2,1)} async-done(((bf16[8,256,512]{2,1,0:T(8,128)(2,1)}), bf16[1,256,512]{2,1,0:T(8,128)(2,1)}) %reduce-scatter.2.cloned.1.call-update) | async-done | bytes 262160 | tf_op jit(solution)/shard_map/reduce_scatter | solution.py:314
  138.5 1.0 slice_bitcast_fusion.1
  139.5 3.3 %collective-permute-start.1 = (bf16[128,512]{1,0:T(8,128)(2,1)S(1)}, bf16[128,512]{1,0:T(8,128)(2,1)S(1)}, u32[]{:S(2)}, u32[]{:S(2)}) collective-permute-start(bf16[128,512]{1,0:T(8,128)(2,1)S(1)} %get-tuple-element.26), channel_id=1, source_target_pairs={{0,256},{32,288},{64,320},{96,352},{128,384},{160,416},{192,448},{... | collective-permute-start | bytes 393224 | tf_op jit(solution)/shard_map/ppermute | solution.py:341
  142.8 0.6 fusion
  143.5 2.9 %collective-permute-done.1 = bf16[128,512]{1,0:T(8,128)(2,1)S(1)} collective-permute-done((bf16[128,512]{1,0:T(8,128)(2,1)S(1)}, bf16[128,512]{1,0:T(8,128)(2,1)S(1)}, u32[]{:S(2)}, u32[]{:S(2)}) %collective-permute-start.1) | collective-permute-done | bytes 131104 | tf_op jit(solution)/shard_map/ppermute | solution.py:341
  146.4 0.7 fusion.2
  (15 shorter events, 0.1 us)
Async XLA Ops:
  7.2 58.6 %all-gather.5.cloned.1.call-start = ((), (), s32[]{:S(2)}) async-start(), calls=%async_computation.7 | async-start | bytes 2654208 | tf_op jit(solution)/shard_map/all_gather | solution.py:258
  37.1 4.8 %copy-start.6 = (s32[2,16,16]{2,1,0:T(8,128)S(1)}, s32[2,16,16]{2,1,0:T(8,128)}, u32[]{:S(2)}) copy-start(s32[2,16,16]{2,1,0:T(8,128)} %mask.1) | copy-start | bytes 6148
  37.2 24.0 %all-to-all-start = ((bf16[4,4,128,512]{3,2,1,0:T(8,128)(2,1)}), bf16[4,4,128,512]{3,2,1,0:T(8,128)(2,1)S(1)}, u32[]{:S(2)}, u32[]{:S(2)}) async-start(bf16[4,4,128,512]{3,2,1,0:T(8,128)(2,1)} %four_copies.1), calls=%async_computation | async-start | bytes 4194304 | tf_op jit(solution)/shard_map/all_to_all | solution.py:270
  41.9 96.6 %reduce-scatter.2.cloned.1.call-start = ((), (), s32[]{:S(2)}) async-start(), calls=%async_computation.6 | async-start | bytes 2359296 | tf_op jit(solution)/shard_map/reduce_scatter | solution.py:314
  65.8 1.7 %copy-start.4 = (bf16[16,144,512]{2,1,0:T(8,128)(2,1)S(1)}, bf16[16,144,512]{2,1,0:T(8,128)(2,1)}, u32[]{:S(2)}) copy-start(bf16[16,144,512]{2,1,0:T(8,128)(2,1)} %all-gather.5.cloned.1.call-done.kv) | copy-start | bytes 7077892
  69.0 28.0 %copy-start = (f32[2,32,128,128]{3,2,1,0:T(8,128)}, f32[2,32,128,128]{3,2,1,0:T(8,128)S(1)}, u32[]{:S(2)}) copy-start(f32[2,32,128,128]{3,2,1,0:T(8,128)S(1)} %get-tuple-element.15.shifted) | copy-start | bytes 12582916
  69.0 28.0 %copy-start.2 = (f32[2,32,128,128]{3,2,1,0:T(8,128)}, f32[2,32,128,128]{3,2,1,0:T(8,128)S(1)}, u32[]{:S(2)}) copy-start(f32[2,32,128,128]{3,2,1,0:T(8,128)S(1)} %get-tuple-element.16.grad_scores) | copy-start | bytes 12582916
  97.1 2.2 %copy-start.1 = (f32[2,32,128,128]{3,2,1,0:T(8,128)S(1)}, f32[2,32,128,128]{3,2,1,0:T(8,128)}, u32[]{:S(2)}) copy-start(f32[2,32,128,128]{3,2,1,0:T(8,128)} %copy-done) | copy-start | bytes 12582916
  99.3 2.2 %copy-start.3 = (f32[2,32,128,128]{3,2,1,0:T(8,128)S(1)}, f32[2,32,128,128]{3,2,1,0:T(8,128)}, u32[]{:S(2)}) copy-start(f32[2,32,128,128]{3,2,1,0:T(8,128)} %copy-done.2) | copy-start | bytes 12582916
  101.4 1.7 %copy-start.5 = (bf16[16,144,512]{2,1,0:T(8,128)(2,1)S(1)}, bf16[16,144,512]{2,1,0:T(8,128)(2,1)}, u32[]{:S(2)}) copy-start(bf16[16,144,512]{2,1,0:T(8,128)(2,1)} %all-gather.5.cloned.1.call-done.kv) | copy-start | bytes 7077892
  122.3 12.5 %all-to-all-start.4 = ((bf16[4,128,256]{2,1,0:T(8,128)(2,1)}), bf16[4,128,256]{2,1,0:T(8,128)(2,1)S(1)}, u32[]{:S(2)}, u32[]{:S(2)}) async-start(bf16[4,128,256]{2,1,0:T(8,128)(2,1)} %reduce_sum.21), calls=%async_computation.4 | async-start | bytes 524288 | tf_op jit(solution)/shard_map/all_to_all | solution.py:336
  125.7 3.1 %collective-permute-start = (f32[8,128]{1,0:T(8,128)S(1)}, f32[8,128]{1,0:T(8,128)S(1)}, u32[]{:S(2)}, u32[]{:S(2)}) collective-permute-start(f32[8,128]{1,0:T(8,128)S(1)} %get-tuple-element.21), channel_id=1, source_target_pairs={{0,1},{1,0},{2,3},{3,2},{4,5},{5,4},{6,7},{7,6},{8,9},{9,8},{10,11... | collective-permute-start | bytes 12296 | tf_op jit(solution)/shard_map/ppermute | solution.py:326
  139.5 6.9 %collective-permute-start.1 = (bf16[128,512]{1,0:T(8,128)(2,1)S(1)}, bf16[128,512]{1,0:T(8,128)(2,1)S(1)}, u32[]{:S(2)}, u32[]{:S(2)}) collective-permute-start(bf16[128,512]{1,0:T(8,128)(2,1)S(1)} %get-tuple-element.26), channel_id=1, source_target_pairs={{0,256},{32,288},{64,320},{96,352},{128,384},{160,416},{192,448},{... | collective-permute-start | bytes 393224 | tf_op jit(solution)/shard_map/ppermute | solution.py:341
Sparse Core Ops, SparseCore 0:
  17.0 48.7 all-gather.4
  97.2 41.3 reduce-scatter.1

commit v9 on v8

--- a/solution.py
+++ b/solution.py
@@ -100,10 +100,20 @@
     return ref[slot, :BLK, first : first + DH], ref[slot, :BLK, second : second + DH]
 
 
-def stat_kernel(lists, qg, kv, stats, shifted, grad_scores, tops, top, total, delta):
+def stat_kernel(
+    lists, qg, kv_from, stats, shifted, grad_scores, tops, kv_same, kv, top, total, delta, sems
+):
+    copies = [
+        pltpu.make_async_copy(kv_from.at[pl.ds(4 * at, 4)], kv.at[pl.ds(4 * at, 4)], sems.at[at])
+        for at in range(4)
+    ]
+    for copy in copies:
+        copy.start()
     top[...] = jnp.full_like(top, neg_big)
     total[...] = jnp.zeros_like(total)
     delta[...] = jnp.zeros_like(delta)
+    for copy in copies:
+        copy.wait()
 
     def work(pairs):
         found = []
@@ -272,17 +282,25 @@
     row_scratch = pltpu.VMEM((SLOTS, 1, DH), jnp.float32)
     block_scratch = pltpu.VMEM((SLOTS, BLK, DH), jnp.float32)
     by_pair = shape(HEADS, 2 * GB, BLK, BLK, dtype=jnp.float32)
-    stats, shifted, grad_scores, tops = pl.pallas_call(
+    stats, shifted, grad_scores, tops, kv = pl.pallas_call(
         stat_kernel,
         out_shape=(
             shape(4, STAT, DH, dtype=jnp.float32),
             by_pair,
             by_pair,
             shape(HEADS, 2 * GB, 1, DH, dtype=jnp.float32),
+            shape(GB, ROWS, 2 * WIDE),
         ),
-        in_specs=[SMEM, VMEM, VMEM],
-        out_specs=(VMEM,) * 4,
-        scratch_shapes=[row_scratch, row_scratch, row_scratch],
+        in_specs=[SMEM, VMEM, pl.BlockSpec(memory_space=pl.ANY)],
+        out_specs=(VMEM,) * 4 + (pl.BlockSpec(memory_space=pl.ANY),),
+        input_output_aliases={2: 4},
+        scratch_shapes=[
+            pltpu.VMEM((GB, ROWS, 2 * WIDE), jnp.bfloat16),
+            row_scratch,
+            row_scratch,
+            row_scratch,
+            pltpu.SemaphoreType.DMA((4,)),
+        ],
         compiler_params=params(28),
         name="row_stats",
     )(lists, qg, kv)

time: 155 us -> 156 us (level)
    unnamed x14 -> x16, local copies, waits for them, and re-layouts: 7.71 us -> 7.72 us
where the time goes in v9:
time: 156 us; the launch traced here: 155 us
  blocking collectives  68.6 us (44%)
  waiting for transfers between devices  31.8 us (20%)
  between operations  16.8 us (11%)
  starting transfers between devices  13.4 us (9%)
  Pallas kernels  12.7 us (8%)
  local copies, waits for them, and re-layouts  9.73 us (6%)
  other arithmetic  2.27 us (1%)
    all_gather x1, blocking collectives, body(): qg = lax.all_gather(qg, 'kb', axis_index_groups=Y_GROUPS)  18.9 us
    all_to_all x1, blocking collectives, body(): lax.all_to_all(qpart.reshape(4, 4, BLK, WIDE), 'kb', 0, 0, axis_index_gro...  16.8 us
    all_to_all x1, waiting for transfers between devices, body(): lax.all_to_all(qg, 'kb', 0, 0, axis_index_groups=X_GROUPS)  16.2 us
    all_to_all x1, blocking collectives, body(): stats = lax.all_to_all(stats, 'kb', 0, 0, axis_index_groups=Y_GROUPS)  15 us
    all_to_all x1, blocking collectives, body(): stats = lax.all_to_all(stats, 'kb', 0, 0, axis_index_groups=X_GROUPS)  9.94 us
    all_gather x1, blocking collectives, body(): kv = lax.all_gather(kv, 'qb', axis_index_groups=Y_PAIRS)  7.95 us
    unnamed x16, local copies, waits for them, and re-layouts  7.72 us
    all_to_all x1, starting transfers between devices, body(): lax.all_to_all(qg, 'kb', 0, 0, axis_index_groups=X_GROUPS)  4.78 us
  transfers between devices with their start and end apart: 6, of which 6 were waited for; matrix products, arithmetic and copies ran while one was open for 2% of the time, Pallas kernels for 4%

profile of v9, /device:TPU:6, one launch (start us, length us, event | category | flops | bytes accessed | tf_op | source)
XLA Modules:
  0.0 155.3 jit_solution(3835931088798238332)
XLA Ops:
  7.2 0.0 all-gather.5.cloned.1.call-start
  7.2 1.7 %pack.1 = (bf16[128,512]{1,0:T(8,128)(2,1)}, bf16[144,512]{1,0:T(8,128)(2,1)}) custom-call(bf16[1,128,256]{2,1,0:T(8,128)(2,1)} %queries.1, bf16[1,128,256]{2,1,0:T(8,128)(2,1)} %keys.1, bf16[1,128,256]{2,1,0:T(8,128)(2,1)} %values.1, bf16[1,128,256]{2,1,0:T(8,128)(2,1)} %out_grad.1, f32[1,128]{1,0:T(1,128)} %token_error.1), custom_call_target="tpu_custom_call" | custom-call | tf_op jit(solution)/shard_map/pack/pallas_call | solution.py:252
  8.9 7.9 %all-gather.1 = bf16[288,512]{1,0:T(8,128)(2,1)} all-gather(bf16[144,512]{1,0:T(8,128)(2,1)} %get-tuple-element.15), channel_id=3, replica_groups={{0,256},{32,288},{64,320},{96,352},{128,384},{160,416},{192,448},{224,4..., dimensions={0}, use_global_device_ids=true | all-gather | bytes 442368 | tf_op jit(solution)/shard_map/all_gather | solution.py:267
  16.9 18.9 %all-gather = bf16[512,512]{1,0:T(8,128)(2,1)S(1)} all-gather(bf16[128,512]{1,0:T(8,128)(2,1)} %get-tuple-element.14), channel_id=2, replica_groups={{0,8,16,24},{2,10,18,26},{4,12,20,28},{6,14,22,30},{1,9,17,25},{3,11,19..., dimensions={0}, use_global_device_ids=true | all-gather | bytes 655360 | tf_op jit(solution)/shard_map/all_gather | solution.py:269
  35.8 1.4 four_copies.1
  37.2 4.8 %all-to-all-start = ((bf16[4,4,128,512]{3,2,1,0:T(8,128)(2,1)}), bf16[4,4,128,512]{3,2,1,0:T(8,128)(2,1)S(1)}, u32[]{:S(2)}, u32[]{:S(2)}) async-start(bf16[4,4,128,512]{3,2,1,0:T(8,128)(2,1)} %four_copies.1), calls=%async_computation | async-start | bytes 4194304 | tf_op jit(solution)/shard_map/all_to_all | solution.py:280
  42.0 3.0 %pair_lists.1.lists = s32[3,40]{1,0:T(4,128)S(1)} custom-call(s32[2,16,16]{2,1,0:T(8,128)S(1)} %copy-done.7, s32[1]{0:T(128)} %bitcast.side), custom_call_target="tpu_custom_call" | custom-call | tf_op jit(solution)/shard_map/pair_lists/pallas_call | solution.py:259
  45.0 16.2 %all-to-all-done = bf16[4,4,128,512]{3,2,1,0:T(8,128)(2,1)S(1)} async-done(((bf16[4,4,128,512]{3,2,1,0:T(8,128)(2,1)}), bf16[4,4,128,512]{3,2,1,0:T(8,128)(2,1)S(1)}, u32[]{:S(2)}, u32[]{:S(2)}) %all-to-all-start) | async-done | bytes 2097184 | tf_op jit(solution)/shard_map/all_to_all | solution.py:280
  61.2 4.6 %all-gather.5.cloned.1.call-done.kv_from = bf16[16,144,512]{2,1,0:T(8,128)(2,1)} async-done(((bf16[2,144,512]{2,1,0:T(8,128)(2,1)}), bf16[16,144,512]{2,1,0:T(8,128)(2,1)}) %all-gather.5.cloned.1.call-update) | async-done | bytes 2359312 | tf_op jit(solution)/shard_map/all_gather | solution.py:268
  65.8 1.7 %copy-done.4 = bf16[16,144,512]{2,1,0:T(8,128)(2,1)S(1)} copy-done((bf16[16,144,512]{2,1,0:T(8,128)(2,1)S(1)}, bf16[16,144,512]{2,1,0:T(8,128)(2,1)}, u32[]{:S(2)}) %copy-start.4) | copy-done | bytes 2359320
  67.5 2.0 %row_stats.1 = (f32[4,104,128]{2,1,0:T(8,128)S(1)}, f32[2,32,128,128]{3,2,1,0:T(8,128)S(1)}, f32[2,32,128,128]{3,2,1,0:T(8,128)S(1)}, f32[2,32,1,128]{3,2,1,0:T(1,128)S(1)}, bf16[16,144,512]{2,1,0:T(8,128)(2,1)S(1)}) custom-call(s32[3,40]{1,0:T(4,128)S(1)} %pair_lists.1.lists, bf16[16,128,512]{2,1,0:T(8,128)(2,1)S(1)} %bitcast.19, ...), custom_call_target="tpu_custom_call", output_to_operand_aliasing={{4}: (2, {})} | custom-call | tf_op jit(solution)/shard_map/row_stats/pallas_call | solution.py:285
  69.6 9.9 %all_to_all.25.stats = f32[4,104,128]{2,1,0:T(8,128)S(1)} all-to-all(f32[4,104,128]{2,1,0:T(8,128)S(1)} %get-tuple-element.20), channel_id=1, replica_groups={{0,2,4,6},{8,10,12,14},{16,18,20,22},{24,26,28,30},{1,3,5,7},{9,11,13,1..., dimensions={0} | all-to-all | bytes 425984 | tf_op jit(solution)/shard_map/all_to_all | solution.py:307
  79.6 15.0 %all_to_all.26.stats = f32[4,104,128]{2,1,0:T(8,128)S(1)} all-to-all(f32[4,104,128]{2,1,0:T(8,128)S(1)} %merge_stats.1), channel_id=1, replica_groups={{0,8,16,24},{2,10,18,26},{4,12,20,28},{6,14,22,30},{1,9,17,25},{3,11,19..., dimensions={0} | all-to-all | bytes 425984 | tf_op jit(solution)/shard_map/all_to_all | solution.py:316
  94.5 3.1 %key_value_grads.1 = (bf16[16,128,512]{2,1,0:T(8,128)(2,1)}, f32[8,128]{1,0:T(8,128)S(1)}, f32[32,1,128]{2,1,0:T(1,128)S(1)}, f32[32,1,128]{2,1,0:T(1,128)S(1)}) custom-call(s32[3,40]{1,0:T(4,128)S(1)} %pair_lists.1.lists, bf16[16,128,512]{2,1,0:T(8,128)(2,1)S(1)} %bitcast.20, f32[4,104,128]{2,1,0:T(8,128)S(1)} %all_to_all.26.stats, ...), custom_call_target="tpu_custom_call", output_to_operand_aliasing={{0}: (6, {})} | custom-call | tf_op jit(solution)/shard_map/key_value_grads/pallas_call | solution.py:317
  97.7 2.2 %copy-done.1 = f32[2,32,128,128]{3,2,1,0:T(8,128)S(1)} copy-done((f32[2,32,128,128]{3,2,1,0:T(8,128)S(1)}, f32[2,32,128,128]{3,2,1,0:T(8,128)}, u32[]{:S(2)}) %copy-start.1) | copy-done | bytes 4194328
  99.8 2.2 %copy-done.3 = f32[2,32,128,128]{3,2,1,0:T(8,128)S(1)} copy-done((f32[2,32,128,128]{3,2,1,0:T(8,128)S(1)}, f32[2,32,128,128]{3,2,1,0:T(8,128)}, u32[]{:S(2)}) %copy-start.3) | copy-done | bytes 4194328
  102.0 1.7 %copy-done.6 = bf16[16,144,512]{2,1,0:T(8,128)(2,1)S(1)} copy-done((bf16[16,144,512]{2,1,0:T(8,128)(2,1)S(1)}, bf16[16,144,512]{2,1,0:T(8,128)(2,1)}, u32[]{:S(2)}) %copy-start.6) | copy-done | bytes 2359320
  103.7 1.4 query_grads.1
  105.1 16.8 %all_to_all.27 = bf16[4,4,128,256]{3,2,1,0:T(8,128)(2,1)S(1)} all-to-all(bf16[4,4,128,256]{3,2,1,0:T(8,128)(2,1)S(1)} %bitcast.21), channel_id=1, replica_groups={{0,2,4,6},{8,10,12,14},{16,18,20,22},{24,26,28,30},{1,3,5,7},{9,11,13,1..., dimensions={0} | all-to-all | bytes 2097152 | tf_op jit(solution)/shard_map/all_to_all | solution.py:352
  122.0 0.9 reduce_sum.21
  122.9 3.4 %all-to-all-start.4 = ((bf16[4,128,256]{2,1,0:T(8,128)(2,1)}), bf16[4,128,256]{2,1,0:T(8,128)(2,1)S(1)}, u32[]{:S(2)}, u32[]{:S(2)}) async-start(bf16[4,128,256]{2,1,0:T(8,128)(2,1)} %reduce_sum.21), calls=%async_computation.4 | async-start | bytes 524288 | tf_op jit(solution)/shard_map/all_to_all | solution.py:354
  126.3 1.9 %collective-permute-start = (f32[8,128]{1,0:T(8,128)S(1)}, f32[8,128]{1,0:T(8,128)S(1)}, u32[]{:S(2)}, u32[]{:S(2)}) collective-permute-start(f32[8,128]{1,0:T(8,128)S(1)} %get-tuple-element.23), channel_id=1, source_target_pairs={{0,1},{1,0},{2,3},{3,2},{4,5},{5,4},{6,7},{7,6},{8,9},{9,8},{10,11... | collective-permute-start | bytes 12296 | tf_op jit(solution)/shard_map/ppermute | solution.py:344
  128.2 0.5 slice.31
  128.7 0.6 collective-permute-done
  129.3 0.5 slice.30
  132.5 2.8 %all-to-all-done.4 = bf16[4,128,256]{2,1,0:T(8,128)(2,1)S(1)} async-done(((bf16[4,128,256]{2,1,0:T(8,128)(2,1)}), bf16[4,128,256]{2,1,0:T(8,128)(2,1)S(1)}, u32[]{:S(2)}, u32[]{:S(2)}) %all-to-all-start.4) | async-done | bytes 262176 | tf_op jit(solution)/shard_map/all_to_all | solution.py:354
  135.4 4.6 %reduce-scatter.2.cloned.1.call-done = bf16[1,256,512]{2,1,0:T(8,128)(2,1)} async-done(((bf16[8,256,512]{2,1,0:T(8,128)(2,1)}), bf16[1,256,512]{2,1,0:T(8,128)(2,1)}) %reduce-scatter.2.cloned.1.call-update) | async-done | bytes 262160 | tf_op jit(solution)/shard_map/reduce_scatter | solution.py:332
  139.9 1.0 slice_bitcast_fusion.1
  140.9 3.3 %collective-permute-start.1 = (bf16[128,512]{1,0:T(8,128)(2,1)S(1)}, bf16[128,512]{1,0:T(8,128)(2,1)S(1)}, u32[]{:S(2)}, u32[]{:S(2)}) collective-permute-start(bf16[128,512]{1,0:T(8,128)(2,1)S(1)} %get-tuple-element.28), channel_id=1, source_target_pairs={{0,256},{32,288},{64,320},{96,352},{128,384},{160,416},{192,448},{... | collective-permute-start | bytes 393224 | tf_op jit(solution)/shard_map/ppermute | solution.py:359
  144.2 0.6 fusion
  144.9 2.9 %collective-permute-done.1 = bf16[128,512]{1,0:T(8,128)(2,1)S(1)} collective-permute-done((bf16[128,512]{1,0:T(8,128)(2,1)S(1)}, bf16[128,512]{1,0:T(8,128)(2,1)S(1)}, u32[]{:S(2)}, u32[]{:S(2)}) %collective-permute-start.1) | collective-permute-done | bytes 131104 | tf_op jit(solution)/shard_map/ppermute | solution.py:359
  147.8 0.7 fusion.2
  (17 shorter events, 0.1 us)
Async XLA Ops:
  7.2 58.7 %all-gather.5.cloned.1.call-start = ((), (), s32[]{:S(2)}) async-start(), calls=%async_computation.7 | async-start | bytes 2654208 | tf_op jit(solution)/shard_map/all_gather | solution.py:268
  37.2 4.8 %copy-start.7 = (s32[2,16,16]{2,1,0:T(8,128)S(1)}, s32[2,16,16]{2,1,0:T(8,128)}, u32[]{:S(2)}) copy-start(s32[2,16,16]{2,1,0:T(8,128)} %mask.1) | copy-start | bytes 6148
  37.2 24.1 %all-to-all-start = ((bf16[4,4,128,512]{3,2,1,0:T(8,128)(2,1)}), bf16[4,4,128,512]{3,2,1,0:T(8,128)(2,1)S(1)}, u32[]{:S(2)}, u32[]{:S(2)}) async-start(bf16[4,4,128,512]{3,2,1,0:T(8,128)(2,1)} %four_copies.1), calls=%async_computation | async-start | bytes 4194304 | tf_op jit(solution)/shard_map/all_to_all | solution.py:280
  42.0 98.0 %reduce-scatter.2.cloned.1.call-start = ((), (), s32[]{:S(2)}) async-start(), calls=%async_computation.6 | async-start | bytes 2359296 | tf_op jit(solution)/shard_map/reduce_scatter | solution.py:332
  65.8 1.7 %copy-start.4 = (bf16[16,144,512]{2,1,0:T(8,128)(2,1)S(1)}, bf16[16,144,512]{2,1,0:T(8,128)(2,1)}, u32[]{:S(2)}) copy-start(bf16[16,144,512]{2,1,0:T(8,128)(2,1)} %all-gather.5.cloned.1.call-done.kv_from) | copy-start | bytes 7077892
  69.6 28.1 %copy-start = (f32[2,32,128,128]{3,2,1,0:T(8,128)}, f32[2,32,128,128]{3,2,1,0:T(8,128)S(1)}, u32[]{:S(2)}) copy-start(f32[2,32,128,128]{3,2,1,0:T(8,128)S(1)} %get-tuple-element.17.shifted) | copy-start | bytes 12582916
  69.6 28.1 %copy-start.2 = (f32[2,32,128,128]{3,2,1,0:T(8,128)}, f32[2,32,128,128]{3,2,1,0:T(8,128)S(1)}, u32[]{:S(2)}) copy-start(f32[2,32,128,128]{3,2,1,0:T(8,128)S(1)} %get-tuple-element.18.grad_scores) | copy-start | bytes 12582916
  69.6 28.0 %copy-start.5 = (bf16[16,144,512]{2,1,0:T(8,128)(2,1)}, bf16[16,144,512]{2,1,0:T(8,128)(2,1)S(1)}, u32[]{:S(2)}) copy-start(bf16[16,144,512]{2,1,0:T(8,128)(2,1)S(1)} %get-tuple-element.16.kv) | copy-start | bytes 7077892
  97.6 2.2 %copy-start.1 = (f32[2,32,128,128]{3,2,1,0:T(8,128)S(1)}, f32[2,32,128,128]{3,2,1,0:T(8,128)}, u32[]{:S(2)}) copy-start(f32[2,32,128,128]{3,2,1,0:T(8,128)} %copy-done) | copy-start | bytes 12582916
  99.8 2.2 %copy-start.3 = (f32[2,32,128,128]{3,2,1,0:T(8,128)S(1)}, f32[2,32,128,128]{3,2,1,0:T(8,128)}, u32[]{:S(2)}) copy-start(f32[2,32,128,128]{3,2,1,0:T(8,128)} %copy-done.2) | copy-start | bytes 12582916
  102.0 1.7 %copy-start.6 = (bf16[16,144,512]{2,1,0:T(8,128)(2,1)S(1)}, bf16[16,144,512]{2,1,0:T(8,128)(2,1)}, u32[]{:S(2)}) copy-start(bf16[16,144,512]{2,1,0:T(8,128)(2,1)} %copy-done.5) | copy-start | bytes 7077892
  122.9 12.5 %all-to-all-start.4 = ((bf16[4,128,256]{2,1,0:T(8,128)(2,1)}), bf16[4,128,256]{2,1,0:T(8,128)(2,1)S(1)}, u32[]{:S(2)}, u32[]{:S(2)}) async-start(bf16[4,128,256]{2,1,0:T(8,128)(2,1)} %reduce_sum.21), calls=%async_computation.4 | async-start | bytes 524288 | tf_op jit(solution)/shard_map/all_to_all | solution.py:354
  126.3 3.1 %collective-permute-start = (f32[8,128]{1,0:T(8,128)S(1)}, f32[8,128]{1,0:T(8,128)S(1)}, u32[]{:S(2)}, u32[]{:S(2)}) collective-permute-start(f32[8,128]{1,0:T(8,128)S(1)} %get-tuple-element.23), channel_id=1, source_target_pairs={{0,1},{1,0},{2,3},{3,2},{4,5},{5,4},{6,7},{7,6},{8,9},{9,8},{10,11... | collective-permute-start | bytes 12296 | tf_op jit(solution)/shard_map/ppermute | solution.py:344
  140.9 6.9 %collective-permute-start.1 = (bf16[128,512]{1,0:T(8,128)(2,1)S(1)}, bf16[128,512]{1,0:T(8,128)(2,1)S(1)}, u32[]{:S(2)}, u32[]{:S(2)}) collective-permute-start(bf16[128,512]{1,0:T(8,128)(2,1)S(1)} %get-tuple-element.28), channel_id=1, source_target_pairs={{0,256},{32,288},{64,320},{96,352},{128,384},{160,416},{192,448},{... | collective-permute-start | bytes 393224 | tf_op jit(solution)/shard_map/ppermute | solution.py:359
Sparse Core Ops, SparseCore 0:
  17.0 48.7 all-gather.4
  97.8 42.1 reduce-scatter.1

commit v10 on v8

--- a/solution.py
+++ b/solution.py
@@ -204,7 +204,7 @@
             kacc[at] += kterm
             vacc[at] += vterm
 
-    for_pairs(lists, work)
+    for_pairs(lists, work, 8)
     for slot in range(GB):
         target = slot // 2 * 2 + ((slot & 1) ^ lists[HEADS, 2])
         for head in range(HEADS):

time: 155 us -> 154 us (level)
  no operation moved by 1% of the time
where the time goes in v10:
time: 154 us; the launch traced here: 153 us
  blocking collectives  68.1 us (44%)
  waiting for transfers between devices  30.7 us (20%)
  between operations  16.8 us (11%)
  starting transfers between devices  13.6 us (9%)
  Pallas kernels  12 us (8%)
  local copies, waits for them, and re-layouts  9.72 us (6%)
  other arithmetic  2.27 us (1%)
    all_gather x1, blocking collectives, body(): qg = lax.all_gather(qg, 'kb', axis_index_groups=Y_GROUPS)  18.9 us
    all_to_all x1, blocking collectives, body(): lax.all_to_all(qpart.reshape(4, 4, BLK, WIDE), 'kb', 0, 0, axis_index_gro...  16.4 us
    all_to_all x1, waiting for transfers between devices, body(): lax.all_to_all(qg, 'kb', 0, 0, axis_index_groups=X_GROUPS)  16.2 us
    all_to_all x1, blocking collectives, body(): stats = lax.all_to_all(stats, 'kb', 0, 0, axis_index_groups=Y_GROUPS)  15 us
    all_to_all x1, blocking collectives, body(): stats = lax.all_to_all(stats, 'kb', 0, 0, axis_index_groups=X_GROUPS)  9.94 us
    all_gather x1, blocking collectives, body(): kv = lax.all_gather(kv, 'qb', axis_index_groups=Y_PAIRS)  7.93 us
    unnamed x14, local copies, waits for them, and re-layouts  7.71 us
    all_to_all x1, starting transfers between devices, body(): lax.all_to_all(qg, 'kb', 0, 0, axis_index_groups=X_GROUPS)  4.78 us
  transfers between devices with their start and end apart: 6, of which 6 were waited for; matrix products, arithmetic and copies ran while one was open for 2% of the time, Pallas kernels for 4%

profile of v10, /device:TPU:6, one launch (start us, length us, event | category | flops | bytes accessed | tf_op | source)
XLA Modules:
  0.0 153.2 jit_solution(13384601025422151401)
XLA Ops:
  7.2 0.0 all-gather.5.cloned.1.call-start
  7.2 1.7 %pack.1 = (bf16[128,512]{1,0:T(8,128)(2,1)}, bf16[144,512]{1,0:T(8,128)(2,1)}) custom-call(bf16[1,128,256]{2,1,0:T(8,128)(2,1)} %queries.1, bf16[1,128,256]{2,1,0:T(8,128)(2,1)} %keys.1, bf16[1,128,256]{2,1,0:T(8,128)(2,1)} %values.1, bf16[1,128,256]{2,1,0:T(8,128)(2,1)} %out_grad.1, f32[1,128]{1,0:T(1,128)} %token_error.1), custom_call_target="tpu_custom_call" | custom-call | tf_op jit(solution)/shard_map/pack/pallas_call | solution.py:242
  8.9 7.9 %all-gather = bf16[288,512]{1,0:T(8,128)(2,1)} all-gather(bf16[144,512]{1,0:T(8,128)(2,1)} %get-tuple-element.13), channel_id=2, replica_groups={{0,256},{32,288},{64,320},{96,352},{128,384},{160,416},{192,448},{224,4..., dimensions={0}, use_global_device_ids=true | all-gather | bytes 442368 | tf_op jit(solution)/shard_map/all_gather | solution.py:257
  16.8 18.9 %all-gather.2 = bf16[512,512]{1,0:T(8,128)(2,1)S(1)} all-gather(bf16[128,512]{1,0:T(8,128)(2,1)} %get-tuple-element.14), channel_id=4, replica_groups={{0,8,16,24},{2,10,18,26},{4,12,20,28},{6,14,22,30},{1,9,17,25},{3,11,19..., dimensions={0}, use_global_device_ids=true | all-gather | bytes 655360 | tf_op jit(solution)/shard_map/all_gather | solution.py:259
  35.7 1.4 four_copies.1
  37.2 4.8 %all-to-all-start = ((bf16[4,4,128,512]{3,2,1,0:T(8,128)(2,1)}), bf16[4,4,128,512]{3,2,1,0:T(8,128)(2,1)S(1)}, u32[]{:S(2)}, u32[]{:S(2)}) async-start(bf16[4,4,128,512]{3,2,1,0:T(8,128)(2,1)} %four_copies.1), calls=%async_computation | async-start | bytes 4194304 | tf_op jit(solution)/shard_map/all_to_all | solution.py:270
  41.9 3.0 %pair_lists.1.lists = s32[3,40]{1,0:T(4,128)S(1)} custom-call(s32[2,16,16]{2,1,0:T(8,128)S(1)} %copy-done.6, s32[1]{0:T(128)} %bitcast.side), custom_call_target="tpu_custom_call" | custom-call | tf_op jit(solution)/shard_map/pair_lists/pallas_call | solution.py:249
  45.0 16.2 %all-to-all-done = bf16[4,4,128,512]{3,2,1,0:T(8,128)(2,1)S(1)} async-done(((bf16[4,4,128,512]{3,2,1,0:T(8,128)(2,1)}), bf16[4,4,128,512]{3,2,1,0:T(8,128)(2,1)S(1)}, u32[]{:S(2)}, u32[]{:S(2)}) %all-to-all-start) | async-done | bytes 2097184 | tf_op jit(solution)/shard_map/all_to_all | solution.py:270
  61.1 4.7 %all-gather.5.cloned.1.call-done.kv = bf16[16,144,512]{2,1,0:T(8,128)(2,1)} async-done(((bf16[2,144,512]{2,1,0:T(8,128)(2,1)}), bf16[16,144,512]{2,1,0:T(8,128)(2,1)}) %all-gather.5.cloned.1.call-update) | async-done | bytes 2359312 | tf_op jit(solution)/shard_map/all_gather | solution.py:258
  65.8 1.7 %copy-done.4 = bf16[16,144,512]{2,1,0:T(8,128)(2,1)S(1)} copy-done((bf16[16,144,512]{2,1,0:T(8,128)(2,1)S(1)}, bf16[16,144,512]{2,1,0:T(8,128)(2,1)}, u32[]{:S(2)}) %copy-start.4) | copy-done | bytes 2359320
  67.5 1.5 row_stats.1
  69.0 9.9 %all_to_all.25.stats = f32[4,104,128]{2,1,0:T(8,128)S(1)} all-to-all(f32[4,104,128]{2,1,0:T(8,128)S(1)} %get-tuple-element.18), channel_id=1, replica_groups={{0,2,4,6},{8,10,12,14},{16,18,20,22},{24,26,28,30},{1,3,5,7},{9,11,13,1..., dimensions={0} | all-to-all | bytes 425984 | tf_op jit(solution)/shard_map/all_to_all | solution.py:289
  79.0 15.0 %all_to_all.26.stats = f32[4,104,128]{2,1,0:T(8,128)S(1)} all-to-all(f32[4,104,128]{2,1,0:T(8,128)S(1)} %merge_stats.1), channel_id=1, replica_groups={{0,8,16,24},{2,10,18,26},{4,12,20,28},{6,14,22,30},{1,9,17,25},{3,11,19..., dimensions={0} | all-to-all | bytes 425984 | tf_op jit(solution)/shard_map/all_to_all | solution.py:298
  93.9 3.0 %key_value_grads.1 = (bf16[16,128,512]{2,1,0:T(8,128)(2,1)}, f32[8,128]{1,0:T(8,128)S(1)}, f32[32,1,128]{2,1,0:T(1,128)S(1)}, f32[32,1,128]{2,1,0:T(1,128)S(1)}) custom-call(s32[3,40]{1,0:T(4,128)S(1)} %pair_lists.1.lists, bf16[16,128,512]{2,1,0:T(8,128)(2,1)S(1)} %bitcast.20, f32[4,104,128]{2,1,0:T(8,128)S(1)} %all_to_all.26.stats, ...), custom_call_target="tpu_custom_call", output_to_operand_aliasing={{0}: (6, {})} | custom-call | tf_op jit(solution)/shard_map/key_value_grads/pallas_call | solution.py:299
  96.9 2.2 %copy-done.1 = f32[2,32,128,128]{3,2,1,0:T(8,128)S(1)} copy-done((f32[2,32,128,128]{3,2,1,0:T(8,128)S(1)}, f32[2,32,128,128]{3,2,1,0:T(8,128)}, u32[]{:S(2)}) %copy-start.1) | copy-done | bytes 4194328
  99.1 2.2 %copy-done.3 = f32[2,32,128,128]{3,2,1,0:T(8,128)S(1)} copy-done((f32[2,32,128,128]{3,2,1,0:T(8,128)S(1)}, f32[2,32,128,128]{3,2,1,0:T(8,128)}, u32[]{:S(2)}) %copy-start.3) | copy-done | bytes 4194328
  101.3 1.7 %copy-done.5 = bf16[16,144,512]{2,1,0:T(8,128)(2,1)S(1)} copy-done((bf16[16,144,512]{2,1,0:T(8,128)(2,1)S(1)}, bf16[16,144,512]{2,1,0:T(8,128)(2,1)}, u32[]{:S(2)}) %copy-start.5) | copy-done | bytes 2359320
  103.0 1.4 query_grads.1
  104.4 16.4 %all_to_all.27 = bf16[4,4,128,256]{3,2,1,0:T(8,128)(2,1)S(1)} all-to-all(bf16[4,4,128,256]{3,2,1,0:T(8,128)(2,1)S(1)} %bitcast.21), channel_id=1, replica_groups={{0,2,4,6},{8,10,12,14},{16,18,20,22},{24,26,28,30},{1,3,5,7},{9,11,13,1..., dimensions={0} | all-to-all | bytes 2097152 | tf_op jit(solution)/shard_map/all_to_all | solution.py:334
  120.8 0.9 reduce_sum.21
  121.7 3.4 %all-to-all-start.4 = ((bf16[4,128,256]{2,1,0:T(8,128)(2,1)}), bf16[4,128,256]{2,1,0:T(8,128)(2,1)S(1)}, u32[]{:S(2)}, u32[]{:S(2)}) async-start(bf16[4,128,256]{2,1,0:T(8,128)(2,1)} %reduce_sum.21), calls=%async_computation.4 | async-start | bytes 524288 | tf_op jit(solution)/shard_map/all_to_all | solution.py:336
  125.1 1.9 %collective-permute-start = (f32[8,128]{1,0:T(8,128)S(1)}, f32[8,128]{1,0:T(8,128)S(1)}, u32[]{:S(2)}, u32[]{:S(2)}) collective-permute-start(f32[8,128]{1,0:T(8,128)S(1)} %get-tuple-element.21), channel_id=1, source_target_pairs={{0,1},{1,0},{2,3},{3,2},{4,5},{5,4},{6,7},{7,6},{8,9},{9,8},{10,11... | collective-permute-start | bytes 12296 | tf_op jit(solution)/shard_map/ppermute | solution.py:326
  127.1 0.5 slice.31
  127.6 0.6 collective-permute-done
  128.2 0.5 slice.30
  131.4 2.8 %all-to-all-done.4 = bf16[4,128,256]{2,1,0:T(8,128)(2,1)S(1)} async-done(((bf16[4,128,256]{2,1,0:T(8,128)(2,1)}), bf16[4,128,256]{2,1,0:T(8,128)(2,1)S(1)}, u32[]{:S(2)}, u32[]{:S(2)}) %all-to-all-start.4) | async-done | bytes 262176 | tf_op jit(solution)/shard_map/all_to_all | solution.py:336
  134.2 3.6 %reduce-scatter.2.cloned.1.call-done = bf16[1,256,512]{2,1,0:T(8,128)(2,1)} async-done(((bf16[8,256,512]{2,1,0:T(8,128)(2,1)}), bf16[1,256,512]{2,1,0:T(8,128)(2,1)}) %reduce-scatter.2.cloned.1.call-update) | async-done | bytes 262160 | tf_op jit(solution)/shard_map/reduce_scatter | solution.py:314
  137.8 1.0 slice_bitcast_fusion.1
  138.8 3.4 %collective-permute-start.1 = (bf16[128,512]{1,0:T(8,128)(2,1)S(1)}, bf16[128,512]{1,0:T(8,128)(2,1)S(1)}, u32[]{:S(2)}, u32[]{:S(2)}) collective-permute-start(bf16[128,512]{1,0:T(8,128)(2,1)S(1)} %get-tuple-element.26), channel_id=1, source_target_pairs={{0,256},{32,288},{64,320},{96,352},{128,384},{160,416},{192,448},{... | collective-permute-start | bytes 393224 | tf_op jit(solution)/shard_map/ppermute | solution.py:341
  142.3 0.6 fusion
  142.9 2.8 %collective-permute-done.1 = bf16[128,512]{1,0:T(8,128)(2,1)S(1)} collective-permute-done((bf16[128,512]{1,0:T(8,128)(2,1)S(1)}, bf16[128,512]{1,0:T(8,128)(2,1)S(1)}, u32[]{:S(2)}, u32[]{:S(2)}) %collective-permute-start.1) | collective-permute-done | bytes 131104 | tf_op jit(solution)/shard_map/ppermute | solution.py:341
  145.7 0.7 fusion.2
  (15 shorter events, 0.1 us)
Async XLA Ops:
  7.2 58.6 %all-gather.5.cloned.1.call-start = ((), (), s32[]{:S(2)}) async-start(), calls=%async_computation.7 | async-start | bytes 2654208 | tf_op jit(solution)/shard_map/all_gather | solution.py:258
  37.1 4.8 %copy-start.6 = (s32[2,16,16]{2,1,0:T(8,128)S(1)}, s32[2,16,16]{2,1,0:T(8,128)}, u32[]{:S(2)}) copy-start(s32[2,16,16]{2,1,0:T(8,128)} %mask.1) | copy-start | bytes 6148
  37.2 24.0 %all-to-all-start = ((bf16[4,4,128,512]{3,2,1,0:T(8,128)(2,1)}), bf16[4,4,128,512]{3,2,1,0:T(8,128)(2,1)S(1)}, u32[]{:S(2)}, u32[]{:S(2)}) async-start(bf16[4,4,128,512]{3,2,1,0:T(8,128)(2,1)} %four_copies.1), calls=%async_computation | async-start | bytes 4194304 | tf_op jit(solution)/shard_map/all_to_all | solution.py:270
  41.9 95.9 %reduce-scatter.2.cloned.1.call-start = ((), (), s32[]{:S(2)}) async-start(), calls=%async_computation.6 | async-start | bytes 2359296 | tf_op jit(solution)/shard_map/reduce_scatter | solution.py:314
  65.8 1.7 %copy-start.4 = (bf16[16,144,512]{2,1,0:T(8,128)(2,1)S(1)}, bf16[16,144,512]{2,1,0:T(8,128)(2,1)}, u32[]{:S(2)}) copy-start(bf16[16,144,512]{2,1,0:T(8,128)(2,1)} %all-gather.5.cloned.1.call-done.kv) | copy-start | bytes 7077892
  69.0 27.9 %copy-start = (f32[2,32,128,128]{3,2,1,0:T(8,128)}, f32[2,32,128,128]{3,2,1,0:T(8,128)S(1)}, u32[]{:S(2)}) copy-start(f32[2,32,128,128]{3,2,1,0:T(8,128)S(1)} %get-tuple-element.15.shifted) | copy-start | bytes 12582916
  69.0 27.9 %copy-start.2 = (f32[2,32,128,128]{3,2,1,0:T(8,128)}, f32[2,32,128,128]{3,2,1,0:T(8,128)S(1)}, u32[]{:S(2)}) copy-start(f32[2,32,128,128]{3,2,1,0:T(8,128)S(1)} %get-tuple-element.16.grad_scores) | copy-start | bytes 12582916
  96.9 2.2 %copy-start.1 = (f32[2,32,128,128]{3,2,1,0:T(8,128)S(1)}, f32[2,32,128,128]{3,2,1,0:T(8,128)}, u32[]{:S(2)}) copy-start(f32[2,32,128,128]{3,2,1,0:T(8,128)} %copy-done) | copy-start | bytes 12582916
  99.1 2.2 %copy-start.3 = (f32[2,32,128,128]{3,2,1,0:T(8,128)S(1)}, f32[2,32,128,128]{3,2,1,0:T(8,128)}, u32[]{:S(2)}) copy-start(f32[2,32,128,128]{3,2,1,0:T(8,128)} %copy-done.2) | copy-start | bytes 12582916
  101.3 1.7 %copy-start.5 = (bf16[16,144,512]{2,1,0:T(8,128)(2,1)S(1)}, bf16[16,144,512]{2,1,0:T(8,128)(2,1)}, u32[]{:S(2)}) copy-start(bf16[16,144,512]{2,1,0:T(8,128)(2,1)} %all-gather.5.cloned.1.call-done.kv) | copy-start | bytes 7077892
  121.7 12.5 %all-to-all-start.4 = ((bf16[4,128,256]{2,1,0:T(8,128)(2,1)}), bf16[4,128,256]{2,1,0:T(8,128)(2,1)S(1)}, u32[]{:S(2)}, u32[]{:S(2)}) async-start(bf16[4,128,256]{2,1,0:T(8,128)(2,1)} %reduce_sum.21), calls=%async_computation.4 | async-start | bytes 524288 | tf_op jit(solution)/shard_map/all_to_all | solution.py:336
  125.1 3.1 %collective-permute-start = (f32[8,128]{1,0:T(8,128)S(1)}, f32[8,128]{1,0:T(8,128)S(1)}, u32[]{:S(2)}, u32[]{:S(2)}) collective-permute-start(f32[8,128]{1,0:T(8,128)S(1)} %get-tuple-element.21), channel_id=1, source_target_pairs={{0,1},{1,0},{2,3},{3,2},{4,5},{5,4},{6,7},{7,6},{8,9},{9,8},{10,11... | collective-permute-start | bytes 12296 | tf_op jit(solution)/shard_map/ppermute | solution.py:326
  138.8 6.9 %collective-permute-start.1 = (bf16[128,512]{1,0:T(8,128)(2,1)S(1)}, bf16[128,512]{1,0:T(8,128)(2,1)S(1)}, u32[]{:S(2)}, u32[]{:S(2)}) collective-permute-start(bf16[128,512]{1,0:T(8,128)(2,1)S(1)} %get-tuple-element.26), channel_id=1, source_target_pairs={{0,256},{32,288},{64,320},{96,352},{128,384},{160,416},{192,448},{... | collective-permute-start | bytes 393224 | tf_op jit(solution)/shard_map/ppermute | solution.py:341
Sparse Core Ops, SparseCore 0:
  17.0 48.7 all-gather.4
  97.1 40.7 reduce-scatter.1
